TPU v7x, 256 devices: a whole 4x4x8 slice. The times are simulated.
256 devices in a mesh: seq: 4 (over z_lo), res: 64 (over y, z_hi, x, core).
Axes of the slice: x: 4, y: 4, z: 8 (z_hi: 2, z_lo: 4; z = z_hi * 4 + z_lo), core: 2. Of those that a mesh axis runs over, the one named last changes fastest.
Arguments:
- sequence_features: bfloat16 [1024, 262144], P('seq', 'res'), may hold values from -6 to 6
- pair_window_rows: bfloat16 [256, 4096, 128], P('seq', 'res'), may hold values from -16 to 16
- residue_mask: int32 [4096], P('res'), may hold values 0 or 1
- sequence_validity: int32 [1024], P('seq'), may hold values 0 or 1
- pair_head_weight: bfloat16 [128, 8], replicated, may hold values from -16 to 16
- content_projection: bfloat16 [64, 64], replicated, may hold values from -0.75 to 0.75
- sigmoid_projection: bfloat16 [64, 64], replicated, may hold values from -0.75 to 0.75
- closing_projection: bfloat16 [64, 64], replicated, may hold values from -0.75 to 0.75
Outputs:
- updated: bfloat16 [1024, 16384], P('seq', 'res')
All inputs are finite; a program needn't handle non-finite values. No bound on the sum of `residue_mask` or of `sequence_validity` on one device may be relied on, other than what follows from the above.
Results may differ from a plain program's by a relative error of at most 0.015.
The roundings to bfloat16 on the way count: a program that leaves them out, or rounds other values in their place, can miss the bound.
Values may be sent and summed in bfloat16 or wider, within the bound.
No kernel may reach another device: no remote copies, remote signals or barrier semaphores. Data moves between devices by JAX's collectives and lax.ppermute only.
A program may use at most 128 MiB of HBM per device.

v0:
```python
import jax
import jax.numpy as jnp
from jax import lax
from jax.sharding import PartitionSpec as P

FEATURE_DEPTH = 64
CZ = 128
HEADS = 8
HEAD_CHANNELS = 8
SHARD_SPAN = 4


def layer_norm_apply(inputs):
    average = jnp.mean(inputs, -1, keepdims=True)
    centered = inputs - average
    variance = jnp.mean(centered * centered, -1, keepdims=True)
    return centered * lax.rsqrt(variance + 1e-05)


def shards(
    sequence_features,
    pair_window_rows,
    residue_mask,
    sequence_validity,
    pair_head_weight,
    content_projection,
    sigmoid_projection,
    closing_projection,
):
    sequence_number = sequence_features.shape[0]
    position_number = sequence_features.shape[1] // FEATURE_DEPTH
    sequence_extent = sequence_features.reshape(sequence_number, position_number, FEATURE_DEPTH)
    standardized_features = layer_norm_apply(sequence_extent.astype(jnp.float32)).astype(
        jnp.bfloat16
    )
    mapped_update = jnp.dot(
        standardized_features.reshape(-1, FEATURE_DEPTH),
        content_projection,
        preferred_element_type=jnp.float32,
    )
    mapped_update = mapped_update.reshape(
        sequence_number, position_number, FEATURE_DEPTH
    ) * sequence_validity[:, None, None].astype(jnp.float32)
    values = mapped_update.astype(jnp.bfloat16).reshape(
        sequence_number, position_number, HEADS, HEAD_CHANNELS
    )
    pair_count = pair_window_rows.shape[0]
    normed_pair = layer_norm_apply(pair_window_rows.astype(jnp.float32)).astype(jnp.bfloat16)
    logits = jnp.dot(
        normed_pair.reshape(-1, CZ), pair_head_weight, preferred_element_type=jnp.float32
    )
    logits = logits.reshape(pair_count, position_number, HEADS)
    logits = jnp.where(residue_mask[None, :, None] == 1, logits, -1000000000.0)
    local_top = jnp.max(logits, axis=1)
    row_top = lax.pmax(local_top, "res")
    exponents = jnp.exp(logits - row_top[:, None, :])
    totals = lax.psum(jnp.sum(exponents, axis=1), "res")
    weights = (exponents / totals[:, None, :]).astype(jnp.bfloat16)
    window_weights = lax.all_gather(weights, "seq", axis=0, tiled=True)
    spread = lax.all_to_all(values, "res", split_axis=0, concat_axis=1, tiled=True)
    gathered = jnp.einsum(
        "ijh,sjhc->ishc",
        lax.all_gather(window_weights, "res", axis=1, tiled=True),
        spread,
        preferred_element_type=jnp.float32,
    )
    coupling_mean = (
        lax.all_to_all(
            gathered.astype(jnp.bfloat16), "res", split_axis=0, concat_axis=1, tiled=True
        )
        .astype(gathered.dtype)
        .reshape(SHARD_SPAN, sequence_number, FEATURE_DEPTH)
    )
    coupling_mean = coupling_mean.transpose(1, 0, 2)
    span_sequences = standardized_features[:, :SHARD_SPAN]
    sigmoid_factor = jax.nn.sigmoid(
        jnp.dot(
            span_sequences.reshape(-1, FEATURE_DEPTH),
            sigmoid_projection,
            preferred_element_type=jnp.float32,
        )
    )
    filtered_update = (
        sigmoid_factor.reshape(sequence_number, SHARD_SPAN, FEATURE_DEPTH) * coupling_mean
    ).astype(jnp.bfloat16)
    returned_update = jnp.dot(
        filtered_update.reshape(-1, FEATURE_DEPTH),
        closing_projection,
        preferred_element_type=jnp.float32,
    )
    return returned_update.astype(jnp.bfloat16).reshape(sequence_number, SHARD_SPAN * FEATURE_DEPTH)


def solution(mesh):
    return jax.shard_map(
        shards,
        mesh=mesh,
        in_specs=(P("seq", "res"), P("seq", "res", None), P("res"), P("seq"), P(), P(), P(), P()),
        out_specs=P("seq", "res"),
        check_vma=False,
    )
```

profile of v0, /device:TPU:32, one launch (start us, length us, event | category | flops | bytes accessed | tf_op | source)
XLA Modules:
  0.0 1074.4 jit_solution(2971494341794782467)
XLA Ops:
  6.5 0.0 copy-start
  6.5 0.0 copy-start.2
  6.5 0.0 copy-start.7
  6.5 0.0 copy-start.6
  6.5 0.0 all-gather.2.cloned.1.call-start
  6.6 1.9 convert_reduce_fusion.1
  8.5 2.3 fusion.8
  10.9 0.0 copy-done.7
  10.9 0.0 copy-done.2
  10.9 0.0 copy-done.6
  10.9 1.3 fusion.27
  12.3 410.3 %pmax.7 = f32[64,8]{1,0:T(8,128)S(1)} all-reduce(f32[64,8]{1,0:T(8,128)S(1)} %get-tuple-element.5), channel_id=1, replica_groups=mesh['seq'=4,'res'=64] {'res'}, use_global_device_ids=true, to_apply=%region_5.6 | all-reduce | flops 512 | bytes 4096 | tf_op jit(solution)/shard_map/pmax | solution.py:55
  422.5 0.2 fusion.24
  422.8 400.3 %psum.7 = f32[64,8]{1,0:T(8,128)S(1)} all-reduce(f32[64,8]{1,0:T(8,128)S(1)} %fusion.24), channel_id=1, replica_groups=mesh['seq'=4,'res'=64] {'res'}, use_global_device_ids=true, to_apply=%region_7.8 | all-reduce | flops 512 | bytes 4096 | tf_op jit(solution)/shard_map/psum | solution.py:57
  823.1 0.2 divide_convert_fusion
  823.3 13.4 %all_gather.6 = bf16[256,64,8]{1,2,0:T(8,128)(2,1)S(1)} all-gather(bf16[64,64,8]{1,2,0:T(8,128)(2,1)S(1)} %divide_convert_fusion), channel_id=1, replica_groups=mesh['seq'=4,'res'=64] {'seq'}, dimensions={0}, use_global_device_ids=true | all-gather | bytes 327680 | tf_op jit(solution)/shard_map/all_gather | solution.py:59
  836.7 1.2 copy.54
  837.9 0.0 all-gather.2.cloned.1.call-update
  837.9 0.0 copy-start.4
  837.9 3.3 copy.48
  841.2 0.0 copy-done.4
  841.2 0.6 convert_reduce_fusion
  841.8 0.8 fusion.4
  842.7 1.0 fusion.5
  843.6 0.0 copy-start.1
  843.6 1.4 copy-done.1
  845.0 0.0 copy-done
  845.0 0.8 fusion.10
  845.8 8.1 copy.52
  853.9 6.9 reshape.89
  860.8 74.6 %all_to_all.27 = bf16[64,2,8192]{2,1,0:T(2,128)(2,1)} all-to-all(bf16[64,2,8192]{2,1,0:T(2,128)(2,1)S(1)} %reshape.89), channel_id=1, replica_groups=mesh['seq'=4,'res'=64] {'res'}, dimensions={0} | all-to-all | bytes 4194304 | tf_op jit(solution)/shard_map/all_to_all | solution.py:60
  935.4 7.9 reshape.90
  943.3 9.0 copy.53
  952.3 5.7 all_to_all.23
  958.0 54.5 %all-gather.2.cloned.1.call-done = bf16[256,4096,8]{0,2,1:T(8,128)(2,1)} async-done(((bf16[256,64,8]{0,2,1:T(8,128)(2,1)}), bf16[256,4096,8]{0,2,1:T(8,128)(2,1)}) %all-gather.2.cloned.1.call-update) | async-done | bytes 16777232 | tf_op jit(solution)/shard_map/all_gather | solution.py:63
  1012.5 10.2 fusion.17
  1022.7 0.0 slice-start
  1022.7 2.9 copy.56
  1025.6 0.0 copy-start.5
  1025.6 6.0 reshape.91
  1031.6 6.6 all-to-all-start.1
  1038.2 0.0 slice-done
  1038.2 0.2 copy.49
  1038.4 0.0 copy-done.5
  1038.4 0.3 fusion.13
  1038.6 0.2 copy.50
  1038.8 11.7 %all-to-all-done.1 = bf16[64,2,512]{2,1,0:T(2,128)(2,1)S(1)} async-done(((bf16[64,2,512]{2,1,0:T(2,128)(2,1)}), bf16[64,2,512]{2,1,0:T(2,128)(2,1)S(1)}, u32[]{:S(2)}, u32[]{:S(2)}) %all-to-all-start.1) | async-done | bytes 131104 | tf_op jit(solution)/shard_map/all_to_all | solution.py:68
  1050.5 2.4 reshape.92
  1053.0 1.5 copy.57
  1054.4 3.6 copy.58
  1058.1 4.7 copy.67
  1062.8 0.0 copy-start.3
  1062.8 3.3 reshape.88
  1066.1 0.1 fusion.23
  1066.3 0.0 copy-done.3
  1066.3 0.2 convolution_convert_fusion
  1066.5 0.2 copy.61
  1066.7 0.9 reshape.81
  (6 shorter events, 0.1 us)
Async XLA Ops:
  6.5 838.5 %copy-start = (bf16[64,64]{1,0:T(8,128)(2,1)S(1)}, bf16[64,64]{1,0:T(8,128)(2,1)}, u32[]{:S(2)}) copy-start(bf16[64,64]{1,0:T(8,128)(2,1)} %param.13) | copy-start | bytes 24580
  6.5 4.4 copy-start.2
  6.5 4.4 copy-start.7
  6.5 4.4 copy-start.6
  6.5 1006.0 %all-gather.2.cloned.1.call-start = ((), (), s32[]{:S(2)}) async-start(), calls=%async_computation.2 | async-start | bytes 17039360 | tf_op jit(solution)/shard_map/all_gather | solution.py:63
  837.9 3.3 copy-start.4
  843.6 1.4 copy-start.1
  1022.7 15.4 %slice-start = ((bf16[256,64,64]{0,2,1:T(8,128)(2,1)}), bf16[256,4,64]{0,2,1:T(8,128)(2,1)S(1)}, s32[]{:S(2)}) async-start(bf16[256,64,64]{0,2,1:T(8,128)(2,1)} %copy-done.1), calls=%async_computation.3 | async-start | bytes 262144 | tf_op jit(solution)/shard_map/slice | solution.py:75
  1025.6 12.7 %copy-start.5 = (bf16[64,64]{1,0:T(8,128)(2,1)S(1)}, bf16[64,64]{1,0:T(8,128)(2,1)}, u32[]{:S(2)}) copy-start(bf16[64,64]{1,0:T(8,128)(2,1)} %param.14) | copy-start | bytes 24580
  1031.6 18.9 %all-to-all-start.1 = ((bf16[64,2,512]{2,1,0:T(2,128)(2,1)}), bf16[64,2,512]{2,1,0:T(2,128)(2,1)S(1)}, u32[]{:S(2)}, u32[]{:S(2)}) async-start(bf16[64,2,512]{2,1,0:T(2,128)(2,1)} %reshape.91), calls=%async_computation.1 | async-start | bytes 262144 | tf_op jit(solution)/shard_map/all_to_all | solution.py:68
  1062.8 3.5 copy-start.3
Sparse Core Ops, SparseCore 0:
  838.0 174.4 all-gather.1
where the time goes:
time: 1080 us; the launch traced here: 1070 us
  blocking collectives  899 us (83%)
  local copies, waits for them, and re-layouts  69.3 us (6%)
  waiting for transfers between devices  66.2 us (6%)
  between operations  13.7 us (1%)
  matrix products  12.8 us (1%)
    pmax x1, blocking collectives, shards(): row_top = lax.pmax(local_top, 'res')  410 us
    psum x1, blocking collectives, shards(): totals = lax.psum(jnp.sum(exponents, axis=1), 'res')  400 us
    all_to_all x1, blocking collectives, shards(): lax.all_to_all(values, 'res', split_axis=0, concat_axis=1, tiled=True)  74.6 us
    all_gather x1, waiting for transfers between devices, shards(): lax.all_gather(window_weights, 'res', axis=1, tiled=True)  54.5 us
    unnamed x21, local copies, waits for them, and re-layouts  27.9 us
  transfers between devices with their start and end apart: 2, of which 2 were waited for; matrix products, arithmetic and copies ran while one was open for 4% of the time, Pallas kernels for 0%

commit v1 on v0

v1 whole, which is shorter than its diff:
```python
import functools

import jax
import jax.numpy as jnp
from jax import lax
from jax.experimental import pallas as pl
from jax.experimental.pallas import tpu as pltpu
from jax.sharding import Mesh
from jax.sharding import PartitionSpec as P

F32 = jnp.float32
BF16 = jnp.bfloat16
EPS = 1e-05
NT = (((1,), (1,)), ((), ()))
NN = (((1,), (0,)), ((), ()))
TN = (((0,), (0,)), ((), ()))
GROUP = ("y", "x")
RES = ("y", "zh", "x", "core")
VMEM_LIMIT = 48 * 1024 * 1024


def dot(a, b, dims=NN):
    return lax.dot_general(a, b, dims, preferred_element_type=F32)


def iota(shape, dim):
    return lax.broadcasted_iota(jnp.int32, shape, dim)


def one_hot(cond):
    return jnp.where(cond, 1.0, 0.0).astype(BF16)


def logits_kernel(pair_ref, mask_ref, weight_ref, out_ref, scr):
    rows = pair_ref.shape[0] * pair_ref.shape[1]
    step = pl.program_id(0)
    x = pair_ref[...].reshape(rows, 128)
    mean_m = jnp.full((128, 128), 1.0 / 128, BF16)
    centered = x.astype(F32) - dot(x, mean_m)
    square = centered * centered
    high = square.astype(BF16)
    low = (square - high.astype(F32)).astype(BF16)
    variance = dot(high, mean_m) + dot(low, mean_m)
    normed = (centered * lax.rsqrt(variance + EPS)).astype(BF16)
    logits = lax.dot_general(
        weight_ref[...], normed, NT, preferred_element_type=F32
    )
    mask = mask_ref[...]
    for k in range(rows // 128):
        part = jnp.where(mask == 1, logits[:, k * 128 : (k + 1) * 128], -1000000000.0)
        scr[pl.ds(k, 8, stride=rows // 128), :] = part
    block = scr[...].reshape(8, rows // 128, 128)
    for sg in range(2):
        out_ref[:, sg, pl.ds(step * (rows // 128), rows // 128), :] = block


def pair_logits(pair, mask2, weight_t):
    steps = 4
    return pl.pallas_call(
        logits_kernel,
        grid=(steps,),
        out_shape=jax.ShapeDtypeStruct((8, 2, 32, 128), F32),
        in_specs=[
            pl.BlockSpec((64 // steps, 64, 128), lambda i: (i, 0, 0)),
            pl.BlockSpec((1, 128), lambda i: (0, 0)),
            pl.BlockSpec((8, 128), lambda i: (0, 0)),
        ],
        out_specs=pl.BlockSpec((8, 2, 32, 128), lambda i: (0, 0, 0, 0)),
        scratch_shapes=[pltpu.VMEM((64 * 32 // 8 // steps, 128), F32)],
        compiler_params=pltpu.CompilerParams(vmem_limit_bytes=VMEM_LIMIT),
        cost_estimate=pl.CostEstimate(
            flops=400_000_000, bytes_accessed=1_400_000, transcendentals=500_000
        ),
        name="pair_logits",
    )(pair, mask2, weight_t)


def values_kernel(m_ref, valid_ref, content_ref, sigmoid_ref, v_ref, gate_ref, wbig):
    step = pl.program_id(0)

    @pl.when(step == 0)
    def _():
        spread = one_hot(iota((512, 64), 0) // 8 == iota((512, 64), 1))
        rep = dot(spread, content_ref[...], NT).astype(BF16)
        tile = one_hot(iota((64, 512), 1) % 64 == iota((64, 512), 0))
        full = dot(rep, tile)
        keep = iota((512, 512), 0) % 8 == iota((512, 512), 1) // 64
        wbig[...] = jnp.where(keep, full, 0.0).astype(BF16)

    eye = one_hot(iota((256, 256), 0) == iota((256, 256), 1))
    parts = []
    for k in range(4):
        xt = dot(eye, m_ref[:, k * 256 : (k + 1) * 256], NT).reshape(4, 64, 256)
        mean = jnp.sum(xt, axis=1, keepdims=True) * (1.0 / 64)
        centered = xt - mean
        variance = jnp.sum(centered * centered, axis=1, keepdims=True) * (1.0 / 64)
        parts.append((centered * lax.rsqrt(variance + EPS)).astype(BF16).reshape(256, 256))
    valid = valid_ref[...].astype(F32)
    halves = []
    for k in range(2):
        normed = jnp.concatenate(parts[2 * k : 2 * k + 2], axis=0)
        halves.append((dot(wbig[...], normed) * valid).reshape(64, 8, 256))
    both = jnp.concatenate(halves, axis=1).astype(BF16).reshape(8, 8, 16, 256)
    v_ref[:, 0] = both[..., :128]
    v_ref[:, 1] = both[..., 128:]

    @pl.when(step == 0)
    def _():
        spread = one_hot(iota((256, 64), 0) % 64 == iota((256, 64), 1))
        rep = dot(spread, sigmoid_ref[...], NT).astype(BF16)
        tile = one_hot(iota((64, 256), 1) % 64 == iota((64, 256), 0))
        full = dot(rep, tile)
        keep = iota((256, 256), 0) // 64 == iota((256, 256), 1) // 64
        wgate = jnp.where(keep, full, 0.0).astype(BF16)
        gate_ref[...] = jax.nn.sigmoid(dot(wgate, parts[0]))


def msa_values(m, valid, content, sigmoid):
    return pl.pallas_call(
        values_kernel,
        grid=(4,),
        out_shape=(
            jax.ShapeDtypeStruct((8, 2, 8, 64, 128), BF16),
            jax.ShapeDtypeStruct((256, 256), F32),
        ),
        in_specs=[
            pl.BlockSpec((256, 1024), lambda i: (0, i)),
            pl.BlockSpec((1, 256), lambda i: (0, 0)),
            pl.BlockSpec((64, 64), lambda i: (0, 0)),
            pl.BlockSpec((64, 64), lambda i: (0, 0)),
        ],
        out_specs=(
            pl.BlockSpec((8, 2, 8, 16, 128), lambda i: (0, 0, 0, i, 0)),
            pl.BlockSpec((256, 256), lambda i: (0, 0)),
        ),
        scratch_shapes=[pltpu.VMEM((512, 512), BF16)],
        compiler_params=pltpu.CompilerParams(vmem_limit_bytes=VMEM_LIMIT),
        cost_estimate=pl.CostEstimate(
            flops=2_000_000_000, bytes_accessed=4_500_000, transcendentals=100_000
        ),
        name="msa_values",
    )(m, valid, content, sigmoid)


def by_halves(x, reduce):
    low = iota(x.shape, 1) < 64
    a = reduce(x[:, :64], axis=1, keepdims=True)
    b = reduce(x[:, 64:], axis=1, keepdims=True)
    return jnp.where(low, a, b)


def stats_kernel(l_ref, out_ref):
    logits = l_ref[...]
    top = by_halves(jnp.max(logits, axis=0), jnp.max)
    total = by_halves(jnp.sum(jnp.exp(logits - top[None]), axis=0), jnp.sum)
    out_ref[0] = top
    out_ref[1] = total


def local_stats(logits):
    return pl.pallas_call(
        stats_kernel,
        out_shape=jax.ShapeDtypeStruct((2, 32, 128), F32),
        cost_estimate=pl.CostEstimate(
            flops=200_000, bytes_accessed=300_000, transcendentals=65536
        ),
        name="local_stats",
    )(logits)


def weights_kernel(l_ref, a_ref, b_ref, c_ref, d_ref, out_ref):
    refs = (a_ref, b_ref, c_ref, d_ref)
    top = jnp.maximum(
        jnp.maximum(a_ref[0], b_ref[0]), jnp.maximum(c_ref[0], d_ref[0])
    )
    total = sum(r[1] * jnp.exp(r[0] - top) for r in refs)
    low = iota((32, 128), 1) < 64
    for k in range(8):
        a = jnp.exp(l_ref[2 * k] - top) / total
        b = jnp.exp(l_ref[2 * k + 1] - top) / total
        even = jnp.where(low, a, pltpu.roll(b, 64, 1))
        odd = jnp.where(low, pltpu.roll(a, 64, 1), b)
        out_ref[0:32, k * 128 : (k + 1) * 128] = even.astype(BF16)
        out_ref[32:64, k * 128 : (k + 1) * 128] = odd.astype(BF16)


def softmax_weights(logits, stats):
    return pl.pallas_call(
        weights_kernel,
        out_shape=jax.ShapeDtypeStruct((64, 1024), BF16),
        cost_estimate=pl.CostEstimate(
            flops=200_000, bytes_accessed=500_000, transcendentals=65536
        ),
        name="softmax_weights",
    )(logits, *stats)


def average_kernel(place_ref, w0, w1, w2, w3, v_ref, out_ref, wall, scr):
    for k, w in enumerate((w0, w1, w2, w3)):
        start = pl.multiple_of(place_ref[k] * 64, 64)
        wall[pl.ds(start, 64), :] = w[...]
    weights = wall[...]
    for c2 in range(4):
        right = jnp.concatenate(
            [v_ref[:, 2 * c2 + e].reshape(1024, 128) for e in range(2)], axis=1
        )
        part = dot(weights, right)
        for e in range(2):
            for q in range(4):
                for par in range(2):
                    row = q * 64 + par * 32
                    scr[pl.ds((q * 64 + par) * 8 + 2 * c2 + e, 32, stride=16), :] = part[
                        row : row + 32, e * 128 : (e + 1) * 128
                    ]
    out_ref[...] = scr[...].astype(BF16).reshape(64, 32, 128)


def partial_average(place, weights, values):
    vmem = pl.BlockSpec(memory_space=pltpu.VMEM)
    return pl.pallas_call(
        average_kernel,
        out_shape=jax.ShapeDtypeStruct((64, 32, 128), BF16),
        in_specs=[pl.BlockSpec(memory_space=pltpu.SMEM)] + [vmem] * 5,
        out_specs=vmem,
        scratch_shapes=[pltpu.VMEM((256, 1024), BF16), pltpu.VMEM((2048, 128), F32)],
        compiler_params=pltpu.CompilerParams(vmem_limit_bytes=VMEM_LIMIT),
        cost_estimate=pl.CostEstimate(
            flops=600_000_000, bytes_accessed=3_100_000, transcendentals=0
        ),
        name="partial_average",
    )(place, *weights, values)


def closing_kernel(p_ref, gate_ref, closing_ref, out_ref, gated):
    for y in range(4):
        for x in range(4):
            head, half = 2 * y + x // 2, x % 2
            total = sum(
                p_ref[y * 16 + zh * 8 + x * 2 + core].astype(F32)
                for zh in range(2)
                for core in range(2)
            )
            cols = slice(half * 128, half * 128 + 128)
            for i in range(4):
                rows = slice(i * 64 + head * 8, i * 64 + head * 8 + 8)
                gated[rows, cols] = total[i * 8 : i * 8 + 8] * gate_ref[rows, cols]
    spread = one_hot(iota((256, 64), 0) % 64 == iota((256, 64), 1))
    rep = dot(spread, closing_ref[...]).astype(BF16)
    tile = one_hot(iota((64, 256), 1) % 64 == iota((64, 256), 0))
    full = dot(rep, tile)
    keep = iota((256, 256), 0) // 64 == iota((256, 256), 1) // 64
    block = jnp.where(keep, full, 0.0).astype(BF16)
    out_ref[...] = dot(gated[...].astype(BF16), block, TN).astype(BF16)


def close(parts, gate, closing):
    return pl.pallas_call(
        closing_kernel,
        out_shape=jax.ShapeDtypeStruct((256, 256), BF16),
        scratch_shapes=[pltpu.VMEM((256, 256), F32)],
        cost_estimate=pl.CostEstimate(
            flops=60_000_000, bytes_accessed=1_000_000, transcendentals=0
        ),
        name="closing",
    )(parts, gate, closing)


def exchange(x, axes):
    return lax.all_to_all(x, axes, split_axis=0, concat_axis=0, tiled=True)


def shards(
    sequence_features,
    pair_window_rows,
    residue_mask,
    sequence_validity,
    pair_head_weight,
    content_projection,
    sigmoid_projection,
    closing_projection,
):
    mask2 = jnp.concatenate([residue_mask, residue_mask]).reshape(1, 128)
    logits = pair_logits(pair_window_rows, mask2, pair_head_weight.T)
    logits = exchange(logits.reshape(16, 32, 128), GROUP)
    values, gate = msa_values(
        sequence_features,
        sequence_validity.reshape(1, 256),
        content_projection,
        sigmoid_projection,
    )
    values = exchange(values.reshape(16, 512, 128), GROUP)
    mine = local_stats(logits)
    swap = ((0, 1), (1, 0))
    both = tuple((k, 3 - k) for k in range(4))
    stats = (
        mine,
        lax.ppermute(mine, "core", swap),
        lax.ppermute(mine, "zh", swap),
        lax.ppermute(mine, ("zh", "core"), both),
    )
    weights = softmax_weights(logits, stats)
    gathered = [weights] + [
        lax.ppermute(weights, "seq", [(k, (k + d) % 4) for k in range(4)])
        for d in (1, 2, 3)
    ]
    q = lax.axis_index("seq")
    place = (q - jnp.arange(4, dtype=jnp.int32)) % 4
    parts = partial_average(place, gathered, values.reshape(16, 8, 64, 128))
    parts = exchange(parts, RES)
    return close(parts, gate, closing_projection)


def solution(mesh):
    fine = Mesh(mesh.devices.reshape(4, 4, 2, 4, 2), ("seq",) + RES)
    return jax.shard_map(
        shards,
        mesh=fine,
        in_specs=(
            P("seq", RES),
            P("seq", RES, None),
            P(RES),
            P("seq"),
            P(),
            P(),
            P(),
            P(),
        ),
        out_specs=P("seq", RES),
        check_vma=False,
    )
```

time: 1080 us -> 101 us (0.09)
  blocking collectives: 899 us -> 30.4 us
  local copies, waits for them, and re-layouts: 69.3 us -> 9.84 us
  waiting for transfers between devices: 66.2 us -> 19.3 us
  starting transfers between devices: 6.59 us -> 24.2 us
  Pallas kernels: 0 us -> 15.5 us
  between operations: 13.7 us -> 0.07 us
  matrix products: 12.8 us -> 0 us
    pmax x1 -> x0, blocking collectives: 410 us -> none  [shards(): row_top = lax.pmax(local_top, 'res')]
    psum x1 -> x0, blocking collectives: 400 us -> none  [shards(): totals = lax.psum(jnp.sum(exponents, axis=1), 'res')]
    all_gather x1 -> x0, waiting for transfers between devices: 54.5 us -> none  [shards(): lax.all_gather(window_weights, 'res', axis=1, tiled=True)]
    all_to_all x1, blocking collectives: 74.6 us -> 30.4 us  [exchange(): return lax.all_to_all(x, axes, split_axis=0, concat_axis=0, tiled=True)]
    ppermute x0 -> x6, waiting for transfers between devices: none -> 19.3 us  [the longest x3 11.9 us: shards(): lax.ppermute(weights, 'seq', [(k, (k + d) % 4) for k in range(4)])]
    unnamed x21 -> x26, local copies, waits for them, and re-layouts: 27.9 us -> 9.84 us
    all_to_all x3 -> x0, local copies, waits for them, and re-layouts: 16.2 us -> none  [the longest x2 14.7 us: shards(): lax.all_to_all(values, 'res', split_axis=0, concat_axis=1, tiled=True)]
    pallas_call x0 -> x6, Pallas kernels: none -> 15.5 us  [the longest x1 4.72 us: msa_values(): pl.pallas_call(values_kernel, grid=(4,), out_shape=(jax.ShapeDtypeStruct(...]
  transfers between devices with their start and end apart: 2 -> 8, of which waited for: 2 -> 5; matrix products, arithmetic and copies ran while one was open for 4% -> 0% of each run, Pallas kernels for 0% -> 8%
where the time goes in v1:
time: 101 us; the launch traced here: 100 us
  blocking collectives  30.4 us (30%)
  starting transfers between devices  24.2 us (24%)
  waiting for transfers between devices  19.3 us (19%)
  Pallas kernels  15.5 us (15%)
  local copies, waits for them, and re-layouts  9.84 us (10%)
    all_to_all x1, blocking collectives, exchange(): return lax.all_to_all(x, axes, split_axis=0, concat_axis=0, tiled=True)  30.4 us
    all_to_all x2, starting transfers between devices, exchange(): return lax.all_to_all(x, axes, split_axis=0, concat_axis=0, tiled=True)  14.3 us
    ppermute x3, waiting for transfers between devices, shards(): lax.ppermute(weights, 'seq', [(k, (k + d) % 4) for k in range(4)])  11.9 us
    unnamed x26, local copies, waits for them, and re-layouts  9.84 us
    ppermute x1, starting transfers between devices, shards(): lax.ppermute(mine, 'zh', swap)  6.28 us
    ppermute x1, waiting for transfers between devices, shards(): lax.ppermute(mine, ('zh', 'core'), both)  5.19 us
    pallas_call x1, Pallas kernels, msa_values(): pl.pallas_call(values_kernel, grid=(4,), out_shape=(jax.ShapeDtypeStruct(...  4.72 us
    ppermute x3, starting transfers between devices, shards(): lax.ppermute(weights, 'seq', [(k, (k + d) % 4) for k in range(4)])  3.51 us
  transfers between devices with their start and end apart: 8, of which 5 were waited for; matrix products, arithmetic and copies ran while one was open for 0% of the time, Pallas kernels for 8%

profile of v1, /device:TPU:32, one launch (start us, length us, event | category | flops | bytes accessed | tf_op | source)
XLA Modules:
  0.0 100.1 jit_solution(16372625058002894933)
XLA Ops:
  0.0 0.8 add_bitcast_fusion.mask_ref
  0.8 0.0 copy-start.4
  0.8 1.2 %copy-done.4 = bf16[64,64,128]{2,1,0:T(8,128)(2,1)S(1)} copy-done((bf16[64,64,128]{2,1,0:T(8,128)(2,1)S(1)}, bf16[64,64,128]{2,1,0:T(8,128)(2,1)}, u32[]{:S(2)}) %copy-start.4) | copy-done | bytes 1048600
  2.0 0.0 copy-start.7
  2.0 0.7 copy-done.7
  2.7 3.4 %pair_logits.1 = f32[8,2,32,128]{3,2,1,0:T(8,128)} custom-call(bf16[64,64,128]{2,1,0:T(8,128)(2,1)S(1)} %copy-done.4, s32[1,128]{1,0:T(1,128)S(1)} %add_bitcast_fusion.mask_ref, bf16[8,128]{1,0:T(8,128)(2,1)S(1)} %bitcast.9), custom_call_target="tpu_custom_call" | custom-call | flops 400000000 | bytes 1400000 | tf_op jit(solution)/shard_map/pair_logits/pallas_call | solution.py:59
  6.1 7.0 %all-to-all-start = ((f32[16,32,128]{2,1,0:T(8,128)}), f32[16,32,128]{2,1,0:T(8,128)S(1)}, u32[]{:S(2)}, u32[]{:S(2)}) async-start(f32[16,32,128]{2,1,0:T(8,128)} %bitcast.2), calls=%async_computation | async-start | bytes 524288 | tf_op jit(solution)/shard_map/all_to_all | solution.py:269
  13.2 0.0 copy-start.3
  13.2 1.6 %copy-done.3 = bf16[256,4096]{1,0:T(8,128)(2,1)S(1)} copy-done((bf16[256,4096]{1,0:T(8,128)(2,1)S(1)}, bf16[256,4096]{1,0:T(8,128)(2,1)}, u32[]{:S(2)}) %copy-start.3) | copy-done | bytes 2097176
  14.8 0.0 copy-start.5
  14.8 0.7 copy-done.5
  15.5 0.0 copy-start.6
  15.5 0.7 copy-done.6
  16.2 0.0 copy-start.8
  16.2 0.7 copy-done.8
  16.9 4.7 %msa_values.1 = (bf16[8,2,8,64,128]{4,3,2,1,0:T(8,128)(2,1)S(1)}, f32[256,256]{1,0:T(8,128)S(1)}) custom-call(bf16[256,4096]{1,0:T(8,128)(2,1)S(1)} %copy-done.3, s32[1,256]{1,0:T(1,128)S(1)} %bitcast.10, bf16[64,64]{1,0:T(8,128)(2,1)S(1)} %copy-done.5, bf16[64,64]{1,0:T(8,128)(2,1)S(1)} %copy-done.6), custom_call_target="tpu_custom_call" | custom-call | flops 2000000000 | bytes 4500000 | tf_op jit(solution)/shard_map/msa_values/pallas_call | solution.py:119
  21.6 0.0 copy-start
  21.6 1.3 %copy-done = bf16[8,2,8,64,128]{4,3,2,1,0:T(8,128)(2,1)} copy-done((bf16[8,2,8,64,128]{4,3,2,1,0:T(8,128)(2,1)}, bf16[8,2,8,64,128]{4,3,2,1,0:T(8,128)(2,1)S(1)}, u32[]{:S(2)}) %copy-start) | copy-done | bytes 2097176
  22.9 0.0 copy-start.2
  22.9 0.7 copy-done.2
  23.7 0.0 all-to-all-done.l_ref
  23.7 0.0 copy-start.9
  23.7 0.7 copy-done.9
  24.4 7.2 %all-to-all-start.1 = ((bf16[16,512,128]{2,1,0:T(8,128)(2,1)}), bf16[16,512,128]{2,1,0:T(8,128)(2,1)S(1)}, u32[]{:S(2)}, u32[]{:S(2)}) async-start(bf16[16,512,128]{2,1,0:T(8,128)(2,1)} %bitcast.8), calls=%async_computation.1 | async-start | bytes 4194304 | tf_op jit(solution)/shard_map/all_to_all | solution.py:269
  31.6 1.8 %local_stats.1.a_ref = f32[2,32,128]{2,1,0:T(8,128)} custom-call(f32[16,32,128]{2,1,0:T(8,128)} %copy-done.9), custom_call_target="tpu_custom_call" | custom-call | flops 200000 | bytes 300000 | tf_op jit(solution)/shard_map/local_stats/pallas_call | solution.py:161
  33.4 0.0 collective-permute-start
  33.4 6.3 %collective-permute-start.1 = (f32[2,32,128]{2,1,0:T(8,128)}, f32[2,32,128]{2,1,0:T(8,128)S(1)}, u32[]{:S(2)}, u32[]{:S(2)}) collective-permute-start(f32[2,32,128]{2,1,0:T(8,128)} %local_stats.1.a_ref), channel_id=1, source_target_pairs={{0,8},{8,0},{1,9},{9,1},{2,10},{10,2},{3,11},{11,3},{4,12},{12,4},... | collective-permute-start | bytes 98312 | tf_op jit(solution)/shard_map/ppermute | solution.py:298
  39.7 0.1 collective-permute-start.2
  39.9 0.0 collective-permute-done.b_ref
  39.9 0.0 copy-start.10
  39.9 2.1 %collective-permute-done.1.c_ref = f32[2,32,128]{2,1,0:T(8,128)S(1)} collective-permute-done((f32[2,32,128]{2,1,0:T(8,128)}, f32[2,32,128]{2,1,0:T(8,128)S(1)}, u32[]{:S(2)}, u32[]{:S(2)}) %collective-permute-start.1) | collective-permute-done | bytes 32800 | tf_op jit(solution)/shard_map/ppermute | solution.py:298
  42.0 0.0 copy-start.11
  42.0 5.2 %collective-permute-done.2.d_ref = f32[2,32,128]{2,1,0:T(8,128)S(1)} collective-permute-done((f32[2,32,128]{2,1,0:T(8,128)}, f32[2,32,128]{2,1,0:T(8,128)S(1)}, u32[]{:S(2)}, u32[]{:S(2)}) %collective-permute-start.2) | collective-permute-done | bytes 32800 | tf_op jit(solution)/shard_map/ppermute | solution.py:299
  47.2 0.0 copy-done.10
  47.2 0.0 copy-done.11
  47.2 0.0 copy-start.12
  47.2 0.6 copy-done.12
  47.8 1.8 %softmax_weights.1.w0 = bf16[64,1024]{1,0:T(8,128)(2,1)} custom-call(f32[16,32,128]{2,1,0:T(8,128)} %copy-done.9, f32[2,32,128]{2,1,0:T(8,128)} %local_stats.1.a_ref, f32[2,32,128]{2,1,0:T(8,128)} %copy-done.10, f32[2,32,128]{2,1,0:T(8,128)} %copy-done.11, f32[2,32,128]{2,1,0:T(8,128)} %copy-done.12), custom_call_target="tpu_custom_call" | custom-call | flops 200000 | bytes 500000 | tf_op jit(solution)/shard_map/softmax_weights/pallas_call | solution.py:188
  49.6 1.0 %collective-permute-start.3 = (bf16[64,1024]{1,0:T(8,128)(2,1)}, bf16[64,1024]{1,0:T(8,128)(2,1)S(1)}, u32[]{:S(2)}, u32[]{:S(2)}) collective-permute-start(bf16[64,1024]{1,0:T(8,128)(2,1)} %softmax_weights.1.w0), channel_id=1, source_target_pairs={{0,64},{64,128},{128,192},{192,0},{1,65},{65,129},{129,193},{193,1... | collective-permute-start | bytes 393224 | tf_op jit(solution)/shard_map/ppermute | solution.py:303
  50.6 2.4 %collective-permute-start.4 = (bf16[64,1024]{1,0:T(8,128)(2,1)}, bf16[64,1024]{1,0:T(8,128)(2,1)S(1)}, u32[]{:S(2)}, u32[]{:S(2)}) collective-permute-start(bf16[64,1024]{1,0:T(8,128)(2,1)} %softmax_weights.1.w0), channel_id=1, source_target_pairs={{0,128},{64,192},{128,0},{192,64},{1,129},{65,193},{129,1},{193,65... | collective-permute-start | bytes 393224 | tf_op jit(solution)/shard_map/ppermute | solution.py:303
  52.9 0.1 collective-permute-start.5
  53.1 3.0 %collective-permute-done.3.w1 = bf16[64,1024]{1,0:T(8,128)(2,1)S(1)} collective-permute-done((bf16[64,1024]{1,0:T(8,128)(2,1)}, bf16[64,1024]{1,0:T(8,128)(2,1)S(1)}, u32[]{:S(2)}, u32[]{:S(2)}) %collective-permute-start.3) | collective-permute-done | bytes 131104 | tf_op jit(solution)/shard_map/ppermute | solution.py:303
  56.1 6.4 %collective-permute-done.4.w2 = bf16[64,1024]{1,0:T(8,128)(2,1)S(1)} collective-permute-done((bf16[64,1024]{1,0:T(8,128)(2,1)}, bf16[64,1024]{1,0:T(8,128)(2,1)S(1)}, u32[]{:S(2)}, u32[]{:S(2)}) %collective-permute-start.4) | collective-permute-done | bytes 131104 | tf_op jit(solution)/shard_map/ppermute | solution.py:303
  62.5 2.6 %collective-permute-done.5.w3 = bf16[64,1024]{1,0:T(8,128)(2,1)S(1)} collective-permute-done((bf16[64,1024]{1,0:T(8,128)(2,1)}, bf16[64,1024]{1,0:T(8,128)(2,1)S(1)}, u32[]{:S(2)}, u32[]{:S(2)}) %collective-permute-start.5) | collective-permute-done | bytes 131104 | tf_op jit(solution)/shard_map/ppermute | solution.py:303
  65.0 0.0 all-to-all-done.1
  65.0 0.0 copy-start.1
  65.0 0.9 copy-done.1
  65.9 1.5 %partial_average.1 = bf16[64,32,128]{2,1,0:T(8,128)(2,1)S(1)} custom-call(s32[4]{0:T(128)S(1)} %and_select_fusion.place_ref, bf16[64,1024]{1,0:T(8,128)(2,1)S(1)} %copy-done.1, bf16[64,1024]{1,0:T(8,128)(2,1)S(1)} %collective-permute-done.3.w1, bf16[64,1024]{1,0:T(8,128)(2,1)S(1)} %collective-permute-done.4.w2, ...), custom_call_target="tpu_custom_call" | custom-call | flops 600000000 | bytes 3100000 | tf_op jit(solution)/shard_map/partial_average/pallas_call | solution.py:220
  67.4 30.4 %all_to_all.15.p_ref = bf16[64,32,128]{2,1,0:T(8,128)(2,1)} all-to-all(bf16[64,32,128]{2,1,0:T(8,128)(2,1)S(1)} %partial_average.1), channel_id=1, replica_groups=mesh['seq'=4,'y'=4,'zh'=2,'x'=4,'core'=2] {'y','zh','x','core'}, dimensions={0} | all-to-all | bytes 1048576 | tf_op jit(solution)/shard_map/all_to_all | solution.py:269
  97.8 2.3 %closing.1 = bf16[256,256]{1,0:T(8,128)(2,1)} custom-call(bf16[64,32,128]{2,1,0:T(8,128)(2,1)} %all_to_all.15.p_ref, f32[256,256]{1,0:T(8,128)} %copy-done.2, bf16[64,64]{1,0:T(8,128)(2,1)} %closing_ref.1), custom_call_target="tpu_custom_call" | custom-call | flops 60000000 | bytes 1000000 | tf_op jit(solution)/shard_map/closing/pallas_call | solution.py:257
  (1 shorter events, 0.0 us)
Async XLA Ops:
  0.8 1.2 %copy-start.4 = (bf16[64,64,128]{2,1,0:T(8,128)(2,1)S(1)}, bf16[64,64,128]{2,1,0:T(8,128)(2,1)}, u32[]{:S(2)}) copy-start(bf16[64,64,128]{2,1,0:T(8,128)(2,1)} %pair_ref.1) | copy-start | bytes 3145732
  2.0 0.7 copy-start.7
  6.1 17.5 %all-to-all-start = ((f32[16,32,128]{2,1,0:T(8,128)}), f32[16,32,128]{2,1,0:T(8,128)S(1)}, u32[]{:S(2)}, u32[]{:S(2)}) async-start(f32[16,32,128]{2,1,0:T(8,128)} %bitcast.2), calls=%async_computation | async-start | bytes 524288 | tf_op jit(solution)/shard_map/all_to_all | solution.py:269
  13.2 1.6 %copy-start.3 = (bf16[256,4096]{1,0:T(8,128)(2,1)S(1)}, bf16[256,4096]{1,0:T(8,128)(2,1)}, u32[]{:S(2)}) copy-start(bf16[256,4096]{1,0:T(8,128)(2,1)} %m_ref.1) | copy-start | bytes 6291460
  14.8 0.7 copy-start.5
  15.5 0.7 copy-start.6
  16.2 0.7 copy-start.8
  21.6 1.3 %copy-start = (bf16[8,2,8,64,128]{4,3,2,1,0:T(8,128)(2,1)}, bf16[8,2,8,64,128]{4,3,2,1,0:T(8,128)(2,1)S(1)}, u32[]{:S(2)}) copy-start(bf16[8,2,8,64,128]{4,3,2,1,0:T(8,128)(2,1)S(1)} %get-tuple-element.7) | copy-start | bytes 6291460
  22.9 0.7 copy-start.2
  23.7 0.7 copy-start.9
  24.4 40.7 %all-to-all-start.1 = ((bf16[16,512,128]{2,1,0:T(8,128)(2,1)}), bf16[16,512,128]{2,1,0:T(8,128)(2,1)S(1)}, u32[]{:S(2)}, u32[]{:S(2)}) async-start(bf16[16,512,128]{2,1,0:T(8,128)(2,1)} %bitcast.8), calls=%async_computation.1 | async-start | bytes 4194304 | tf_op jit(solution)/shard_map/all_to_all | solution.py:269
  33.4 6.4 %collective-permute-start = (f32[2,32,128]{2,1,0:T(8,128)}, f32[2,32,128]{2,1,0:T(8,128)S(1)}, u32[]{:S(2)}, u32[]{:S(2)}) collective-permute-start(f32[2,32,128]{2,1,0:T(8,128)} %local_stats.1.a_ref), channel_id=1, source_target_pairs={{0,1},{1,0},{2,3},{3,2},{4,5},{5,4},{6,7},{7,6},{8,9},{9,8},{10,11... | collective-permute-start | bytes 98312 | tf_op jit(solution)/shard_map/ppermute | solution.py:297
  33.4 8.5 %collective-permute-start.1 = (f32[2,32,128]{2,1,0:T(8,128)}, f32[2,32,128]{2,1,0:T(8,128)S(1)}, u32[]{:S(2)}, u32[]{:S(2)}) collective-permute-start(f32[2,32,128]{2,1,0:T(8,128)} %local_stats.1.a_ref), channel_id=1, source_target_pairs={{0,8},{8,0},{1,9},{9,1},{2,10},{10,2},{3,11},{11,3},{4,12},{12,4},... | collective-permute-start | bytes 98312 | tf_op jit(solution)/shard_map/ppermute | solution.py:298
  39.7 7.5 %collective-permute-start.2 = (f32[2,32,128]{2,1,0:T(8,128)}, f32[2,32,128]{2,1,0:T(8,128)S(1)}, u32[]{:S(2)}, u32[]{:S(2)}) collective-permute-start(f32[2,32,128]{2,1,0:T(8,128)} %local_stats.1.a_ref), channel_id=1, source_target_pairs={{0,9},{1,8},{8,1},{9,0},{2,11},{3,10},{10,3},{11,2},{4,13},{5,12},... | collective-permute-start | bytes 98312 | tf_op jit(solution)/shard_map/ppermute | solution.py:299
  39.9 7.3 %copy-start.10 = (f32[2,32,128]{2,1,0:T(8,128)}, f32[2,32,128]{2,1,0:T(8,128)S(1)}, u32[]{:S(2)}) copy-start(f32[2,32,128]{2,1,0:T(8,128)S(1)} %collective-permute-done.b_ref) | copy-start | bytes 98308
  42.0 5.2 %copy-start.11 = (f32[2,32,128]{2,1,0:T(8,128)}, f32[2,32,128]{2,1,0:T(8,128)S(1)}, u32[]{:S(2)}) copy-start(f32[2,32,128]{2,1,0:T(8,128)S(1)} %collective-permute-done.1.c_ref) | copy-start | bytes 98308
  47.2 0.6 copy-start.12
  49.6 6.5 %collective-permute-start.3 = (bf16[64,1024]{1,0:T(8,128)(2,1)}, bf16[64,1024]{1,0:T(8,128)(2,1)S(1)}, u32[]{:S(2)}, u32[]{:S(2)}) collective-permute-start(bf16[64,1024]{1,0:T(8,128)(2,1)} %softmax_weights.1.w0), channel_id=1, source_target_pairs={{0,64},{64,128},{128,192},{192,0},{1,65},{65,129},{129,193},{193,1... | collective-permute-start | bytes 393224 | tf_op jit(solution)/shard_map/ppermute | solution.py:303
  50.6 11.9 %collective-permute-start.4 = (bf16[64,1024]{1,0:T(8,128)(2,1)}, bf16[64,1024]{1,0:T(8,128)(2,1)S(1)}, u32[]{:S(2)}, u32[]{:S(2)}) collective-permute-start(bf16[64,1024]{1,0:T(8,128)(2,1)} %softmax_weights.1.w0), channel_id=1, source_target_pairs={{0,128},{64,192},{128,0},{192,64},{1,129},{65,193},{129,1},{193,65... | collective-permute-start | bytes 393224 | tf_op jit(solution)/shard_map/ppermute | solution.py:303
  52.9 12.1 %collective-permute-start.5 = (bf16[64,1024]{1,0:T(8,128)(2,1)}, bf16[64,1024]{1,0:T(8,128)(2,1)S(1)}, u32[]{:S(2)}, u32[]{:S(2)}) collective-permute-start(bf16[64,1024]{1,0:T(8,128)(2,1)} %softmax_weights.1.w0), channel_id=1, source_target_pairs={{0,192},{64,0},{128,64},{192,128},{1,193},{65,1},{129,65},{193,129... | collective-permute-start | bytes 393224 | tf_op jit(solution)/shard_map/ppermute | solution.py:303
  65.0 0.9 copy-start.1

commit v2 on v1

--- a/solution.py
+++ b/solution.py
@@ -16,7 +16,7 @@
 TN = (((0,), (0,)), ((), ()))
 GROUP = ("y", "x")
 RES = ("y", "zh", "x", "core")
-VMEM_LIMIT = 48 * 1024 * 1024
+SMALL_LIMIT = 24 * 1024 * 1024
 
 
 def dot(a, b, dims=NN):
@@ -45,7 +45,7 @@
     logits = lax.dot_general(
         weight_ref[...], normed, NT, preferred_element_type=F32
     )
-    mask = mask_ref[...]
+    mask = jnp.concatenate([mask_ref[...], mask_ref[...]], axis=1)
     for k in range(rows // 128):
         part = jnp.where(mask == 1, logits[:, k * 128 : (k + 1) * 128], -1000000000.0)
         scr[pl.ds(k, 8, stride=rows // 128), :] = part
@@ -54,7 +54,7 @@
         out_ref[:, sg, pl.ds(step * (rows // 128), rows // 128), :] = block
 
 
-def pair_logits(pair, mask2, weight_t):
+def pair_logits(pair, mask, weight_t):
     steps = 4
     return pl.pallas_call(
         logits_kernel,
@@ -62,17 +62,16 @@
         out_shape=jax.ShapeDtypeStruct((8, 2, 32, 128), F32),
         in_specs=[
             pl.BlockSpec((64 // steps, 64, 128), lambda i: (i, 0, 0)),
-            pl.BlockSpec((1, 128), lambda i: (0, 0)),
+            pl.BlockSpec((1, 64), lambda i: (0, 0)),
             pl.BlockSpec((8, 128), lambda i: (0, 0)),
         ],
         out_specs=pl.BlockSpec((8, 2, 32, 128), lambda i: (0, 0, 0, 0)),
         scratch_shapes=[pltpu.VMEM((64 * 32 // 8 // steps, 128), F32)],
-        compiler_params=pltpu.CompilerParams(vmem_limit_bytes=VMEM_LIMIT),
         cost_estimate=pl.CostEstimate(
             flops=400_000_000, bytes_accessed=1_400_000, transcendentals=500_000
         ),
         name="pair_logits",
-    )(pair, mask2, weight_t)
+    )(pair, mask, weight_t)
 
 
 def values_kernel(m_ref, valid_ref, content_ref, sigmoid_ref, v_ref, gate_ref, wbig):
@@ -134,7 +133,6 @@
             pl.BlockSpec((256, 256), lambda i: (0, 0)),
         ),
         scratch_shapes=[pltpu.VMEM((512, 512), BF16)],
-        compiler_params=pltpu.CompilerParams(vmem_limit_bytes=VMEM_LIMIT),
         cost_estimate=pl.CostEstimate(
             flops=2_000_000_000, bytes_accessed=4_500_000, transcendentals=100_000
         ),
@@ -161,6 +159,7 @@
     return pl.pallas_call(
         stats_kernel,
         out_shape=jax.ShapeDtypeStruct((2, 32, 128), F32),
+        compiler_params=pltpu.CompilerParams(vmem_limit_bytes=SMALL_LIMIT),
         cost_estimate=pl.CostEstimate(
             flops=200_000, bytes_accessed=300_000, transcendentals=65536
         ),
@@ -168,7 +167,7 @@
     )(logits)
 
 
-def weights_kernel(l_ref, a_ref, b_ref, c_ref, d_ref, out_ref):
+def weights_kernel(l_ref, a_ref, b_ref, c_ref, d_ref, out_ref, own_ref):
     refs = (a_ref, b_ref, c_ref, d_ref)
     top = jnp.maximum(
         jnp.maximum(a_ref[0], b_ref[0]), jnp.maximum(c_ref[0], d_ref[0])
@@ -180,14 +179,16 @@
         b = jnp.exp(l_ref[2 * k + 1] - top) / total
         even = jnp.where(low, a, pltpu.roll(b, 64, 1))
         odd = jnp.where(low, pltpu.roll(a, 64, 1), b)
-        out_ref[0:32, k * 128 : (k + 1) * 128] = even.astype(BF16)
-        out_ref[32:64, k * 128 : (k + 1) * 128] = odd.astype(BF16)
+        block = jnp.concatenate([even, odd], axis=0).astype(BF16)
+        out_ref[:, k * 128 : (k + 1) * 128] = block
+        own_ref[:, k * 128 : (k + 1) * 128] = block
 
 
 def softmax_weights(logits, stats):
     return pl.pallas_call(
         weights_kernel,
-        out_shape=jax.ShapeDtypeStruct((64, 1024), BF16),
+        out_shape=(jax.ShapeDtypeStruct((64, 1024), BF16),) * 2,
+        compiler_params=pltpu.CompilerParams(vmem_limit_bytes=SMALL_LIMIT),
         cost_estimate=pl.CostEstimate(
             flops=200_000, bytes_accessed=500_000, transcendentals=65536
         ),
@@ -223,7 +224,7 @@
         in_specs=[pl.BlockSpec(memory_space=pltpu.SMEM)] + [vmem] * 5,
         out_specs=vmem,
         scratch_shapes=[pltpu.VMEM((256, 1024), BF16), pltpu.VMEM((2048, 128), F32)],
-        compiler_params=pltpu.CompilerParams(vmem_limit_bytes=VMEM_LIMIT),
+        compiler_params=pltpu.CompilerParams(vmem_limit_bytes=SMALL_LIMIT),
         cost_estimate=pl.CostEstimate(
             flops=600_000_000, bytes_accessed=3_100_000, transcendentals=0
         ),
@@ -258,6 +259,7 @@
         closing_kernel,
         out_shape=jax.ShapeDtypeStruct((256, 256), BF16),
         scratch_shapes=[pltpu.VMEM((256, 256), F32)],
+        compiler_params=pltpu.CompilerParams(vmem_limit_bytes=SMALL_LIMIT),
         cost_estimate=pl.CostEstimate(
             flops=60_000_000, bytes_accessed=1_000_000, transcendentals=0
         ),
@@ -279,8 +281,7 @@
     sigmoid_projection,
     closing_projection,
 ):
-    mask2 = jnp.concatenate([residue_mask, residue_mask]).reshape(1, 128)
-    logits = pair_logits(pair_window_rows, mask2, pair_head_weight.T)
+    logits = pair_logits(pair_window_rows, residue_mask.reshape(1, 64), pair_head_weight.T)
     logits = exchange(logits.reshape(16, 32, 128), GROUP)
     values, gate = msa_values(
         sequence_features,
@@ -298,8 +299,8 @@
         lax.ppermute(mine, "zh", swap),
         lax.ppermute(mine, ("zh", "core"), both),
     )
-    weights = softmax_weights(logits, stats)
-    gathered = [weights] + [
+    weights, own = softmax_weights(logits, stats)
+    gathered = [own] + [
         lax.ppermute(weights, "seq", [(k, (k + d) % 4) for k in range(4)])
         for d in (1, 2, 3)
     ]

time: 101 us -> 90.8 us (0.90)
  local copies, waits for them, and re-layouts: 9.84 us -> 0.01 us
  waiting for transfers between devices: 19.3 us -> 21.4 us
  starting transfers between devices: 24.2 us -> 22.7 us
  blocking collectives: 30.4 us -> 31.6 us
  Pallas kernels: 15.5 us -> 14.4 us
    unnamed x26 -> x4, local copies, waits for them, and re-layouts: 9.84 us -> 0.01 us
    all_to_all x2, waiting for transfers between devices: 0.01 us -> 2.86 us  [exchange(): return lax.all_to_all(x, axes, split_axis=0, concat_axis=0, tiled=True)]
    pallas_call x1, Pallas kernels: 4.72 us -> 6.74 us  [msa_values(): pl.pallas_call(values_kernel, grid=(4,), out_shape=(jax.ShapeDtypeStruct(...]
    all_to_all x2, starting transfers between devices: 14.3 us -> 12.3 us  [exchange(): return lax.all_to_all(x, axes, split_axis=0, concat_axis=0, tiled=True)]
    pallas_call x1, Pallas kernels: 1.78 us -> 0.14 us  [softmax_weights(): pl.pallas_call(weights_kernel, out_shape=(jax.ShapeDtypeStruct((64, 1024)...]
    pallas_call x1, Pallas kernels: 1.84 us -> 0.24 us  [local_stats(): pl.pallas_call(stats_kernel, out_shape=jax.ShapeDtypeStruct((2, 32, 128),...]
    pallas_call x1, Pallas kernels: 3.43 us -> 4.66 us  [pair_logits(): pl.pallas_call(logits_kernel, grid=(steps,), out_shape=jax.ShapeDtypeStru...]
    all_to_all x1, blocking collectives: 30.4 us -> 31.6 us  [exchange(): return lax.all_to_all(x, axes, split_axis=0, concat_axis=0, tiled=True)]
  transfers between devices with their start and end apart: 8 -> 8, of which waited for: 5 -> 7; matrix products, arithmetic and copies ran while one was open for 0% -> 0% of each run, Pallas kernels for 8% -> 8%
where the time goes in v2:
time: 90.8 us; the launch traced here: 90.1 us
  blocking collectives  31.6 us (35%)
  starting transfers between devices  22.7 us (25%)
  waiting for transfers between devices  21.4 us (24%)
  Pallas kernels  14.4 us (16%)
    all_to_all x1, blocking collectives, exchange(): return lax.all_to_all(x, axes, split_axis=0, concat_axis=0, tiled=True)  31.6 us
    all_to_all x2, starting transfers between devices, exchange(): return lax.all_to_all(x, axes, split_axis=0, concat_axis=0, tiled=True)  12.3 us
    ppermute x3, waiting for transfers between devices, shards(): lax.ppermute(weights, 'seq', [(k, (k + d) % 4) for k in range(4)])  11.4 us
    pallas_call x1, Pallas kernels, msa_values(): pl.pallas_call(values_kernel, grid=(4,), out_shape=(jax.ShapeDtypeStruct(...  6.74 us
    ppermute x1, starting transfers between devices, shards(): lax.ppermute(mine, 'zh', swap)  6.36 us
    ppermute x1, waiting for transfers between devices, shards(): lax.ppermute(mine, ('zh', 'core'), both)  5.31 us
    pallas_call x1, Pallas kernels, pair_logits(): pl.pallas_call(logits_kernel, grid=(steps,), out_shape=jax.ShapeDtypeStru...  4.66 us
    ppermute x3, starting transfers between devices, shards(): lax.ppermute(weights, 'seq', [(k, (k + d) % 4) for k in range(4)])  3.9 us
  transfers between devices with their start and end apart: 8, of which 7 were waited for; matrix products, arithmetic and copies ran while one was open for 0% of the time, Pallas kernels for 8%

profile of v2, /device:TPU:32, one launch (start us, length us, event | category | flops | bytes accessed | tf_op | source)
XLA Modules:
  0.0 90.1 jit_solution(12130717461213405314)
XLA Ops:
  0.0 4.7 %pair_logits.1 = f32[8,2,32,128]{3,2,1,0:T(8,128)} custom-call(bf16[64,64,128]{2,1,0:T(8,128)(2,1)} %pair_ref.1, s32[1,64]{1,0:T(1,128)} %bitcast.11, bf16[8,128]{1,0:T(8,128)(2,1)} %bitcast.9), custom_call_target="tpu_custom_call" | custom-call | flops 400000000 | bytes 1400000 | tf_op jit(solution)/shard_map/pair_logits/pallas_call | solution.py:59
  4.7 7.0 %all-to-all-start = ((f32[16,32,128]{2,1,0:T(8,128)}), f32[16,32,128]{2,1,0:T(8,128)S(1)}, u32[]{:S(2)}, u32[]{:S(2)}) async-start(f32[16,32,128]{2,1,0:T(8,128)} %bitcast.8), calls=%async_computation | async-start | bytes 524288 | tf_op jit(solution)/shard_map/all_to_all | solution.py:271
  11.7 6.7 %msa_values.1 = (bf16[8,2,8,64,128]{4,3,2,1,0:T(8,128)(2,1)}, f32[256,256]{1,0:T(8,128)}) custom-call(bf16[256,4096]{1,0:T(8,128)(2,1)} %m_ref.1, s32[1,256]{1,0:T(1,128)} %bitcast.10, bf16[64,64]{1,0:T(8,128)(2,1)} %content_ref.1, bf16[64,64]{1,0:T(8,128)(2,1)} %sigmoid_ref.1), custom_call_target="tpu_custom_call" | custom-call | flops 2000000000 | bytes 4500000 | tf_op jit(solution)/shard_map/msa_values/pallas_call | solution.py:118
  18.4 1.9 %all-to-all-done.l_ref = f32[16,32,128]{2,1,0:T(8,128)S(1)} async-done(((f32[16,32,128]{2,1,0:T(8,128)}), f32[16,32,128]{2,1,0:T(8,128)S(1)}, u32[]{:S(2)}, u32[]{:S(2)}) %all-to-all-start) | async-done | bytes 262176 | tf_op jit(solution)/shard_map/all_to_all | solution.py:271
  20.4 5.3 %all-to-all-start.1 = ((bf16[16,512,128]{2,1,0:T(8,128)(2,1)}), bf16[16,512,128]{2,1,0:T(8,128)(2,1)S(1)}, u32[]{:S(2)}, u32[]{:S(2)}) async-start(bf16[16,512,128]{2,1,0:T(8,128)(2,1)} %bitcast.7), calls=%async_computation.1 | async-start | bytes 4194304 | tf_op jit(solution)/shard_map/all_to_all | solution.py:271
  25.7 0.2 local_stats.1.a_ref
  25.9 0.1 collective-permute-start
  26.0 6.4 %collective-permute-start.1 = (f32[2,32,128]{2,1,0:T(8,128)S(1)}, f32[2,32,128]{2,1,0:T(8,128)S(1)}, u32[]{:S(2)}, u32[]{:S(2)}) collective-permute-start(f32[2,32,128]{2,1,0:T(8,128)S(1)} %local_stats.1.a_ref), channel_id=1, source_target_pairs={{0,8},{8,0},{1,9},{9,1},{2,10},{10,2},{3,11},{11,3},{4,12},{12,4},... | collective-permute-start | bytes 98312 | tf_op jit(solution)/shard_map/ppermute | solution.py:299
  32.4 0.1 collective-permute-start.2
  32.4 0.0 collective-permute-done.b_ref
  32.4 1.9 %collective-permute-done.1.c_ref = f32[2,32,128]{2,1,0:T(8,128)S(1)} collective-permute-done((f32[2,32,128]{2,1,0:T(8,128)S(1)}, f32[2,32,128]{2,1,0:T(8,128)S(1)}, u32[]{:S(2)}, u32[]{:S(2)}) %collective-permute-start.1) | collective-permute-done | bytes 32800 | tf_op jit(solution)/shard_map/ppermute | solution.py:299
  34.3 5.3 %collective-permute-done.2.d_ref = f32[2,32,128]{2,1,0:T(8,128)S(1)} collective-permute-done((f32[2,32,128]{2,1,0:T(8,128)S(1)}, f32[2,32,128]{2,1,0:T(8,128)S(1)}, u32[]{:S(2)}, u32[]{:S(2)}) %collective-permute-start.2) | collective-permute-done | bytes 32800 | tf_op jit(solution)/shard_map/ppermute | solution.py:300
  39.6 0.1 softmax_weights.1
  39.8 1.1 %collective-permute-start.3 = (bf16[64,1024]{1,0:T(8,128)(2,1)S(1)}, bf16[64,1024]{1,0:T(8,128)(2,1)S(1)}, u32[]{:S(2)}, u32[]{:S(2)}) collective-permute-start(bf16[64,1024]{1,0:T(8,128)(2,1)S(1)} %get-tuple-element.10), channel_id=1, source_target_pairs={{0,64},{64,128},{128,192},{192,0},{1,65},{65,129},{129,193},{193,1... | collective-permute-start | bytes 393224 | tf_op jit(solution)/shard_map/ppermute | solution.py:304
  40.9 2.5 %collective-permute-start.4 = (bf16[64,1024]{1,0:T(8,128)(2,1)S(1)}, bf16[64,1024]{1,0:T(8,128)(2,1)S(1)}, u32[]{:S(2)}, u32[]{:S(2)}) collective-permute-start(bf16[64,1024]{1,0:T(8,128)(2,1)S(1)} %get-tuple-element.10), channel_id=1, source_target_pairs={{0,128},{64,192},{128,0},{192,64},{1,129},{65,193},{129,1},{193,65... | collective-permute-start | bytes 393224 | tf_op jit(solution)/shard_map/ppermute | solution.py:304
  43.4 0.3 collective-permute-start.5
  43.7 2.5 %collective-permute-done.3.w1 = bf16[64,1024]{1,0:T(8,128)(2,1)S(1)} collective-permute-done((bf16[64,1024]{1,0:T(8,128)(2,1)S(1)}, bf16[64,1024]{1,0:T(8,128)(2,1)S(1)}, u32[]{:S(2)}, u32[]{:S(2)}) %collective-permute-start.3) | collective-permute-done | bytes 131104 | tf_op jit(solution)/shard_map/ppermute | solution.py:304
  46.2 6.2 %collective-permute-done.4.w2 = bf16[64,1024]{1,0:T(8,128)(2,1)S(1)} collective-permute-done((bf16[64,1024]{1,0:T(8,128)(2,1)S(1)}, bf16[64,1024]{1,0:T(8,128)(2,1)S(1)}, u32[]{:S(2)}, u32[]{:S(2)}) %collective-permute-start.4) | collective-permute-done | bytes 131104 | tf_op jit(solution)/shard_map/ppermute | solution.py:304
  52.4 2.7 %collective-permute-done.5.w3 = bf16[64,1024]{1,0:T(8,128)(2,1)S(1)} collective-permute-done((bf16[64,1024]{1,0:T(8,128)(2,1)S(1)}, bf16[64,1024]{1,0:T(8,128)(2,1)S(1)}, u32[]{:S(2)}, u32[]{:S(2)}) %collective-permute-start.5) | collective-permute-done | bytes 131104 | tf_op jit(solution)/shard_map/ppermute | solution.py:304
  55.1 0.9 %all-to-all-done.1 = bf16[16,512,128]{2,1,0:T(8,128)(2,1)S(1)} async-done(((bf16[16,512,128]{2,1,0:T(8,128)(2,1)}), bf16[16,512,128]{2,1,0:T(8,128)(2,1)S(1)}, u32[]{:S(2)}, u32[]{:S(2)}) %all-to-all-start.1) | async-done | bytes 2097184 | tf_op jit(solution)/shard_map/all_to_all | solution.py:271
  56.0 0.0 copy-start
  56.0 0.0 copy-start.1
  56.0 1.5 %partial_average.1 = bf16[64,32,128]{2,1,0:T(8,128)(2,1)S(1)} custom-call(s32[4]{0:T(128)S(1)} %and_select_fusion.place_ref, bf16[64,1024]{1,0:T(8,128)(2,1)S(1)} %get-tuple-element.9.w0, bf16[64,1024]{1,0:T(8,128)(2,1)S(1)} %collective-permute-done.3.w1, bf16[64,1024]{1,0:T(8,128)(2,1)S(1)} %collective-permute-done.4.w2, ...), custom_call_target="tpu_custom_call" | custom-call | flops 600000000 | bytes 3100000 | tf_op jit(solution)/shard_map/partial_average/pallas_call | solution.py:221
  57.5 31.6 %all_to_all.15.p_ref = bf16[64,32,128]{2,1,0:T(8,128)(2,1)S(1)} all-to-all(bf16[64,32,128]{2,1,0:T(8,128)(2,1)S(1)} %partial_average.1), channel_id=1, replica_groups=mesh['seq'=4,'y'=4,'zh'=2,'x'=4,'core'=2] {'y','zh','x','core'}, dimensions={0} | all-to-all | bytes 1048576 | tf_op jit(solution)/shard_map/all_to_all | solution.py:271
  89.0 0.0 copy-done
  89.0 0.0 copy-done.1
  89.0 1.1 %closing.1 = bf16[256,256]{1,0:T(8,128)(2,1)} custom-call(bf16[64,32,128]{2,1,0:T(8,128)(2,1)S(1)} %all_to_all.15.p_ref, f32[256,256]{1,0:T(8,128)S(1)} %copy-done, bf16[64,64]{1,0:T(8,128)(2,1)S(1)} %copy-done.1), custom_call_target="tpu_custom_call" | custom-call | flops 60000000 | bytes 1000000 | tf_op jit(solution)/shard_map/closing/pallas_call | solution.py:258
  (1 shorter events, 0.0 us)
Async XLA Ops:
  4.7 15.7 %all-to-all-start = ((f32[16,32,128]{2,1,0:T(8,128)}), f32[16,32,128]{2,1,0:T(8,128)S(1)}, u32[]{:S(2)}, u32[]{:S(2)}) async-start(f32[16,32,128]{2,1,0:T(8,128)} %bitcast.8), calls=%async_computation | async-start | bytes 524288 | tf_op jit(solution)/shard_map/all_to_all | solution.py:271
  20.4 35.6 %all-to-all-start.1 = ((bf16[16,512,128]{2,1,0:T(8,128)(2,1)}), bf16[16,512,128]{2,1,0:T(8,128)(2,1)S(1)}, u32[]{:S(2)}, u32[]{:S(2)}) async-start(bf16[16,512,128]{2,1,0:T(8,128)(2,1)} %bitcast.7), calls=%async_computation.1 | async-start | bytes 4194304 | tf_op jit(solution)/shard_map/all_to_all | solution.py:271
  25.9 6.5 %collective-permute-start = (f32[2,32,128]{2,1,0:T(8,128)S(1)}, f32[2,32,128]{2,1,0:T(8,128)S(1)}, u32[]{:S(2)}, u32[]{:S(2)}) collective-permute-start(f32[2,32,128]{2,1,0:T(8,128)S(1)} %local_stats.1.a_ref), channel_id=1, source_target_pairs={{0,1},{1,0},{2,3},{3,2},{4,5},{5,4},{6,7},{7,6},{8,9},{9,8},{10,11... | collective-permute-start | bytes 98312 | tf_op jit(solution)/shard_map/ppermute | solution.py:298
  26.0 8.3 %collective-permute-start.1 = (f32[2,32,128]{2,1,0:T(8,128)S(1)}, f32[2,32,128]{2,1,0:T(8,128)S(1)}, u32[]{:S(2)}, u32[]{:S(2)}) collective-permute-start(f32[2,32,128]{2,1,0:T(8,128)S(1)} %local_stats.1.a_ref), channel_id=1, source_target_pairs={{0,8},{8,0},{1,9},{9,1},{2,10},{10,2},{3,11},{11,3},{4,12},{12,4},... | collective-permute-start | bytes 98312 | tf_op jit(solution)/shard_map/ppermute | solution.py:299
  32.4 7.3 %collective-permute-start.2 = (f32[2,32,128]{2,1,0:T(8,128)S(1)}, f32[2,32,128]{2,1,0:T(8,128)S(1)}, u32[]{:S(2)}, u32[]{:S(2)}) collective-permute-start(f32[2,32,128]{2,1,0:T(8,128)S(1)} %local_stats.1.a_ref), channel_id=1, source_target_pairs={{0,9},{1,8},{8,1},{9,0},{2,11},{3,10},{10,3},{11,2},{4,13},{5,12},... | collective-permute-start | bytes 98312 | tf_op jit(solution)/shard_map/ppermute | solution.py:300
  39.8 6.4 %collective-permute-start.3 = (bf16[64,1024]{1,0:T(8,128)(2,1)S(1)}, bf16[64,1024]{1,0:T(8,128)(2,1)S(1)}, u32[]{:S(2)}, u32[]{:S(2)}) collective-permute-start(bf16[64,1024]{1,0:T(8,128)(2,1)S(1)} %get-tuple-element.10), channel_id=1, source_target_pairs={{0,64},{64,128},{128,192},{192,0},{1,65},{65,129},{129,193},{193,1... | collective-permute-start | bytes 393224 | tf_op jit(solution)/shard_map/ppermute | solution.py:304
  40.9 11.5 %collective-permute-start.4 = (bf16[64,1024]{1,0:T(8,128)(2,1)S(1)}, bf16[64,1024]{1,0:T(8,128)(2,1)S(1)}, u32[]{:S(2)}, u32[]{:S(2)}) collective-permute-start(bf16[64,1024]{1,0:T(8,128)(2,1)S(1)} %get-tuple-element.10), channel_id=1, source_target_pairs={{0,128},{64,192},{128,0},{192,64},{1,129},{65,193},{129,1},{193,65... | collective-permute-start | bytes 393224 | tf_op jit(solution)/shard_map/ppermute | solution.py:304
  43.4 11.7 %collective-permute-start.5 = (bf16[64,1024]{1,0:T(8,128)(2,1)S(1)}, bf16[64,1024]{1,0:T(8,128)(2,1)S(1)}, u32[]{:S(2)}, u32[]{:S(2)}) collective-permute-start(bf16[64,1024]{1,0:T(8,128)(2,1)S(1)} %get-tuple-element.10), channel_id=1, source_target_pairs={{0,192},{64,0},{128,64},{192,128},{1,193},{65,1},{129,65},{193,129... | collective-permute-start | bytes 393224 | tf_op jit(solution)/shard_map/ppermute | solution.py:304
  56.0 33.0 %copy-start = (f32[256,256]{1,0:T(8,128)S(1)}, f32[256,256]{1,0:T(8,128)}, u32[]{:S(2)}) copy-start(f32[256,256]{1,0:T(8,128)} %get-tuple-element.12.gate_ref) | copy-start | bytes 786436
  56.0 33.0 %copy-start.1 = (bf16[64,64]{1,0:T(8,128)(2,1)S(1)}, bf16[64,64]{1,0:T(8,128)(2,1)}, u32[]{:S(2)}) copy-start(bf16[64,64]{1,0:T(8,128)(2,1)} %closing_ref.1) | copy-start | bytes 24580

commit v3 on v2

--- a/solution.py
+++ b/solution.py
@@ -15,7 +15,8 @@
 NN = (((1,), (0,)), ((), ()))
 TN = (((0,), (0,)), ((), ()))
 GROUP = ("y", "x")
-RES = ("y", "zh", "x", "core")
+CHIPS = ("y", "zh", "x")
+RES = CHIPS + ("core",)
 SMALL_LIMIT = 24 * 1024 * 1024
 
 
@@ -42,16 +43,18 @@
     low = (square - high.astype(F32)).astype(BF16)
     variance = dot(high, mean_m) + dot(low, mean_m)
     normed = (centered * lax.rsqrt(variance + EPS)).astype(BF16)
-    logits = lax.dot_general(
-        weight_ref[...], normed, NT, preferred_element_type=F32
-    )
+    logits = dot(weight_ref[...], normed, NT)
     mask = jnp.concatenate([mask_ref[...], mask_ref[...]], axis=1)
     for k in range(rows // 128):
         part = jnp.where(mask == 1, logits[:, k * 128 : (k + 1) * 128], -1000000000.0)
-        scr[pl.ds(k, 8, stride=rows // 128), :] = part
-    block = scr[...].reshape(8, rows // 128, 128)
-    for sg in range(2):
-        out_ref[:, sg, pl.ds(step * (rows // 128), rows // 128), :] = block
+        row = step * (rows // 256) + (k // 2 % 2) * 16 + k // 4 * 2 + k % 2
+        scr[pl.ds(row, 8, stride=32), :] = part
+
+    @pl.when(step == pl.num_programs(0) - 1)
+    def _():
+        block = scr[...].reshape(8, 32, 128)
+        for sg in range(2):
+            out_ref[:, sg] = block
 
 
 def pair_logits(pair, mask, weight_t):
@@ -66,7 +69,7 @@
             pl.BlockSpec((8, 128), lambda i: (0, 0)),
         ],
         out_specs=pl.BlockSpec((8, 2, 32, 128), lambda i: (0, 0, 0, 0)),
-        scratch_shapes=[pltpu.VMEM((64 * 32 // 8 // steps, 128), F32)],
+        scratch_shapes=[pltpu.VMEM((256, 128), F32)],
         cost_estimate=pl.CostEstimate(
             flops=400_000_000, bytes_accessed=1_400_000, transcendentals=500_000
         ),
@@ -94,11 +97,10 @@
         centered = xt - mean
         variance = jnp.sum(centered * centered, axis=1, keepdims=True) * (1.0 / 64)
         parts.append((centered * lax.rsqrt(variance + EPS)).astype(BF16).reshape(256, 256))
-    valid = valid_ref[...].astype(F32)
     halves = []
     for k in range(2):
         normed = jnp.concatenate(parts[2 * k : 2 * k + 2], axis=0)
-        halves.append((dot(wbig[...], normed) * valid).reshape(64, 8, 256))
+        halves.append(dot(wbig[...], normed).reshape(64, 8, 256))
     both = jnp.concatenate(halves, axis=1).astype(BF16).reshape(8, 8, 16, 256)
     v_ref[:, 0] = both[..., :128]
     v_ref[:, 1] = both[..., 128:]
@@ -111,7 +113,7 @@
         full = dot(rep, tile)
         keep = iota((256, 256), 0) // 64 == iota((256, 256), 1) // 64
         wgate = jnp.where(keep, full, 0.0).astype(BF16)
-        gate_ref[...] = jax.nn.sigmoid(dot(wgate, parts[0]))
+        gate_ref[...] = jax.nn.sigmoid(dot(wgate, parts[0])) * valid_ref[...].astype(F32)
 
 
 def msa_values(m, valid, content, sigmoid):
@@ -167,24 +169,42 @@
     )(logits)
 
 
-def weights_kernel(l_ref, a_ref, b_ref, c_ref, d_ref, out_ref, own_ref):
-    refs = (a_ref, b_ref, c_ref, d_ref)
-    top = jnp.maximum(
-        jnp.maximum(a_ref[0], b_ref[0]), jnp.maximum(c_ref[0], d_ref[0])
-    )
-    total = sum(r[1] * jnp.exp(r[0] - top) for r in refs)
+def merge(a, b):
+    top = jnp.maximum(a[0], b[0])
+    return top, a[1] * jnp.exp(a[0] - top) + b[1] * jnp.exp(b[0] - top)
+
+
+def merge_kernel(a_ref, b_ref, out_ref):
+    out_ref[0], out_ref[1] = merge(a_ref, b_ref)
+
+
+def merge_stats(a, b):
+    return pl.pallas_call(
+        merge_kernel,
+        out_shape=jax.ShapeDtypeStruct((2, 32, 128), F32),
+        compiler_params=pltpu.CompilerParams(vmem_limit_bytes=SMALL_LIMIT),
+        cost_estimate=pl.CostEstimate(
+            flops=20_000, bytes_accessed=100_000, transcendentals=8192
+        ),
+        name="merge_stats",
+    )(a, b)
+
+
+def weights_kernel(l_ref, a_ref, b_ref, out_ref, own_ref):
+    top, total = merge(a_ref, b_ref)
     low = iota((32, 128), 1) < 64
     for k in range(8):
         a = jnp.exp(l_ref[2 * k] - top) / total
         b = jnp.exp(l_ref[2 * k + 1] - top) / total
         even = jnp.where(low, a, pltpu.roll(b, 64, 1))
         odd = jnp.where(low, pltpu.roll(a, 64, 1), b)
-        block = jnp.concatenate([even, odd], axis=0).astype(BF16)
+        block = jnp.concatenate([even[:16], odd[:16], even[16:], odd[16:]], axis=0)
+        block = block.astype(BF16)
         out_ref[:, k * 128 : (k + 1) * 128] = block
         own_ref[:, k * 128 : (k + 1) * 128] = block
 
 
-def softmax_weights(logits, stats):
+def softmax_weights(logits, a, b):
     return pl.pallas_call(
         weights_kernel,
         out_shape=(jax.ShapeDtypeStruct((64, 1024), BF16),) * 2,
@@ -193,13 +213,14 @@
             flops=200_000, bytes_accessed=500_000, transcendentals=65536
         ),
         name="softmax_weights",
-    )(logits, *stats)
+    )(logits, a, b)
 
 
 def average_kernel(place_ref, w0, w1, w2, w3, v_ref, out_ref, wall, scr):
+    side = pl.multiple_of(place_ref[4] * 32, 32)
     for k, w in enumerate((w0, w1, w2, w3)):
-        start = pl.multiple_of(place_ref[k] * 64, 64)
-        wall[pl.ds(start, 64), :] = w[...]
+        start = pl.multiple_of(place_ref[k] * 32, 32)
+        wall[pl.ds(start, 32), :] = w[pl.ds(side, 32), :]
     weights = wall[...]
     for c2 in range(4):
         right = jnp.concatenate(
@@ -209,38 +230,50 @@
         for e in range(2):
             for q in range(4):
                 for par in range(2):
-                    row = q * 64 + par * 32
-                    scr[pl.ds((q * 64 + par) * 8 + 2 * c2 + e, 32, stride=16), :] = part[
-                        row : row + 32, e * 128 : (e + 1) * 128
+                    row = q * 32 + par * 16
+                    scr[pl.ds(q * 256 + par * 8 + 2 * c2 + e, 16, stride=16), :] = part[
+                        row : row + 16, e * 128 : (e + 1) * 128
                     ]
-    out_ref[...] = scr[...].astype(BF16).reshape(64, 32, 128)
-
-
-def partial_average(place, weights, values):
+    out_ref[...] = scr[...].astype(out_ref.dtype).reshape(32, 32, 128)
+
+
+def partial_average(place, weights, values, dtype):
     vmem = pl.BlockSpec(memory_space=pltpu.VMEM)
     return pl.pallas_call(
         average_kernel,
-        out_shape=jax.ShapeDtypeStruct((64, 32, 128), BF16),
+        out_shape=jax.ShapeDtypeStruct((32, 32, 128), dtype),
         in_specs=[pl.BlockSpec(memory_space=pltpu.SMEM)] + [vmem] * 5,
         out_specs=vmem,
-        scratch_shapes=[pltpu.VMEM((256, 1024), BF16), pltpu.VMEM((2048, 128), F32)],
-        compiler_params=pltpu.CompilerParams(vmem_limit_bytes=SMALL_LIMIT),
-        cost_estimate=pl.CostEstimate(
-            flops=600_000_000, bytes_accessed=3_100_000, transcendentals=0
+        scratch_shapes=[pltpu.VMEM((128, 1024), BF16), pltpu.VMEM((1024, 128), F32)],
+        compiler_params=pltpu.CompilerParams(vmem_limit_bytes=SMALL_LIMIT),
+        cost_estimate=pl.CostEstimate(
+            flops=300_000_000, bytes_accessed=2_800_000, transcendentals=0
         ),
         name="partial_average",
     )(place, *weights, values)
+
+
+def add_kernel(a_ref, b_ref, out_ref):
+    out_ref[...] = (a_ref[...] + b_ref[...].astype(F32)).astype(BF16)
+
+
+def add_cores(a, b):
+    return pl.pallas_call(
+        add_kernel,
+        out_shape=jax.ShapeDtypeStruct((32, 32, 128), BF16),
+        compiler_params=pltpu.CompilerParams(vmem_limit_bytes=SMALL_LIMIT),
+        cost_estimate=pl.CostEstimate(
+            flops=200_000, bytes_accessed=1_000_000, transcendentals=0
+        ),
+        name="add_cores",
+    )(a, b)
 
 
 def closing_kernel(p_ref, gate_ref, closing_ref, out_ref, gated):
     for y in range(4):
         for x in range(4):
             head, half = 2 * y + x // 2, x % 2
-            total = sum(
-                p_ref[y * 16 + zh * 8 + x * 2 + core].astype(F32)
-                for zh in range(2)
-                for core in range(2)
-            )
+            total = p_ref[y * 8 + x].astype(F32) + p_ref[y * 8 + 4 + x].astype(F32)
             cols = slice(half * 128, half * 128 + 128)
             for i in range(4):
                 rows = slice(i * 64 + head * 8, i * 64 + head * 8 + 8)
@@ -290,24 +323,21 @@
         sigmoid_projection,
     )
     values = exchange(values.reshape(16, 512, 128), GROUP)
+    swap = ((0, 1), (1, 0))
     mine = local_stats(logits)
-    swap = ((0, 1), (1, 0))
-    both = tuple((k, 3 - k) for k in range(4))
-    stats = (
-        mine,
-        lax.ppermute(mine, "core", swap),
-        lax.ppermute(mine, "zh", swap),
-        lax.ppermute(mine, ("zh", "core"), both),
-    )
-    weights, own = softmax_weights(logits, stats)
+    mine = merge_stats(mine, lax.ppermute(mine, "core", swap))
+    weights, own = softmax_weights(logits, mine, lax.ppermute(mine, "zh", swap))
     gathered = [own] + [
         lax.ppermute(weights, "seq", [(k, (k + d) % 4) for k in range(4)])
         for d in (1, 2, 3)
     ]
-    q = lax.axis_index("seq")
-    place = (q - jnp.arange(4, dtype=jnp.int32)) % 4
-    parts = partial_average(place, gathered, values.reshape(16, 8, 64, 128))
-    parts = exchange(parts, RES)
+    q, core = lax.axis_index("seq"), lax.axis_index("core")
+    order = [(q - d) % 4 for d in range(4)]
+    values = values.reshape(16, 8, 64, 128)
+    theirs = partial_average(jnp.stack(order + [1 - core]), gathered, values, BF16)
+    theirs = lax.ppermute(theirs, "core", swap)
+    ours = partial_average(jnp.stack(order + [core]), gathered, values, F32)
+    parts = exchange(add_cores(ours, theirs), CHIPS)
     return close(parts, gate, closing_projection)
 
 

time: 90.8 us -> 85.4 us (0.941)
  blocking collectives: 31.6 us -> 25.1 us
  starting transfers between devices: 22.7 us -> 24.7 us
  waiting for transfers between devices: 21.4 us -> 19.8 us
    all_to_all x1, blocking collectives: 31.6 us -> 25.1 us  [exchange(): return lax.all_to_all(x, axes, split_axis=0, concat_axis=0, tiled=True)]
    all_to_all x2, waiting for transfers between devices: 2.86 us -> 8.58 us  [exchange(): return lax.all_to_all(x, axes, split_axis=0, concat_axis=0, tiled=True)]
    ppermute x3, waiting for transfers between devices: 7.22 us -> 3.45 us  [the longest x1 1.89 us: shards(): weights, own = softmax_weights(logits, mine, lax.ppermute(mine, 'zh', swap))]
    ppermute x3, waiting for transfers between devices: 11.4 us -> 7.74 us  [shards(): lax.ppermute(weights, 'seq', [(k, (k + d) % 4) for k in range(4)])]
    ppermute x3, starting transfers between devices: 3.9 us -> 5.92 us  [shards(): lax.ppermute(weights, 'seq', [(k, (k + d) % 4) for k in range(4)])]
    pallas_call x1 -> x4, Pallas kernels: 1.47 us -> 2.2 us  [the longest x2 2.11 us: partial_average(): pl.pallas_call(average_kernel, out_shape=jax.ShapeDtypeStruct((32, 32, 12...]
  transfers between devices with their start and end apart: 8 -> 8, of which waited for: 7 -> 8; matrix products, arithmetic and copies ran while one was open for 0% -> 0% of each run, Pallas kernels for 8% -> 10%
where the time goes in v3:
time: 85.4 us; the launch traced here: 85 us
  blocking collectives  25.1 us (29%)
  starting transfers between devices  24.7 us (29%)
  waiting for transfers between devices  19.8 us (23%)
  Pallas kernels  15.1 us (18%)
    all_to_all x1, blocking collectives, exchange(): return lax.all_to_all(x, axes, split_axis=0, concat_axis=0, tiled=True)  25.1 us
    all_to_all x2, starting transfers between devices, exchange(): return lax.all_to_all(x, axes, split_axis=0, concat_axis=0, tiled=True)  12.3 us
    all_to_all x2, waiting for transfers between devices, exchange(): return lax.all_to_all(x, axes, split_axis=0, concat_axis=0, tiled=True)  8.58 us
    ppermute x3, waiting for transfers between devices, shards(): lax.ppermute(weights, 'seq', [(k, (k + d) % 4) for k in range(4)])  7.74 us
    pallas_call x1, Pallas kernels, msa_values(): pl.pallas_call(values_kernel, grid=(4,), out_shape=(jax.ShapeDtypeStruct(...  6.72 us
    ppermute x1, starting transfers between devices, shards(): weights, own = softmax_weights(logits, mine, lax.ppermute(mine, 'zh', swap))  6.38 us
    ppermute x3, starting transfers between devices, shards(): lax.ppermute(weights, 'seq', [(k, (k + d) % 4) for k in range(4)])  5.92 us
    pallas_call x1, Pallas kernels, pair_logits(): pl.pallas_call(logits_kernel, grid=(steps,), out_shape=jax.ShapeDtypeStru...  4.66 us
  transfers between devices with their start and end apart: 8, of which 8 were waited for; matrix products, arithmetic and copies ran while one was open for 0% of the time, Pallas kernels for 10%

profile of v3, /device:TPU:32, one launch (start us, length us, event | category | flops | bytes accessed | tf_op | source)
XLA Modules:
  0.0 85.0 jit_solution(8714808062059453202)
XLA Ops:
  0.0 4.7 %pair_logits.1 = f32[8,2,32,128]{3,2,1,0:T(8,128)} custom-call(bf16[64,64,128]{2,1,0:T(8,128)(2,1)} %pair_ref.1, s32[1,64]{1,0:T(1,128)} %bitcast.18, bf16[8,128]{1,0:T(8,128)(2,1)} %bitcast.16), custom_call_target="tpu_custom_call" | custom-call | flops 400000000 | bytes 1400000 | tf_op jit(solution)/shard_map/pair_logits/pallas_call | solution.py:62
  4.7 7.0 %all-to-all-start = ((f32[16,32,128]{2,1,0:T(8,128)}), f32[16,32,128]{2,1,0:T(8,128)S(1)}, u32[]{:S(2)}, u32[]{:S(2)}) async-start(f32[16,32,128]{2,1,0:T(8,128)} %bitcast.15), calls=%async_computation | async-start | bytes 524288 | tf_op jit(solution)/shard_map/all_to_all | solution.py:304
  11.7 6.7 %msa_values.1 = (bf16[8,2,8,64,128]{4,3,2,1,0:T(8,128)(2,1)}, f32[256,256]{1,0:T(8,128)}) custom-call(bf16[256,4096]{1,0:T(8,128)(2,1)} %m_ref.1, s32[1,256]{1,0:T(1,128)} %bitcast.17, bf16[64,64]{1,0:T(8,128)(2,1)} %content_ref.1, bf16[64,64]{1,0:T(8,128)(2,1)} %sigmoid_ref.1), custom_call_target="tpu_custom_call" | custom-call | flops 2000000000 | bytes 4500000 | tf_op jit(solution)/shard_map/msa_values/pallas_call | solution.py:120
  18.4 2.0 %all-to-all-done.l_ref = f32[16,32,128]{2,1,0:T(8,128)S(1)} async-done(((f32[16,32,128]{2,1,0:T(8,128)}), f32[16,32,128]{2,1,0:T(8,128)S(1)}, u32[]{:S(2)}, u32[]{:S(2)}) %all-to-all-start) | async-done | bytes 262176 | tf_op jit(solution)/shard_map/all_to_all | solution.py:304
  20.4 5.2 %all-to-all-start.1 = ((bf16[16,512,128]{2,1,0:T(8,128)(2,1)}), bf16[16,512,128]{2,1,0:T(8,128)(2,1)S(1)}, u32[]{:S(2)}, u32[]{:S(2)}) async-start(bf16[16,512,128]{2,1,0:T(8,128)(2,1)} %bitcast.14), calls=%async_computation.1 | async-start | bytes 4194304 | tf_op jit(solution)/shard_map/all_to_all | solution.py:304
  25.6 0.2 local_stats.1.a_ref
  25.9 0.1 collective-permute-start
  26.0 1.2 %collective-permute-done.b_ref = f32[2,32,128]{2,1,0:T(8,128)S(1)} collective-permute-done((f32[2,32,128]{2,1,0:T(8,128)S(1)}, f32[2,32,128]{2,1,0:T(8,128)S(1)}, u32[]{:S(2)}, u32[]{:S(2)}) %collective-permute-start) | collective-permute-done | bytes 32800 | tf_op jit(solution)/shard_map/ppermute | solution.py:328
  27.2 6.4 %collective-permute-start.1 = (f32[2,32,128]{2,1,0:T(8,128)S(1)}, f32[2,32,128]{2,1,0:T(8,128)S(1)}, u32[]{:S(2)}, u32[]{:S(2)}) collective-permute-start(f32[2,32,128]{2,1,0:T(8,128)S(1)} %merge_stats.1.a_ref), channel_id=1, source_target_pairs={{0,8},{8,0},{1,9},{9,1},{2,10},{10,2},{3,11},{11,3},{4,12},{12,4},... | collective-permute-start | bytes 98312 | tf_op jit(solution)/shard_map/ppermute | solution.py:329
  33.6 1.9 %collective-permute-done.1.b_ref = f32[2,32,128]{2,1,0:T(8,128)S(1)} collective-permute-done((f32[2,32,128]{2,1,0:T(8,128)S(1)}, f32[2,32,128]{2,1,0:T(8,128)S(1)}, u32[]{:S(2)}, u32[]{:S(2)}) %collective-permute-start.1) | collective-permute-done | bytes 32800 | tf_op jit(solution)/shard_map/ppermute | solution.py:329
  35.5 0.1 softmax_weights.1
  35.6 1.1 %collective-permute-start.4 = (bf16[64,1024]{1,0:T(8,128)(2,1)S(1)}, bf16[64,1024]{1,0:T(8,128)(2,1)S(1)}, u32[]{:S(2)}, u32[]{:S(2)}) collective-permute-start(bf16[64,1024]{1,0:T(8,128)(2,1)S(1)} %get-tuple-element.10), channel_id=1, source_target_pairs={{0,192},{64,0},{128,64},{192,128},{1,193},{65,1},{129,65},{193,129... | collective-permute-start | bytes 393224 | tf_op jit(solution)/shard_map/ppermute | solution.py:331
  36.7 2.5 %collective-permute-start.3 = (bf16[64,1024]{1,0:T(8,128)(2,1)S(1)}, bf16[64,1024]{1,0:T(8,128)(2,1)S(1)}, u32[]{:S(2)}, u32[]{:S(2)}) collective-permute-start(bf16[64,1024]{1,0:T(8,128)(2,1)S(1)} %get-tuple-element.10), channel_id=1, source_target_pairs={{0,128},{64,192},{128,0},{192,64},{1,129},{65,193},{129,1},{193,65... | collective-permute-start | bytes 393224 | tf_op jit(solution)/shard_map/ppermute | solution.py:331
  39.2 2.3 %collective-permute-start.2 = (bf16[64,1024]{1,0:T(8,128)(2,1)S(1)}, bf16[64,1024]{1,0:T(8,128)(2,1)S(1)}, u32[]{:S(2)}, u32[]{:S(2)}) collective-permute-start(bf16[64,1024]{1,0:T(8,128)(2,1)S(1)} %get-tuple-element.10), channel_id=1, source_target_pairs={{0,64},{64,128},{128,192},{192,0},{1,65},{65,129},{129,193},{193,1... | collective-permute-start | bytes 393224 | tf_op jit(solution)/shard_map/ppermute | solution.py:331
  41.5 0.1 stack.35.place_ref
  41.6 1.0 %collective-permute-done.4.w3 = bf16[64,1024]{1,0:T(8,128)(2,1)S(1)} collective-permute-done((bf16[64,1024]{1,0:T(8,128)(2,1)S(1)}, bf16[64,1024]{1,0:T(8,128)(2,1)S(1)}, u32[]{:S(2)}, u32[]{:S(2)}) %collective-permute-start.4) | collective-permute-done | bytes 131104 | tf_op jit(solution)/shard_map/ppermute | solution.py:331
  42.6 4.9 %collective-permute-done.3.w2 = bf16[64,1024]{1,0:T(8,128)(2,1)S(1)} collective-permute-done((bf16[64,1024]{1,0:T(8,128)(2,1)S(1)}, bf16[64,1024]{1,0:T(8,128)(2,1)S(1)}, u32[]{:S(2)}, u32[]{:S(2)}) %collective-permute-start.3) | collective-permute-done | bytes 131104 | tf_op jit(solution)/shard_map/ppermute | solution.py:331
  47.5 1.8 %collective-permute-done.2.w1 = bf16[64,1024]{1,0:T(8,128)(2,1)S(1)} collective-permute-done((bf16[64,1024]{1,0:T(8,128)(2,1)S(1)}, bf16[64,1024]{1,0:T(8,128)(2,1)S(1)}, u32[]{:S(2)}, u32[]{:S(2)}) %collective-permute-start.2) | collective-permute-done | bytes 131104 | tf_op jit(solution)/shard_map/ppermute | solution.py:331
  49.3 6.6 %all-to-all-done.1 = bf16[16,512,128]{2,1,0:T(8,128)(2,1)S(1)} async-done(((bf16[16,512,128]{2,1,0:T(8,128)(2,1)}), bf16[16,512,128]{2,1,0:T(8,128)(2,1)S(1)}, u32[]{:S(2)}, u32[]{:S(2)}) %all-to-all-start.1) | async-done | bytes 2097184 | tf_op jit(solution)/shard_map/all_to_all | solution.py:304
  56.0 1.0 %partial_average.3 = bf16[32,32,128]{2,1,0:T(8,128)(2,1)S(1)} custom-call(s32[5]{0:T(128)S(1)} %stack.35.place_ref, bf16[64,1024]{1,0:T(8,128)(2,1)S(1)} %get-tuple-element.9.w0, bf16[64,1024]{1,0:T(8,128)(2,1)S(1)} %collective-permute-done.2.w1, bf16[64,1024]{1,0:T(8,128)(2,1)S(1)} %collective-permute-done.3.w2, ...), custom_call_target="tpu_custom_call" | custom-call | flops 300000000 | bytes 2800000 | tf_op jit(solution)/shard_map/partial_average/pallas_call | solution.py:242
  57.0 0.1 collective-permute-start.5
  57.1 0.1 stack.33.place_ref
  57.2 0.0 copy-start
  57.2 0.0 copy-start.1
  57.2 1.1 %partial_average.2.a_ref = f32[32,32,128]{2,1,0:T(8,128)S(1)} custom-call(s32[5]{0:T(128)S(1)} %stack.33.place_ref, bf16[64,1024]{1,0:T(8,128)(2,1)S(1)} %get-tuple-element.9.w0, bf16[64,1024]{1,0:T(8,128)(2,1)S(1)} %collective-permute-done.2.w1, bf16[64,1024]{1,0:T(8,128)(2,1)S(1)} %collective-permute-done.3.w2, ...), custom_call_target="tpu_custom_call" | custom-call | flops 300000000 | bytes 2800000 | tf_op jit(solution)/shard_map/partial_average/pallas_call | solution.py:242
  58.3 0.4 collective-permute-done.5.b_ref
  58.6 0.1 add_cores.1
  58.7 25.1 %all_to_all.15.p_ref = bf16[32,32,128]{2,1,0:T(8,128)(2,1)S(1)} all-to-all(bf16[32,32,128]{2,1,0:T(8,128)(2,1)S(1)} %add_cores.1), channel_id=1, replica_groups=mesh['seq'=4,'y'=4,'zh'=2,'x'=4,'core'=2] {'y','zh','x'}, dimensions={0} | all-to-all | bytes 524288 | tf_op jit(solution)/shard_map/all_to_all | solution.py:304
  83.8 0.0 copy-done
  83.8 0.0 copy-done.1
  83.8 1.1 %closing.1 = bf16[256,256]{1,0:T(8,128)(2,1)} custom-call(bf16[32,32,128]{2,1,0:T(8,128)(2,1)S(1)} %all_to_all.15.p_ref, f32[256,256]{1,0:T(8,128)S(1)} %copy-done, bf16[64,64]{1,0:T(8,128)(2,1)S(1)} %copy-done.1), custom_call_target="tpu_custom_call" | custom-call | flops 60000000 | bytes 1000000 | tf_op jit(solution)/shard_map/closing/pallas_call | solution.py:291
  (1 shorter events, 0.0 us)
Async XLA Ops:
  4.7 15.7 %all-to-all-start = ((f32[16,32,128]{2,1,0:T(8,128)}), f32[16,32,128]{2,1,0:T(8,128)S(1)}, u32[]{:S(2)}, u32[]{:S(2)}) async-start(f32[16,32,128]{2,1,0:T(8,128)} %bitcast.15), calls=%async_computation | async-start | bytes 524288 | tf_op jit(solution)/shard_map/all_to_all | solution.py:304
  20.4 35.6 %all-to-all-start.1 = ((bf16[16,512,128]{2,1,0:T(8,128)(2,1)}), bf16[16,512,128]{2,1,0:T(8,128)(2,1)S(1)}, u32[]{:S(2)}, u32[]{:S(2)}) async-start(bf16[16,512,128]{2,1,0:T(8,128)(2,1)} %bitcast.14), calls=%async_computation.1 | async-start | bytes 4194304 | tf_op jit(solution)/shard_map/all_to_all | solution.py:304
  25.9 1.3 %collective-permute-start = (f32[2,32,128]{2,1,0:T(8,128)S(1)}, f32[2,32,128]{2,1,0:T(8,128)S(1)}, u32[]{:S(2)}, u32[]{:S(2)}) collective-permute-start(f32[2,32,128]{2,1,0:T(8,128)S(1)} %local_stats.1.a_ref), channel_id=1, source_target_pairs={{0,1},{1,0},{2,3},{3,2},{4,5},{5,4},{6,7},{7,6},{8,9},{9,8},{10,11... | collective-permute-start | bytes 98312 | tf_op jit(solution)/shard_map/ppermute | solution.py:328
  27.2 8.3 %collective-permute-start.1 = (f32[2,32,128]{2,1,0:T(8,128)S(1)}, f32[2,32,128]{2,1,0:T(8,128)S(1)}, u32[]{:S(2)}, u32[]{:S(2)}) collective-permute-start(f32[2,32,128]{2,1,0:T(8,128)S(1)} %merge_stats.1.a_ref), channel_id=1, source_target_pairs={{0,8},{8,0},{1,9},{9,1},{2,10},{10,2},{3,11},{11,3},{4,12},{12,4},... | collective-permute-start | bytes 98312 | tf_op jit(solution)/shard_map/ppermute | solution.py:329
  35.6 7.0 %collective-permute-start.4 = (bf16[64,1024]{1,0:T(8,128)(2,1)S(1)}, bf16[64,1024]{1,0:T(8,128)(2,1)S(1)}, u32[]{:S(2)}, u32[]{:S(2)}) collective-permute-start(bf16[64,1024]{1,0:T(8,128)(2,1)S(1)} %get-tuple-element.10), channel_id=1, source_target_pairs={{0,192},{64,0},{128,64},{192,128},{1,193},{65,1},{129,65},{193,129... | collective-permute-start | bytes 393224 | tf_op jit(solution)/shard_map/ppermute | solution.py:331
  36.7 10.8 %collective-permute-start.3 = (bf16[64,1024]{1,0:T(8,128)(2,1)S(1)}, bf16[64,1024]{1,0:T(8,128)(2,1)S(1)}, u32[]{:S(2)}, u32[]{:S(2)}) collective-permute-start(bf16[64,1024]{1,0:T(8,128)(2,1)S(1)} %get-tuple-element.10), channel_id=1, source_target_pairs={{0,128},{64,192},{128,0},{192,64},{1,129},{65,193},{129,1},{193,65... | collective-permute-start | bytes 393224 | tf_op jit(solution)/shard_map/ppermute | solution.py:331
  39.2 10.1 %collective-permute-start.2 = (bf16[64,1024]{1,0:T(8,128)(2,1)S(1)}, bf16[64,1024]{1,0:T(8,128)(2,1)S(1)}, u32[]{:S(2)}, u32[]{:S(2)}) collective-permute-start(bf16[64,1024]{1,0:T(8,128)(2,1)S(1)} %get-tuple-element.10), channel_id=1, source_target_pairs={{0,64},{64,128},{128,192},{192,0},{1,65},{65,129},{129,193},{193,1... | collective-permute-start | bytes 393224 | tf_op jit(solution)/shard_map/ppermute | solution.py:331
  57.0 1.6 %collective-permute-start.5 = (bf16[32,32,128]{2,1,0:T(8,128)(2,1)S(1)}, bf16[32,32,128]{2,1,0:T(8,128)(2,1)S(1)}, u32[]{:S(2)}, u32[]{:S(2)}) collective-permute-start(bf16[32,32,128]{2,1,0:T(8,128)(2,1)S(1)} %partial_average.3), channel_id=1, source_target_pairs={{0,1},{1,0},{2,3},{3,2},{4,5},{5,4},{6,7},{7,6},{8,9},{9,8},{10,11... | collective-permute-start | bytes 786440 | tf_op jit(solution)/shard_map/ppermute | solution.py:338
  57.2 26.6 %copy-start = (f32[256,256]{1,0:T(8,128)S(1)}, f32[256,256]{1,0:T(8,128)}, u32[]{:S(2)}) copy-start(f32[256,256]{1,0:T(8,128)} %get-tuple-element.12.gate_ref) | copy-start | bytes 786436
  57.2 26.6 %copy-start.1 = (bf16[64,64]{1,0:T(8,128)(2,1)S(1)}, bf16[64,64]{1,0:T(8,128)(2,1)}, u32[]{:S(2)}) copy-start(bf16[64,64]{1,0:T(8,128)(2,1)} %closing_ref.1) | copy-start | bytes 24580

commit v4 on v3

--- a/solution.py
+++ b/solution.py
@@ -33,38 +33,28 @@
 
 
 def logits_kernel(pair_ref, mask_ref, weight_ref, out_ref, scr):
-    rows = pair_ref.shape[0] * pair_ref.shape[1]
-    step = pl.program_id(0)
-    x = pair_ref[...].reshape(rows, 128)
-    mean_m = jnp.full((128, 128), 1.0 / 128, BF16)
-    centered = x.astype(F32) - dot(x, mean_m)
-    square = centered * centered
-    high = square.astype(BF16)
-    low = (square - high.astype(F32)).astype(BF16)
-    variance = dot(high, mean_m) + dot(low, mean_m)
+    x = pair_ref[...].reshape(4096, 128)
+    centered = x.astype(F32) - dot(x, jnp.full((128, 128), 1.0 / 128, BF16))
+    variance = jnp.mean(centered * centered, axis=-1, keepdims=True)
     normed = (centered * lax.rsqrt(variance + EPS)).astype(BF16)
     logits = dot(weight_ref[...], normed, NT)
     mask = jnp.concatenate([mask_ref[...], mask_ref[...]], axis=1)
-    for k in range(rows // 128):
+    for k in range(32):
         part = jnp.where(mask == 1, logits[:, k * 128 : (k + 1) * 128], -1000000000.0)
-        row = step * (rows // 256) + (k // 2 % 2) * 16 + k // 4 * 2 + k % 2
+        row = (k // 2 % 2) * 16 + k // 4 * 2 + k % 2
         scr[pl.ds(row, 8, stride=32), :] = part
-
-    @pl.when(step == pl.num_programs(0) - 1)
-    def _():
-        block = scr[...].reshape(8, 32, 128)
-        for sg in range(2):
-            out_ref[:, sg] = block
+    block = scr[...].reshape(8, 32, 128)
+    for sg in range(2):
+        out_ref[:, sg] = block
 
 
 def pair_logits(pair, mask, weight_t):
-    steps = 4
     return pl.pallas_call(
         logits_kernel,
-        grid=(steps,),
+        grid=(1,),
         out_shape=jax.ShapeDtypeStruct((8, 2, 32, 128), F32),
         in_specs=[
-            pl.BlockSpec((64 // steps, 64, 128), lambda i: (i, 0, 0)),
+            pl.BlockSpec((64, 64, 128), lambda i: (0, 0, 0)),
             pl.BlockSpec((1, 64), lambda i: (0, 0)),
             pl.BlockSpec((8, 128), lambda i: (0, 0)),
         ],
@@ -77,69 +67,92 @@
     )(pair, mask, weight_t)
 
 
-def values_kernel(m_ref, valid_ref, content_ref, sigmoid_ref, v_ref, gate_ref, wbig):
-    step = pl.program_id(0)
-
-    @pl.when(step == 0)
+def diagonal(matrix, transposed=False, by_column=False):
+    rows = iota((256, 64), 0)
+    spread = one_hot((rows // 4 if by_column else rows % 64) == iota((256, 64), 1))
+    rep = dot(spread, matrix, NT if transposed else NN).astype(BF16)
+    tile = one_hot(iota((64, 256), 1) % 64 == iota((64, 256), 0))
+    copy = iota((256, 256), 0)
+    copy = copy % 4 if by_column else copy // 64
+    return jnp.where(copy == iota((256, 256), 1) // 64, dot(rep, tile), 0.0).astype(BF16)
+
+
+def normed_columns(block):
+    xt = block.T.astype(F32).reshape(4, 64, 256)
+    mean = jnp.sum(xt, axis=1, keepdims=True) * (1.0 / 64)
+    centered = xt - mean
+    variance = jnp.sum(centered * centered, axis=1, keepdims=True) * (1.0 / 64)
+    return (centered * lax.rsqrt(variance + EPS)).astype(BF16).reshape(256, 256)
+
+
+def values_kernel(m_ref, content_ref, v_ref, block):
+    @pl.when(pl.program_id(0) == 0)
     def _():
-        spread = one_hot(iota((512, 64), 0) // 8 == iota((512, 64), 1))
-        rep = dot(spread, content_ref[...], NT).astype(BF16)
-        tile = one_hot(iota((64, 512), 1) % 64 == iota((64, 512), 0))
-        full = dot(rep, tile)
-        keep = iota((512, 512), 0) % 8 == iota((512, 512), 1) // 64
-        wbig[...] = jnp.where(keep, full, 0.0).astype(BF16)
-
-    eye = one_hot(iota((256, 256), 0) == iota((256, 256), 1))
-    parts = []
-    for k in range(4):
-        xt = dot(eye, m_ref[:, k * 256 : (k + 1) * 256], NT).reshape(4, 64, 256)
-        mean = jnp.sum(xt, axis=1, keepdims=True) * (1.0 / 64)
-        centered = xt - mean
-        variance = jnp.sum(centered * centered, axis=1, keepdims=True) * (1.0 / 64)
-        parts.append((centered * lax.rsqrt(variance + EPS)).astype(BF16).reshape(256, 256))
-    halves = []
-    for k in range(2):
-        normed = jnp.concatenate(parts[2 * k : 2 * k + 2], axis=0)
-        halves.append(dot(wbig[...], normed).reshape(64, 8, 256))
-    both = jnp.concatenate(halves, axis=1).astype(BF16).reshape(8, 8, 16, 256)
-    v_ref[:, 0] = both[..., :128]
-    v_ref[:, 1] = both[..., 128:]
-
-    @pl.when(step == 0)
-    def _():
-        spread = one_hot(iota((256, 64), 0) % 64 == iota((256, 64), 1))
-        rep = dot(spread, sigmoid_ref[...], NT).astype(BF16)
-        tile = one_hot(iota((64, 256), 1) % 64 == iota((64, 256), 0))
-        full = dot(rep, tile)
-        keep = iota((256, 256), 0) // 64 == iota((256, 256), 1) // 64
-        wgate = jnp.where(keep, full, 0.0).astype(BF16)
-        gate_ref[...] = jax.nn.sigmoid(dot(wgate, parts[0])) * valid_ref[...].astype(F32)
-
-
-def msa_values(m, valid, content, sigmoid):
+        block[...] = diagonal(content_ref[...], transposed=True, by_column=True)
+
+    low = iota((32, 8, 256), 1) < 4
+    for part in range(m_ref.shape[1] // 1024):
+        eights = []
+        for k in range(2):
+            start = part * 1024 + k * 512
+            a, b = (
+                dot(block[...], normed_columns(m_ref[:, at : at + 256])).reshape(32, 8, 256)
+                for at in (start, start + 256)
+            )
+            even = jnp.where(low, a, pltpu.roll(b, 4, 1))
+            odd = jnp.where(low, pltpu.roll(a, 4, 1), b)
+            eights.append(jnp.stack([even, odd], axis=1).reshape(64, 8, 256))
+        both = jnp.concatenate(eights, axis=1).astype(BF16).reshape(8, 8, 16, 256)
+        rows = slice(part * 16, part * 16 + 16)
+        v_ref[:, 0, :, rows] = both[..., :128]
+        v_ref[:, 1, :, rows] = both[..., 128:]
+
+
+def msa_values(m, content):
     return pl.pallas_call(
         values_kernel,
-        grid=(4,),
-        out_shape=(
-            jax.ShapeDtypeStruct((8, 2, 8, 64, 128), BF16),
-            jax.ShapeDtypeStruct((256, 256), F32),
-        ),
+        grid=(2,),
+        out_shape=jax.ShapeDtypeStruct((8, 2, 8, 64, 128), BF16),
         in_specs=[
-            pl.BlockSpec((256, 1024), lambda i: (0, i)),
-            pl.BlockSpec((1, 256), lambda i: (0, 0)),
-            pl.BlockSpec((64, 64), lambda i: (0, 0)),
+            pl.BlockSpec((256, 2048), lambda i: (0, i)),
             pl.BlockSpec((64, 64), lambda i: (0, 0)),
         ],
-        out_specs=(
-            pl.BlockSpec((8, 2, 8, 16, 128), lambda i: (0, 0, 0, i, 0)),
-            pl.BlockSpec((256, 256), lambda i: (0, 0)),
-        ),
-        scratch_shapes=[pltpu.VMEM((512, 512), BF16)],
+        out_specs=pl.BlockSpec((8, 2, 8, 32, 128), lambda i: (0, 0, 0, i, 0)),
+        scratch_shapes=[pltpu.VMEM((256, 256), BF16)],
         cost_estimate=pl.CostEstimate(
             flops=2_000_000_000, bytes_accessed=4_500_000, transcendentals=100_000
         ),
         name="msa_values",
-    )(m, valid, content, sigmoid)
+    )(m, content)
+
+
+def gate_kernel(m_ref, valid_ref, sigmoid_ref, closing_ref, gate_ref, block_ref):
+    inner = dot(diagonal(sigmoid_ref[...], transposed=True), normed_columns(m_ref[...]))
+    gate_ref[...] = jax.nn.sigmoid(inner) * valid_ref[...].astype(F32)
+    block_ref[...] = diagonal(closing_ref[...])
+
+
+def msa_gate(m, valid, sigmoid, closing):
+    whole = lambda i: (0, 0)
+    return pl.pallas_call(
+        gate_kernel,
+        grid=(1,),
+        out_shape=(
+            jax.ShapeDtypeStruct((256, 256), F32),
+            jax.ShapeDtypeStruct((256, 256), BF16),
+        ),
+        in_specs=[
+            pl.BlockSpec((256, 256), whole),
+            pl.BlockSpec((1, 256), whole),
+            pl.BlockSpec((64, 64), whole),
+            pl.BlockSpec((64, 64), whole),
+        ],
+        out_specs=(pl.BlockSpec((256, 256), whole), pl.BlockSpec((256, 256), whole)),
+        cost_estimate=pl.CostEstimate(
+            flops=100_000_000, bytes_accessed=600_000, transcendentals=100_000
+        ),
+        name="msa_gate",
+    )(m, valid, sigmoid, closing)
 
 
 def by_halves(x, reduce):
@@ -269,7 +282,7 @@
     )(a, b)
 
 
-def closing_kernel(p_ref, gate_ref, closing_ref, out_ref, gated):
+def closing_kernel(p_ref, gate_ref, block_ref, out_ref, gated):
     for y in range(4):
         for x in range(4):
             head, half = 2 * y + x // 2, x % 2
@@ -278,16 +291,10 @@
             for i in range(4):
                 rows = slice(i * 64 + head * 8, i * 64 + head * 8 + 8)
                 gated[rows, cols] = total[i * 8 : i * 8 + 8] * gate_ref[rows, cols]
-    spread = one_hot(iota((256, 64), 0) % 64 == iota((256, 64), 1))
-    rep = dot(spread, closing_ref[...]).astype(BF16)
-    tile = one_hot(iota((64, 256), 1) % 64 == iota((64, 256), 0))
-    full = dot(rep, tile)
-    keep = iota((256, 256), 0) // 64 == iota((256, 256), 1) // 64
-    block = jnp.where(keep, full, 0.0).astype(BF16)
-    out_ref[...] = dot(gated[...].astype(BF16), block, TN).astype(BF16)
-
-
-def close(parts, gate, closing):
+    out_ref[...] = dot(gated[...].astype(BF16), block_ref[...], TN).astype(BF16)
+
+
+def close(parts, gate, block):
     return pl.pallas_call(
         closing_kernel,
         out_shape=jax.ShapeDtypeStruct((256, 256), BF16),
@@ -297,7 +304,7 @@
             flops=60_000_000, bytes_accessed=1_000_000, transcendentals=0
         ),
         name="closing",
-    )(parts, gate, closing)
+    )(parts, gate, block)
 
 
 def exchange(x, axes):
@@ -316,12 +323,7 @@
 ):
     logits = pair_logits(pair_window_rows, residue_mask.reshape(1, 64), pair_head_weight.T)
     logits = exchange(logits.reshape(16, 32, 128), GROUP)
-    values, gate = msa_values(
-        sequence_features,
-        sequence_validity.reshape(1, 256),
-        content_projection,
-        sigmoid_projection,
-    )
+    values = msa_values(sequence_features, content_projection)
     values = exchange(values.reshape(16, 512, 128), GROUP)
     swap = ((0, 1), (1, 0))
     mine = local_stats(logits)
@@ -331,6 +333,11 @@
         lax.ppermute(weights, "seq", [(k, (k + d) % 4) for k in range(4)])
         for d in (1, 2, 3)
     ]
+    late, _ = lax.optimization_barrier((sequence_features, weights))
+    gate, block = msa_gate(
+        late, sequence_validity.reshape(1, 256), sigmoid_projection, closing_projection
+    )
+    gathered, gate, block = lax.optimization_barrier((gathered, gate, block))
     q, core = lax.axis_index("seq"), lax.axis_index("core")
     order = [(q - d) % 4 for d in range(4)]
     values = values.reshape(16, 8, 64, 128)
@@ -338,7 +345,7 @@
     theirs = lax.ppermute(theirs, "core", swap)
     ours = partial_average(jnp.stack(order + [core]), gathered, values, F32)
     parts = exchange(add_cores(ours, theirs), CHIPS)
-    return close(parts, gate, closing_projection)
+    return close(parts, gate, block)
 
 
 def solution(mesh):

time: 85.4 us -> 80.9 us (0.947)
  Pallas kernels: 15.1 us -> 13.3 us
  starting transfers between devices: 24.7 us -> 23.2 us
    ppermute x3, waiting for transfers between devices: 7.74 us -> 5.63 us  [shards(): lax.ppermute(weights, 'seq', [(k, (k + d) % 4) for k in range(4)])]
    pallas_call x2 -> x3, Pallas kernels: 11.4 us -> 9.8 us  [the longest x1 4.79 us: msa_values(): pl.pallas_call(values_kernel, grid=(2,), out_shape=jax.ShapeDtypeStruct((...]
    all_to_all x2, starting transfers between devices: 12.3 us -> 10.8 us  [exchange(): return lax.all_to_all(x, axes, split_axis=0, concat_axis=0, tiled=True)]
    all_to_all x2, waiting for transfers between devices: 8.58 us -> 9.92 us  [exchange(): return lax.all_to_all(x, axes, split_axis=0, concat_axis=0, tiled=True)]
  transfers between devices with their start and end apart: 8 -> 8, of which waited for: 8 -> 7; matrix products, arithmetic and copies ran while one was open for 0% -> 0% of each run, Pallas kernels for 10% -> 10%
where the time goes in v4:
time: 80.9 us; the launch traced here: 80.6 us
  blocking collectives  24.9 us (31%)
  starting transfers between devices  23.2 us (29%)
  waiting for transfers between devices  19 us (23%)
  Pallas kernels  13.3 us (16%)
    all_to_all x1, blocking collectives, exchange(): return lax.all_to_all(x, axes, split_axis=0, concat_axis=0, tiled=True)  24.9 us
    all_to_all x2, starting transfers between devices, exchange(): return lax.all_to_all(x, axes, split_axis=0, concat_axis=0, tiled=True)  10.8 us
    all_to_all x2, waiting for transfers between devices, exchange(): return lax.all_to_all(x, axes, split_axis=0, concat_axis=0, tiled=True)  9.92 us
    ppermute x1, starting transfers between devices, shards(): weights, own = softmax_weights(logits, mine, lax.ppermute(mine, 'zh', swap))  6.38 us
    ppermute x3, starting transfers between devices, shards(): lax.ppermute(weights, 'seq', [(k, (k + d) % 4) for k in range(4)])  5.91 us
    ppermute x3, waiting for transfers between devices, shards(): lax.ppermute(weights, 'seq', [(k, (k + d) % 4) for k in range(4)])  5.63 us
    pallas_call x1, Pallas kernels, msa_values(): pl.pallas_call(values_kernel, grid=(2,), out_shape=jax.ShapeDtypeStruct((...  4.79 us
    pallas_call x1, Pallas kernels, pair_logits(): pl.pallas_call(logits_kernel, grid=(1,), out_shape=jax.ShapeDtypeStruct((...  2.91 us
  transfers between devices with their start and end apart: 8, of which 7 were waited for; matrix products, arithmetic and copies ran while one was open for 0% of the time, Pallas kernels for 10%

profile of v4, /device:TPU:32, one launch (start us, length us, event | category | flops | bytes accessed | tf_op | source)
XLA Modules:
  0.0 80.6 jit_solution(8790585576231446651)
XLA Ops:
  0.0 2.9 %pair_logits.1 = f32[8,2,32,128]{3,2,1,0:T(8,128)} custom-call(bf16[64,64,128]{2,1,0:T(8,128)(2,1)} %pair_ref.1, s32[1,64]{1,0:T(1,128)} %bitcast.18, bf16[8,128]{1,0:T(8,128)(2,1)} %bitcast.17), custom_call_target="tpu_custom_call" | custom-call | flops 400000000 | bytes 1400000 | tf_op jit(solution)/shard_map/pair_logits/pallas_call | solution.py:52
  2.9 7.0 %all-to-all-start = ((f32[16,32,128]{2,1,0:T(8,128)}), f32[16,32,128]{2,1,0:T(8,128)S(1)}, u32[]{:S(2)}, u32[]{:S(2)}) async-start(f32[16,32,128]{2,1,0:T(8,128)} %bitcast.15), calls=%async_computation | async-start | bytes 524288 | tf_op jit(solution)/shard_map/all_to_all | solution.py:311
  10.0 4.8 %msa_values.1 = bf16[8,2,8,64,128]{4,3,2,1,0:T(8,128)(2,1)} custom-call(bf16[256,4096]{1,0:T(8,128)(2,1)} %m_ref.2, bf16[64,64]{1,0:T(8,128)(2,1)} %content_ref.1), custom_call_target="tpu_custom_call" | custom-call | flops 2000000000 | bytes 4500000 | tf_op jit(solution)/shard_map/msa_values/pallas_call | solution.py:112
  14.7 3.9 %all-to-all-done.l_ref = f32[16,32,128]{2,1,0:T(8,128)S(1)} async-done(((f32[16,32,128]{2,1,0:T(8,128)}), f32[16,32,128]{2,1,0:T(8,128)S(1)}, u32[]{:S(2)}, u32[]{:S(2)}) %all-to-all-start) | async-done | bytes 262176 | tf_op jit(solution)/shard_map/all_to_all | solution.py:311
  18.6 3.7 %all-to-all-start.1 = ((bf16[16,512,128]{2,1,0:T(8,128)(2,1)}), bf16[16,512,128]{2,1,0:T(8,128)(2,1)S(1)}, u32[]{:S(2)}, u32[]{:S(2)}) async-start(bf16[16,512,128]{2,1,0:T(8,128)(2,1)} %bitcast.14), calls=%async_computation.1 | async-start | bytes 4194304 | tf_op jit(solution)/shard_map/all_to_all | solution.py:311
  22.4 0.2 local_stats.1.a_ref
  22.6 0.1 collective-permute-start
  22.7 1.2 %collective-permute-done.b_ref = f32[2,32,128]{2,1,0:T(8,128)S(1)} collective-permute-done((f32[2,32,128]{2,1,0:T(8,128)S(1)}, f32[2,32,128]{2,1,0:T(8,128)S(1)}, u32[]{:S(2)}, u32[]{:S(2)}) %collective-permute-start) | collective-permute-done | bytes 32800 | tf_op jit(solution)/shard_map/ppermute | solution.py:330
  23.9 6.4 %collective-permute-start.1 = (f32[2,32,128]{2,1,0:T(8,128)S(1)}, f32[2,32,128]{2,1,0:T(8,128)S(1)}, u32[]{:S(2)}, u32[]{:S(2)}) collective-permute-start(f32[2,32,128]{2,1,0:T(8,128)S(1)} %merge_stats.1.a_ref), channel_id=1, source_target_pairs={{0,8},{8,0},{1,9},{9,1},{2,10},{10,2},{3,11},{11,3},{4,12},{12,4},... | collective-permute-start | bytes 98312 | tf_op jit(solution)/shard_map/ppermute | solution.py:331
  30.3 1.9 %collective-permute-done.1.b_ref = f32[2,32,128]{2,1,0:T(8,128)S(1)} collective-permute-done((f32[2,32,128]{2,1,0:T(8,128)S(1)}, f32[2,32,128]{2,1,0:T(8,128)S(1)}, u32[]{:S(2)}, u32[]{:S(2)}) %collective-permute-start.1) | collective-permute-done | bytes 32800 | tf_op jit(solution)/shard_map/ppermute | solution.py:331
  32.2 0.1 softmax_weights.1
  32.3 1.1 %collective-permute-start.4 = (bf16[64,1024]{1,0:T(8,128)(2,1)S(1)}, bf16[64,1024]{1,0:T(8,128)(2,1)S(1)}, u32[]{:S(2)}, u32[]{:S(2)}) collective-permute-start(bf16[64,1024]{1,0:T(8,128)(2,1)S(1)} %get-tuple-element.17), channel_id=1, source_target_pairs={{0,192},{64,0},{128,64},{192,128},{1,193},{65,1},{129,65},{193,129... | collective-permute-start | bytes 393224 | tf_op jit(solution)/shard_map/ppermute | solution.py:333
  33.4 2.5 %collective-permute-start.3 = (bf16[64,1024]{1,0:T(8,128)(2,1)S(1)}, bf16[64,1024]{1,0:T(8,128)(2,1)S(1)}, u32[]{:S(2)}, u32[]{:S(2)}) collective-permute-start(bf16[64,1024]{1,0:T(8,128)(2,1)S(1)} %get-tuple-element.17), channel_id=1, source_target_pairs={{0,128},{64,192},{128,0},{192,64},{1,129},{65,193},{129,1},{193,65... | collective-permute-start | bytes 393224 | tf_op jit(solution)/shard_map/ppermute | solution.py:333
  35.9 2.3 %collective-permute-start.2 = (bf16[64,1024]{1,0:T(8,128)(2,1)S(1)}, bf16[64,1024]{1,0:T(8,128)(2,1)S(1)}, u32[]{:S(2)}, u32[]{:S(2)}) collective-permute-start(bf16[64,1024]{1,0:T(8,128)(2,1)S(1)} %get-tuple-element.17), channel_id=1, source_target_pairs={{0,64},{64,128},{128,192},{192,0},{1,65},{65,129},{129,193},{193,1... | collective-permute-start | bytes 393224 | tf_op jit(solution)/shard_map/ppermute | solution.py:333
  38.2 0.1 stack.35.place_ref
  38.3 2.1 %msa_gate.1 = (f32[256,256]{1,0:T(8,128)}, bf16[256,256]{1,0:T(8,128)(2,1)}) custom-call(bf16[256,4096]{1,0:T(8,128)(2,1)} %m_ref.2, s32[1,256]{1,0:T(1,128)} %bitcast.16, bf16[64,64]{1,0:T(8,128)(2,1)} %sigmoid_ref.1, bf16[64,64]{1,0:T(8,128)(2,1)} %closing_ref.1), custom_call_target="tpu_custom_call" | custom-call | flops 100000000 | bytes 600000 | tf_op jit(solution)/shard_map/msa_gate/pallas_call | solution.py:137
  40.4 0.0 collective-permute-done.4.w3
  40.4 3.8 %collective-permute-done.3.w2 = bf16[64,1024]{1,0:T(8,128)(2,1)S(1)} collective-permute-done((bf16[64,1024]{1,0:T(8,128)(2,1)S(1)}, bf16[64,1024]{1,0:T(8,128)(2,1)S(1)}, u32[]{:S(2)}, u32[]{:S(2)}) %collective-permute-start.3) | collective-permute-done | bytes 131104 | tf_op jit(solution)/shard_map/ppermute | solution.py:333
  44.2 1.8 %collective-permute-done.2.w1 = bf16[64,1024]{1,0:T(8,128)(2,1)S(1)} collective-permute-done((bf16[64,1024]{1,0:T(8,128)(2,1)S(1)}, bf16[64,1024]{1,0:T(8,128)(2,1)S(1)}, u32[]{:S(2)}, u32[]{:S(2)}) %collective-permute-start.2) | collective-permute-done | bytes 131104 | tf_op jit(solution)/shard_map/ppermute | solution.py:333
  46.1 6.0 %all-to-all-done.1 = bf16[16,512,128]{2,1,0:T(8,128)(2,1)S(1)} async-done(((bf16[16,512,128]{2,1,0:T(8,128)(2,1)}), bf16[16,512,128]{2,1,0:T(8,128)(2,1)S(1)}, u32[]{:S(2)}, u32[]{:S(2)}) %all-to-all-start.1) | async-done | bytes 2097184 | tf_op jit(solution)/shard_map/all_to_all | solution.py:311
  52.1 1.1 %partial_average.3 = bf16[32,32,128]{2,1,0:T(8,128)(2,1)S(1)} custom-call(s32[5]{0:T(128)S(1)} %stack.35.place_ref, bf16[64,1024]{1,0:T(8,128)(2,1)S(1)} %get-tuple-element.21.w0, bf16[64,1024]{1,0:T(8,128)(2,1)S(1)} %collective-permute-done.2.w1, bf16[64,1024]{1,0:T(8,128)(2,1)S(1)} %collective-permute-done.3.w2, ...), custom_call_target="tpu_custom_call" | custom-call | flops 300000000 | bytes 2800000 | tf_op jit(solution)/shard_map/partial_average/pallas_call | solution.py:255
  53.1 0.1 collective-permute-start.5
  53.2 0.1 stack.33.place_ref
  53.3 0.0 copy-start
  53.3 0.0 copy-start.1
  53.3 1.1 %partial_average.2.a_ref = f32[32,32,128]{2,1,0:T(8,128)S(1)} custom-call(s32[5]{0:T(128)S(1)} %stack.33.place_ref, bf16[64,1024]{1,0:T(8,128)(2,1)S(1)} %get-tuple-element.21.w0, bf16[64,1024]{1,0:T(8,128)(2,1)S(1)} %collective-permute-done.2.w1, bf16[64,1024]{1,0:T(8,128)(2,1)S(1)} %collective-permute-done.3.w2, ...), custom_call_target="tpu_custom_call" | custom-call | flops 300000000 | bytes 2800000 | tf_op jit(solution)/shard_map/partial_average/pallas_call | solution.py:255
  54.4 0.4 collective-permute-done.5.b_ref
  54.8 0.1 add_cores.1
  54.8 24.9 %all_to_all.15.p_ref = bf16[32,32,128]{2,1,0:T(8,128)(2,1)S(1)} all-to-all(bf16[32,32,128]{2,1,0:T(8,128)(2,1)S(1)} %add_cores.1), channel_id=1, replica_groups=mesh['seq'=4,'y'=4,'zh'=2,'x'=4,'core'=2] {'y','zh','x'}, dimensions={0} | all-to-all | bytes 524288 | tf_op jit(solution)/shard_map/all_to_all | solution.py:311
  79.7 0.0 copy-done
  79.7 0.0 copy-done.1
  79.7 0.9 %closing.1 = bf16[256,256]{1,0:T(8,128)(2,1)} custom-call(bf16[32,32,128]{2,1,0:T(8,128)(2,1)S(1)} %all_to_all.15.p_ref, f32[256,256]{1,0:T(8,128)S(1)} %copy-done, bf16[256,256]{1,0:T(8,128)(2,1)S(1)} %copy-done.1), custom_call_target="tpu_custom_call" | custom-call | flops 60000000 | bytes 1000000 | tf_op jit(solution)/shard_map/closing/pallas_call | solution.py:298
  (1 shorter events, 0.0 us)
Async XLA Ops:
  2.9 15.7 %all-to-all-start = ((f32[16,32,128]{2,1,0:T(8,128)}), f32[16,32,128]{2,1,0:T(8,128)S(1)}, u32[]{:S(2)}, u32[]{:S(2)}) async-start(f32[16,32,128]{2,1,0:T(8,128)} %bitcast.15), calls=%async_computation | async-start | bytes 524288 | tf_op jit(solution)/shard_map/all_to_all | solution.py:311
  18.6 33.4 %all-to-all-start.1 = ((bf16[16,512,128]{2,1,0:T(8,128)(2,1)}), bf16[16,512,128]{2,1,0:T(8,128)(2,1)S(1)}, u32[]{:S(2)}, u32[]{:S(2)}) async-start(bf16[16,512,128]{2,1,0:T(8,128)(2,1)} %bitcast.14), calls=%async_computation.1 | async-start | bytes 4194304 | tf_op jit(solution)/shard_map/all_to_all | solution.py:311
  22.6 1.3 %collective-permute-start = (f32[2,32,128]{2,1,0:T(8,128)S(1)}, f32[2,32,128]{2,1,0:T(8,128)S(1)}, u32[]{:S(2)}, u32[]{:S(2)}) collective-permute-start(f32[2,32,128]{2,1,0:T(8,128)S(1)} %local_stats.1.a_ref), channel_id=1, source_target_pairs={{0,1},{1,0},{2,3},{3,2},{4,5},{5,4},{6,7},{7,6},{8,9},{9,8},{10,11... | collective-permute-start | bytes 98312 | tf_op jit(solution)/shard_map/ppermute | solution.py:330
  23.9 8.3 %collective-permute-start.1 = (f32[2,32,128]{2,1,0:T(8,128)S(1)}, f32[2,32,128]{2,1,0:T(8,128)S(1)}, u32[]{:S(2)}, u32[]{:S(2)}) collective-permute-start(f32[2,32,128]{2,1,0:T(8,128)S(1)} %merge_stats.1.a_ref), channel_id=1, source_target_pairs={{0,8},{8,0},{1,9},{9,1},{2,10},{10,2},{3,11},{11,3},{4,12},{12,4},... | collective-permute-start | bytes 98312 | tf_op jit(solution)/shard_map/ppermute | solution.py:331
  32.3 8.1 %collective-permute-start.4 = (bf16[64,1024]{1,0:T(8,128)(2,1)S(1)}, bf16[64,1024]{1,0:T(8,128)(2,1)S(1)}, u32[]{:S(2)}, u32[]{:S(2)}) collective-permute-start(bf16[64,1024]{1,0:T(8,128)(2,1)S(1)} %get-tuple-element.17), channel_id=1, source_target_pairs={{0,192},{64,0},{128,64},{192,128},{1,193},{65,1},{129,65},{193,129... | collective-permute-start | bytes 393224 | tf_op jit(solution)/shard_map/ppermute | solution.py:333
  33.4 10.8 %collective-permute-start.3 = (bf16[64,1024]{1,0:T(8,128)(2,1)S(1)}, bf16[64,1024]{1,0:T(8,128)(2,1)S(1)}, u32[]{:S(2)}, u32[]{:S(2)}) collective-permute-start(bf16[64,1024]{1,0:T(8,128)(2,1)S(1)} %get-tuple-element.17), channel_id=1, source_target_pairs={{0,128},{64,192},{128,0},{192,64},{1,129},{65,193},{129,1},{193,65... | collective-permute-start | bytes 393224 | tf_op jit(solution)/shard_map/ppermute | solution.py:333
  35.9 10.1 %collective-permute-start.2 = (bf16[64,1024]{1,0:T(8,128)(2,1)S(1)}, bf16[64,1024]{1,0:T(8,128)(2,1)S(1)}, u32[]{:S(2)}, u32[]{:S(2)}) collective-permute-start(bf16[64,1024]{1,0:T(8,128)(2,1)S(1)} %get-tuple-element.17), channel_id=1, source_target_pairs={{0,64},{64,128},{128,192},{192,0},{1,65},{65,129},{129,193},{193,1... | collective-permute-start | bytes 393224 | tf_op jit(solution)/shard_map/ppermute | solution.py:333
  53.1 1.6 %collective-permute-start.5 = (bf16[32,32,128]{2,1,0:T(8,128)(2,1)S(1)}, bf16[32,32,128]{2,1,0:T(8,128)(2,1)S(1)}, u32[]{:S(2)}, u32[]{:S(2)}) collective-permute-start(bf16[32,32,128]{2,1,0:T(8,128)(2,1)S(1)} %partial_average.3), channel_id=1, source_target_pairs={{0,1},{1,0},{2,3},{3,2},{4,5},{5,4},{6,7},{7,6},{8,9},{9,8},{10,11... | collective-permute-start | bytes 786440 | tf_op jit(solution)/shard_map/ppermute | solution.py:345
  53.3 26.4 %copy-start = (f32[256,256]{1,0:T(8,128)S(1)}, f32[256,256]{1,0:T(8,128)}, u32[]{:S(2)}) copy-start(f32[256,256]{1,0:T(8,128)} %get-tuple-element.25.gate_ref) | copy-start | bytes 786436
  53.3 26.4 %copy-start.1 = (bf16[256,256]{1,0:T(8,128)(2,1)S(1)}, bf16[256,256]{1,0:T(8,128)(2,1)}, u32[]{:S(2)}) copy-start(bf16[256,256]{1,0:T(8,128)(2,1)} %get-tuple-element.26.block_ref) | copy-start | bytes 393220

commit v5 on v4

--- a/solution.py
+++ b/solution.py
@@ -14,9 +14,9 @@
 NT = (((1,), (1,)), ((), ()))
 NN = (((1,), (0,)), ((), ()))
 TN = (((0,), (0,)), ((), ()))
-GROUP = ("y", "x")
-CHIPS = ("y", "zh", "x")
-RES = CHIPS + ("core",)
+GROUP = ("x", "y")
+CHIPS = ("zh", "y", "x")
+RES = ("y", "zh", "x", "core")
 SMALL_LIMIT = 24 * 1024 * 1024
 
 
@@ -247,7 +247,11 @@
                     scr[pl.ds(q * 256 + par * 8 + 2 * c2 + e, 16, stride=16), :] = part[
                         row : row + 16, e * 128 : (e + 1) * 128
                     ]
-    out_ref[...] = scr[...].astype(out_ref.dtype).reshape(32, 32, 128)
+    for y in range(4):
+        for zh in range(2):
+            for x in range(4):
+                start = (y * 8 + zh * 4 + x) * 32
+                out_ref[y * 4 + zh * 16 + x * 1] = scr[start : start + 32].astype(out_ref.dtype)
 
 
 def partial_average(place, weights, values, dtype):
@@ -285,8 +289,10 @@
 def closing_kernel(p_ref, gate_ref, block_ref, out_ref, gated):
     for y in range(4):
         for x in range(4):
-            head, half = 2 * y + x // 2, x % 2
-            total = p_ref[y * 8 + x].astype(F32) + p_ref[y * 8 + 4 + x].astype(F32)
+            head, half = 2 * x + y // 2, y % 2
+            total = sum(
+                p_ref[y * 4 + zh * 16 + x * 1].astype(F32) for zh in range(2)
+            )
             cols = slice(half * 128, half * 128 + 128)
             for i in range(4):
                 rows = slice(i * 64 + head * 8, i * 64 + head * 8 + 8)

time: 80.9 us -> 80.9 us (level)
  blocking collectives: 24.9 us -> 25.8 us
  waiting for transfers between devices: 19 us -> 18.1 us
    all_to_all x1, blocking collectives: 24.9 us -> 25.8 us  [exchange(): return lax.all_to_all(x, axes, split_axis=0, concat_axis=0, tiled=True)]
  transfers between devices with their start and end apart: 8 -> 8, of which waited for: 7 -> 8; matrix products, arithmetic and copies ran while one was open for 0% -> 0% of each run, Pallas kernels for 10% -> 10%
where the time goes in v5:
time: 80.9 us; the launch traced here: 80.6 us
  blocking collectives  25.8 us (32%)
  starting transfers between devices  23.2 us (29%)
  waiting for transfers between devices  18.1 us (22%)
  Pallas kernels  13.3 us (16%)
    all_to_all x1, blocking collectives, exchange(): return lax.all_to_all(x, axes, split_axis=0, concat_axis=0, tiled=True)  25.8 us
    all_to_all x2, starting transfers between devices, exchange(): return lax.all_to_all(x, axes, split_axis=0, concat_axis=0, tiled=True)  10.8 us
    all_to_all x2, waiting for transfers between devices, exchange(): return lax.all_to_all(x, axes, split_axis=0, concat_axis=0, tiled=True)  9.25 us
    ppermute x1, starting transfers between devices, shards(): weights, own = softmax_weights(logits, mine, lax.ppermute(mine, 'zh', swap))  6.38 us
    ppermute x3, starting transfers between devices, shards(): lax.ppermute(weights, 'seq', [(k, (k + d) % 4) for k in range(4)])  5.91 us
    ppermute x3, waiting for transfers between devices, shards(): lax.ppermute(weights, 'seq', [(k, (k + d) % 4) for k in range(4)])  5.38 us
    pallas_call x1, Pallas kernels, msa_values(): pl.pallas_call(values_kernel, grid=(2,), out_shape=jax.ShapeDtypeStruct((...  4.79 us
    pallas_call x1, Pallas kernels, pair_logits(): pl.pallas_call(logits_kernel, grid=(1,), out_shape=jax.ShapeDtypeStruct((...  2.91 us
  transfers between devices with their start and end apart: 8, of which 8 were waited for; matrix products, arithmetic and copies ran while one was open for 0% of the time, Pallas kernels for 10%

profile of v5, /device:TPU:32, one launch (start us, length us, event | category | flops | bytes accessed | tf_op | source)
XLA Modules:
  0.0 80.6 jit_solution(6348009308666753933)
XLA Ops:
  0.0 2.9 %pair_logits.1 = f32[8,2,32,128]{3,2,1,0:T(8,128)} custom-call(bf16[64,64,128]{2,1,0:T(8,128)(2,1)} %pair_ref.1, s32[1,64]{1,0:T(1,128)} %bitcast.18, bf16[8,128]{1,0:T(8,128)(2,1)} %bitcast.17), custom_call_target="tpu_custom_call" | custom-call | flops 400000000 | bytes 1400000 | tf_op jit(solution)/shard_map/pair_logits/pallas_call | solution.py:52
  2.9 7.0 %all-to-all-start = ((f32[16,32,128]{2,1,0:T(8,128)}), f32[16,32,128]{2,1,0:T(8,128)S(1)}, u32[]{:S(2)}, u32[]{:S(2)}) async-start(f32[16,32,128]{2,1,0:T(8,128)} %bitcast.15), calls=%async_computation | async-start | bytes 524288 | tf_op jit(solution)/shard_map/all_to_all | solution.py:317
  10.0 4.8 %msa_values.1 = bf16[8,2,8,64,128]{4,3,2,1,0:T(8,128)(2,1)} custom-call(bf16[256,4096]{1,0:T(8,128)(2,1)} %m_ref.2, bf16[64,64]{1,0:T(8,128)(2,1)} %content_ref.1), custom_call_target="tpu_custom_call" | custom-call | flops 2000000000 | bytes 4500000 | tf_op jit(solution)/shard_map/msa_values/pallas_call | solution.py:112
  14.7 3.7 %all-to-all-done.l_ref = f32[16,32,128]{2,1,0:T(8,128)S(1)} async-done(((f32[16,32,128]{2,1,0:T(8,128)}), f32[16,32,128]{2,1,0:T(8,128)S(1)}, u32[]{:S(2)}, u32[]{:S(2)}) %all-to-all-start) | async-done | bytes 262176 | tf_op jit(solution)/shard_map/all_to_all | solution.py:317
  18.5 3.7 %all-to-all-start.1 = ((bf16[16,512,128]{2,1,0:T(8,128)(2,1)}), bf16[16,512,128]{2,1,0:T(8,128)(2,1)S(1)}, u32[]{:S(2)}, u32[]{:S(2)}) async-start(bf16[16,512,128]{2,1,0:T(8,128)(2,1)} %bitcast.14), calls=%async_computation.1 | async-start | bytes 4194304 | tf_op jit(solution)/shard_map/all_to_all | solution.py:317
  22.2 0.2 local_stats.1.a_ref
  22.4 0.1 collective-permute-start
  22.5 1.2 %collective-permute-done.b_ref = f32[2,32,128]{2,1,0:T(8,128)S(1)} collective-permute-done((f32[2,32,128]{2,1,0:T(8,128)S(1)}, f32[2,32,128]{2,1,0:T(8,128)S(1)}, u32[]{:S(2)}, u32[]{:S(2)}) %collective-permute-start) | collective-permute-done | bytes 32800 | tf_op jit(solution)/shard_map/ppermute | solution.py:336
  23.7 6.4 %collective-permute-start.1 = (f32[2,32,128]{2,1,0:T(8,128)S(1)}, f32[2,32,128]{2,1,0:T(8,128)S(1)}, u32[]{:S(2)}, u32[]{:S(2)}) collective-permute-start(f32[2,32,128]{2,1,0:T(8,128)S(1)} %merge_stats.1.a_ref), channel_id=1, source_target_pairs={{0,8},{8,0},{1,9},{9,1},{2,10},{10,2},{3,11},{11,3},{4,12},{12,4},... | collective-permute-start | bytes 98312 | tf_op jit(solution)/shard_map/ppermute | solution.py:337
  30.1 1.9 %collective-permute-done.1.b_ref = f32[2,32,128]{2,1,0:T(8,128)S(1)} collective-permute-done((f32[2,32,128]{2,1,0:T(8,128)S(1)}, f32[2,32,128]{2,1,0:T(8,128)S(1)}, u32[]{:S(2)}, u32[]{:S(2)}) %collective-permute-start.1) | collective-permute-done | bytes 32800 | tf_op jit(solution)/shard_map/ppermute | solution.py:337
  32.0 0.1 softmax_weights.1
  32.1 1.1 %collective-permute-start.4 = (bf16[64,1024]{1,0:T(8,128)(2,1)S(1)}, bf16[64,1024]{1,0:T(8,128)(2,1)S(1)}, u32[]{:S(2)}, u32[]{:S(2)}) collective-permute-start(bf16[64,1024]{1,0:T(8,128)(2,1)S(1)} %get-tuple-element.17), channel_id=1, source_target_pairs={{0,192},{64,0},{128,64},{192,128},{1,193},{65,1},{129,65},{193,129... | collective-permute-start | bytes 393224 | tf_op jit(solution)/shard_map/ppermute | solution.py:339
  33.2 2.5 %collective-permute-start.3 = (bf16[64,1024]{1,0:T(8,128)(2,1)S(1)}, bf16[64,1024]{1,0:T(8,128)(2,1)S(1)}, u32[]{:S(2)}, u32[]{:S(2)}) collective-permute-start(bf16[64,1024]{1,0:T(8,128)(2,1)S(1)} %get-tuple-element.17), channel_id=1, source_target_pairs={{0,128},{64,192},{128,0},{192,64},{1,129},{65,193},{129,1},{193,65... | collective-permute-start | bytes 393224 | tf_op jit(solution)/shard_map/ppermute | solution.py:339
  35.8 2.3 %collective-permute-start.2 = (bf16[64,1024]{1,0:T(8,128)(2,1)S(1)}, bf16[64,1024]{1,0:T(8,128)(2,1)S(1)}, u32[]{:S(2)}, u32[]{:S(2)}) collective-permute-start(bf16[64,1024]{1,0:T(8,128)(2,1)S(1)} %get-tuple-element.17), channel_id=1, source_target_pairs={{0,64},{64,128},{128,192},{192,0},{1,65},{65,129},{129,193},{193,1... | collective-permute-start | bytes 393224 | tf_op jit(solution)/shard_map/ppermute | solution.py:339
  38.1 0.1 stack.35.place_ref
  38.1 2.1 %msa_gate.1 = (f32[256,256]{1,0:T(8,128)}, bf16[256,256]{1,0:T(8,128)(2,1)}) custom-call(bf16[256,4096]{1,0:T(8,128)(2,1)} %m_ref.2, s32[1,256]{1,0:T(1,128)} %bitcast.16, bf16[64,64]{1,0:T(8,128)(2,1)} %sigmoid_ref.1, bf16[64,64]{1,0:T(8,128)(2,1)} %closing_ref.1), custom_call_target="tpu_custom_call" | custom-call | flops 100000000 | bytes 600000 | tf_op jit(solution)/shard_map/msa_gate/pallas_call | solution.py:137
  40.2 3.3 %collective-permute-done.4.w3 = bf16[64,1024]{1,0:T(8,128)(2,1)S(1)} collective-permute-done((bf16[64,1024]{1,0:T(8,128)(2,1)S(1)}, bf16[64,1024]{1,0:T(8,128)(2,1)S(1)}, u32[]{:S(2)}, u32[]{:S(2)}) %collective-permute-start.4) | collective-permute-done | bytes 131104 | tf_op jit(solution)/shard_map/ppermute | solution.py:339
  43.6 0.2 collective-permute-done.3.w2
  43.8 1.8 %collective-permute-done.2.w1 = bf16[64,1024]{1,0:T(8,128)(2,1)S(1)} collective-permute-done((bf16[64,1024]{1,0:T(8,128)(2,1)S(1)}, bf16[64,1024]{1,0:T(8,128)(2,1)S(1)}, u32[]{:S(2)}, u32[]{:S(2)}) %collective-permute-start.2) | collective-permute-done | bytes 131104 | tf_op jit(solution)/shard_map/ppermute | solution.py:339
  45.6 5.5 %all-to-all-done.1 = bf16[16,512,128]{2,1,0:T(8,128)(2,1)S(1)} async-done(((bf16[16,512,128]{2,1,0:T(8,128)(2,1)}), bf16[16,512,128]{2,1,0:T(8,128)(2,1)S(1)}, u32[]{:S(2)}, u32[]{:S(2)}) %all-to-all-start.1) | async-done | bytes 2097184 | tf_op jit(solution)/shard_map/all_to_all | solution.py:317
  51.2 1.1 %partial_average.3 = bf16[32,32,128]{2,1,0:T(8,128)(2,1)S(1)} custom-call(s32[5]{0:T(128)S(1)} %stack.35.place_ref, bf16[64,1024]{1,0:T(8,128)(2,1)S(1)} %get-tuple-element.21.w0, bf16[64,1024]{1,0:T(8,128)(2,1)S(1)} %collective-permute-done.2.w1, bf16[64,1024]{1,0:T(8,128)(2,1)S(1)} %collective-permute-done.3.w2, ...), custom_call_target="tpu_custom_call" | custom-call | flops 300000000 | bytes 2800000 | tf_op jit(solution)/shard_map/partial_average/pallas_call | solution.py:259
  52.2 0.1 collective-permute-start.5
  52.3 0.1 stack.33.place_ref
  52.4 0.0 copy-start
  52.4 0.0 copy-start.1
  52.4 1.1 %partial_average.2.a_ref = f32[32,32,128]{2,1,0:T(8,128)S(1)} custom-call(s32[5]{0:T(128)S(1)} %stack.33.place_ref, bf16[64,1024]{1,0:T(8,128)(2,1)S(1)} %get-tuple-element.21.w0, bf16[64,1024]{1,0:T(8,128)(2,1)S(1)} %collective-permute-done.2.w1, bf16[64,1024]{1,0:T(8,128)(2,1)S(1)} %collective-permute-done.3.w2, ...), custom_call_target="tpu_custom_call" | custom-call | flops 300000000 | bytes 2800000 | tf_op jit(solution)/shard_map/partial_average/pallas_call | solution.py:259
  53.5 0.4 collective-permute-done.5.b_ref
  53.8 0.1 add_cores.1
  53.9 25.8 %all_to_all.15.p_ref = bf16[32,32,128]{2,1,0:T(8,128)(2,1)S(1)} all-to-all(bf16[32,32,128]{2,1,0:T(8,128)(2,1)S(1)} %add_cores.1), channel_id=1, replica_groups=mesh['seq'=4,'y'=4,'zh'=2,'x'=4,'core'=2] {'zh','y','x'}, dimensions={0} | all-to-all | bytes 524288 | tf_op jit(solution)/shard_map/all_to_all | solution.py:317
  79.7 0.0 copy-done
  79.7 0.0 copy-done.1
  79.7 0.9 %closing.1 = bf16[256,256]{1,0:T(8,128)(2,1)} custom-call(bf16[32,32,128]{2,1,0:T(8,128)(2,1)S(1)} %all_to_all.15.p_ref, f32[256,256]{1,0:T(8,128)S(1)} %copy-done, bf16[256,256]{1,0:T(8,128)(2,1)S(1)} %copy-done.1), custom_call_target="tpu_custom_call" | custom-call | flops 60000000 | bytes 1000000 | tf_op jit(solution)/shard_map/closing/pallas_call | solution.py:304
  (1 shorter events, 0.0 us)
Async XLA Ops:
  2.9 15.6 %all-to-all-start = ((f32[16,32,128]{2,1,0:T(8,128)}), f32[16,32,128]{2,1,0:T(8,128)S(1)}, u32[]{:S(2)}, u32[]{:S(2)}) async-start(f32[16,32,128]{2,1,0:T(8,128)} %bitcast.15), calls=%async_computation | async-start | bytes 524288 | tf_op jit(solution)/shard_map/all_to_all | solution.py:317
  18.5 32.7 %all-to-all-start.1 = ((bf16[16,512,128]{2,1,0:T(8,128)(2,1)}), bf16[16,512,128]{2,1,0:T(8,128)(2,1)S(1)}, u32[]{:S(2)}, u32[]{:S(2)}) async-start(bf16[16,512,128]{2,1,0:T(8,128)(2,1)} %bitcast.14), calls=%async_computation.1 | async-start | bytes 4194304 | tf_op jit(solution)/shard_map/all_to_all | solution.py:317
  22.4 1.3 %collective-permute-start = (f32[2,32,128]{2,1,0:T(8,128)S(1)}, f32[2,32,128]{2,1,0:T(8,128)S(1)}, u32[]{:S(2)}, u32[]{:S(2)}) collective-permute-start(f32[2,32,128]{2,1,0:T(8,128)S(1)} %local_stats.1.a_ref), channel_id=1, source_target_pairs={{0,1},{1,0},{2,3},{3,2},{4,5},{5,4},{6,7},{7,6},{8,9},{9,8},{10,11... | collective-permute-start | bytes 98312 | tf_op jit(solution)/shard_map/ppermute | solution.py:336
  23.7 8.3 %collective-permute-start.1 = (f32[2,32,128]{2,1,0:T(8,128)S(1)}, f32[2,32,128]{2,1,0:T(8,128)S(1)}, u32[]{:S(2)}, u32[]{:S(2)}) collective-permute-start(f32[2,32,128]{2,1,0:T(8,128)S(1)} %merge_stats.1.a_ref), channel_id=1, source_target_pairs={{0,8},{8,0},{1,9},{9,1},{2,10},{10,2},{3,11},{11,3},{4,12},{12,4},... | collective-permute-start | bytes 98312 | tf_op jit(solution)/shard_map/ppermute | solution.py:337
  32.1 11.4 %collective-permute-start.4 = (bf16[64,1024]{1,0:T(8,128)(2,1)S(1)}, bf16[64,1024]{1,0:T(8,128)(2,1)S(1)}, u32[]{:S(2)}, u32[]{:S(2)}) collective-permute-start(bf16[64,1024]{1,0:T(8,128)(2,1)S(1)} %get-tuple-element.17), channel_id=1, source_target_pairs={{0,192},{64,0},{128,64},{192,128},{1,193},{65,1},{129,65},{193,129... | collective-permute-start | bytes 393224 | tf_op jit(solution)/shard_map/ppermute | solution.py:339
  33.2 10.5 %collective-permute-start.3 = (bf16[64,1024]{1,0:T(8,128)(2,1)S(1)}, bf16[64,1024]{1,0:T(8,128)(2,1)S(1)}, u32[]{:S(2)}, u32[]{:S(2)}) collective-permute-start(bf16[64,1024]{1,0:T(8,128)(2,1)S(1)} %get-tuple-element.17), channel_id=1, source_target_pairs={{0,128},{64,192},{128,0},{192,64},{1,129},{65,193},{129,1},{193,65... | collective-permute-start | bytes 393224 | tf_op jit(solution)/shard_map/ppermute | solution.py:339
  35.8 9.9 %collective-permute-start.2 = (bf16[64,1024]{1,0:T(8,128)(2,1)S(1)}, bf16[64,1024]{1,0:T(8,128)(2,1)S(1)}, u32[]{:S(2)}, u32[]{:S(2)}) collective-permute-start(bf16[64,1024]{1,0:T(8,128)(2,1)S(1)} %get-tuple-element.17), channel_id=1, source_target_pairs={{0,64},{64,128},{128,192},{192,0},{1,65},{65,129},{129,193},{193,1... | collective-permute-start | bytes 393224 | tf_op jit(solution)/shard_map/ppermute | solution.py:339
  52.2 1.6 %collective-permute-start.5 = (bf16[32,32,128]{2,1,0:T(8,128)(2,1)S(1)}, bf16[32,32,128]{2,1,0:T(8,128)(2,1)S(1)}, u32[]{:S(2)}, u32[]{:S(2)}) collective-permute-start(bf16[32,32,128]{2,1,0:T(8,128)(2,1)S(1)} %partial_average.3), channel_id=1, source_target_pairs={{0,1},{1,0},{2,3},{3,2},{4,5},{5,4},{6,7},{7,6},{8,9},{9,8},{10,11... | collective-permute-start | bytes 786440 | tf_op jit(solution)/shard_map/ppermute | solution.py:351
  52.4 27.3 %copy-start = (f32[256,256]{1,0:T(8,128)S(1)}, f32[256,256]{1,0:T(8,128)}, u32[]{:S(2)}) copy-start(f32[256,256]{1,0:T(8,128)} %get-tuple-element.25.gate_ref) | copy-start | bytes 786436
  52.4 27.3 %copy-start.1 = (bf16[256,256]{1,0:T(8,128)(2,1)S(1)}, bf16[256,256]{1,0:T(8,128)(2,1)}, u32[]{:S(2)}) copy-start(bf16[256,256]{1,0:T(8,128)(2,1)} %get-tuple-element.26.block_ref) | copy-start | bytes 393220

commit v6 on v5

--- a/solution.py
+++ b/solution.py
@@ -15,7 +15,6 @@
 NN = (((1,), (0,)), ((), ()))
 TN = (((0,), (0,)), ((), ()))
 GROUP = ("x", "y")
-CHIPS = ("zh", "y", "x")
 RES = ("y", "zh", "x", "core")
 SMALL_LIMIT = 24 * 1024 * 1024
 
@@ -251,7 +250,7 @@
         for zh in range(2):
             for x in range(4):
                 start = (y * 8 + zh * 4 + x) * 32
-                out_ref[y * 4 + zh * 16 + x * 1] = scr[start : start + 32].astype(out_ref.dtype)
+                out_ref[zh * 16 + x * 4 + y] = scr[start : start + 32].astype(out_ref.dtype)
 
 
 def partial_average(place, weights, values, dtype):
@@ -270,19 +269,42 @@
     )(place, *weights, values)
 
 
-def add_kernel(a_ref, b_ref, out_ref):
+def add_kernel(a_ref, b_ref, own_ref, cross_ref):
+    zh = lax.axis_index("zh")
+    own = pl.ds(pl.multiple_of(zh * 16, 16), 16)
+    cross = pl.ds(pl.multiple_of(16 - zh * 16, 16), 16)
+    own_ref[...] = a_ref[own] + b_ref[own].astype(F32)
+    cross_ref[...] = (a_ref[cross] + b_ref[cross].astype(F32)).astype(BF16)
+
+
+def add_cores(a, b):
+    return pl.pallas_call(
+        add_kernel,
+        out_shape=(
+            jax.ShapeDtypeStruct((16, 32, 128), F32),
+            jax.ShapeDtypeStruct((16, 32, 128), BF16),
+        ),
+        compiler_params=pltpu.CompilerParams(vmem_limit_bytes=SMALL_LIMIT),
+        cost_estimate=pl.CostEstimate(
+            flops=200_000, bytes_accessed=1_000_000, transcendentals=0
+        ),
+        name="add_cores",
+    )(a, b)
+
+
+def join_kernel(a_ref, b_ref, out_ref):
     out_ref[...] = (a_ref[...] + b_ref[...].astype(F32)).astype(BF16)
 
 
-def add_cores(a, b):
-    return pl.pallas_call(
-        add_kernel,
-        out_shape=jax.ShapeDtypeStruct((32, 32, 128), BF16),
-        compiler_params=pltpu.CompilerParams(vmem_limit_bytes=SMALL_LIMIT),
-        cost_estimate=pl.CostEstimate(
-            flops=200_000, bytes_accessed=1_000_000, transcendentals=0
-        ),
-        name="add_cores",
+def add_halves(a, b):
+    return pl.pallas_call(
+        join_kernel,
+        out_shape=jax.ShapeDtypeStruct((16, 32, 128), BF16),
+        compiler_params=pltpu.CompilerParams(vmem_limit_bytes=SMALL_LIMIT),
+        cost_estimate=pl.CostEstimate(
+            flops=100_000, bytes_accessed=500_000, transcendentals=0
+        ),
+        name="add_halves",
     )(a, b)
 
 
@@ -290,9 +312,7 @@
     for y in range(4):
         for x in range(4):
             head, half = 2 * x + y // 2, y % 2
-            total = sum(
-                p_ref[y * 4 + zh * 16 + x * 1].astype(F32) for zh in range(2)
-            )
+            total = p_ref[x * 4 + y].astype(F32)
             cols = slice(half * 128, half * 128 + 128)
             for i in range(4):
                 rows = slice(i * 64 + head * 8, i * 64 + head * 8 + 8)
@@ -350,7 +370,8 @@
     theirs = partial_average(jnp.stack(order + [1 - core]), gathered, values, BF16)
     theirs = lax.ppermute(theirs, "core", swap)
     ours = partial_average(jnp.stack(order + [core]), gathered, values, F32)
-    parts = exchange(add_cores(ours, theirs), CHIPS)
+    mine, cross = add_cores(ours, theirs)
+    parts = exchange(add_halves(mine, lax.ppermute(cross, "zh", swap)), GROUP)
     return close(parts, gate, block)
 
 

time: 80.9 us -> 79.7 us (0.985)
  blocking collectives: 25.8 us -> 11.5 us
  waiting for transfers between devices: 18.1 us -> 24.8 us
  starting transfers between devices: 23.2 us -> 29.6 us
    all_to_all x1, blocking collectives: 25.8 us -> 11.5 us  [exchange(): return lax.all_to_all(x, axes, split_axis=0, concat_axis=0, tiled=True)]
    ppermute x0 -> x1, waiting for transfers between devices: none -> 6.67 us  [shards(): parts = exchange(add_halves(mine, lax.ppermute(cross, 'zh', swap)), GROUP)]
    ppermute x0 -> x1, starting transfers between devices: none -> 6.37 us  [shards(): parts = exchange(add_halves(mine, lax.ppermute(cross, 'zh', swap)), GROUP)]
  transfers between devices with their start and end apart: 8 -> 9, of which waited for: 8 -> 9; matrix products, arithmetic and copies ran while one was open for 0% -> 0% of each run, Pallas kernels for 10% -> 11%
where the time goes in v6:
time: 79.7 us; the launch traced here: 79.4 us
  starting transfers between devices  29.6 us (37%)
  waiting for transfers between devices  24.8 us (31%)
  Pallas kernels  13.3 us (17%)
  blocking collectives  11.5 us (14%)
    all_to_all x1, blocking collectives, exchange(): return lax.all_to_all(x, axes, split_axis=0, concat_axis=0, tiled=True)  11.5 us
    all_to_all x2, starting transfers between devices, exchange(): return lax.all_to_all(x, axes, split_axis=0, concat_axis=0, tiled=True)  10.8 us
    all_to_all x2, waiting for transfers between devices, exchange(): return lax.all_to_all(x, axes, split_axis=0, concat_axis=0, tiled=True)  9.25 us
    ppermute x1, waiting for transfers between devices, shards(): parts = exchange(add_halves(mine, lax.ppermute(cross, 'zh', swap)), GROUP)  6.67 us
    ppermute x1, starting transfers between devices, shards(): weights, own = softmax_weights(logits, mine, lax.ppermute(mine, 'zh', swap))  6.38 us
    ppermute x1, starting transfers between devices, shards(): parts = exchange(add_halves(mine, lax.ppermute(cross, 'zh', swap)), GROUP)  6.37 us
    ppermute x3, starting transfers between devices, shards(): lax.ppermute(weights, 'seq', [(k, (k + d) % 4) for k in range(4)])  5.91 us
    ppermute x3, waiting for transfers between devices, shards(): lax.ppermute(weights, 'seq', [(k, (k + d) % 4) for k in range(4)])  5.38 us
  transfers between devices with their start and end apart: 9, of which 9 were waited for; matrix products, arithmetic and copies ran while one was open for 0% of the time, Pallas kernels for 11%

profile of v6, /device:TPU:32, one launch (start us, length us, event | category | flops | bytes accessed | tf_op | source)
XLA Modules:
  0.0 79.4 jit_solution(17221784673626869645)
XLA Ops:
  0.0 2.9 %pair_logits.1 = f32[8,2,32,128]{3,2,1,0:T(8,128)} custom-call(bf16[64,64,128]{2,1,0:T(8,128)(2,1)} %pair_ref.1, s32[1,64]{1,0:T(1,128)} %bitcast.18, bf16[8,128]{1,0:T(8,128)(2,1)} %bitcast.17), custom_call_target="tpu_custom_call" | custom-call | flops 400000000 | bytes 1400000 | tf_op jit(solution)/shard_map/pair_logits/pallas_call | solution.py:51
  2.9 7.0 %all-to-all-start = ((f32[16,32,128]{2,1,0:T(8,128)}), f32[16,32,128]{2,1,0:T(8,128)S(1)}, u32[]{:S(2)}, u32[]{:S(2)}) async-start(f32[16,32,128]{2,1,0:T(8,128)} %bitcast.15), calls=%async_computation | async-start | bytes 524288 | tf_op jit(solution)/shard_map/all_to_all | solution.py:337
  10.0 4.8 %msa_values.1 = bf16[8,2,8,64,128]{4,3,2,1,0:T(8,128)(2,1)} custom-call(bf16[256,4096]{1,0:T(8,128)(2,1)} %m_ref.2, bf16[64,64]{1,0:T(8,128)(2,1)} %content_ref.1), custom_call_target="tpu_custom_call" | custom-call | flops 2000000000 | bytes 4500000 | tf_op jit(solution)/shard_map/msa_values/pallas_call | solution.py:111
  14.8 3.7 %all-to-all-done.l_ref = f32[16,32,128]{2,1,0:T(8,128)S(1)} async-done(((f32[16,32,128]{2,1,0:T(8,128)}), f32[16,32,128]{2,1,0:T(8,128)S(1)}, u32[]{:S(2)}, u32[]{:S(2)}) %all-to-all-start) | async-done | bytes 262176 | tf_op jit(solution)/shard_map/all_to_all | solution.py:337
  18.5 3.7 %all-to-all-start.1 = ((bf16[16,512,128]{2,1,0:T(8,128)(2,1)}), bf16[16,512,128]{2,1,0:T(8,128)(2,1)S(1)}, u32[]{:S(2)}, u32[]{:S(2)}) async-start(bf16[16,512,128]{2,1,0:T(8,128)(2,1)} %bitcast.14), calls=%async_computation.1 | async-start | bytes 4194304 | tf_op jit(solution)/shard_map/all_to_all | solution.py:337
  22.2 0.2 local_stats.1.a_ref
  22.4 0.1 collective-permute-start
  22.5 1.2 %collective-permute-done.b_ref = f32[2,32,128]{2,1,0:T(8,128)S(1)} collective-permute-done((f32[2,32,128]{2,1,0:T(8,128)S(1)}, f32[2,32,128]{2,1,0:T(8,128)S(1)}, u32[]{:S(2)}, u32[]{:S(2)}) %collective-permute-start) | collective-permute-done | bytes 32800 | tf_op jit(solution)/shard_map/ppermute | solution.py:356
  23.7 6.4 %collective-permute-start.1 = (f32[2,32,128]{2,1,0:T(8,128)S(1)}, f32[2,32,128]{2,1,0:T(8,128)S(1)}, u32[]{:S(2)}, u32[]{:S(2)}) collective-permute-start(f32[2,32,128]{2,1,0:T(8,128)S(1)} %merge_stats.1.a_ref), channel_id=1, source_target_pairs={{0,8},{8,0},{1,9},{9,1},{2,10},{10,2},{3,11},{11,3},{4,12},{12,4},... | collective-permute-start | bytes 98312 | tf_op jit(solution)/shard_map/ppermute | solution.py:357
  30.1 1.9 %collective-permute-done.1.b_ref = f32[2,32,128]{2,1,0:T(8,128)S(1)} collective-permute-done((f32[2,32,128]{2,1,0:T(8,128)S(1)}, f32[2,32,128]{2,1,0:T(8,128)S(1)}, u32[]{:S(2)}, u32[]{:S(2)}) %collective-permute-start.1) | collective-permute-done | bytes 32800 | tf_op jit(solution)/shard_map/ppermute | solution.py:357
  32.0 0.1 softmax_weights.1
  32.2 1.1 %collective-permute-start.4 = (bf16[64,1024]{1,0:T(8,128)(2,1)S(1)}, bf16[64,1024]{1,0:T(8,128)(2,1)S(1)}, u32[]{:S(2)}, u32[]{:S(2)}) collective-permute-start(bf16[64,1024]{1,0:T(8,128)(2,1)S(1)} %get-tuple-element.19), channel_id=1, source_target_pairs={{0,192},{64,0},{128,64},{192,128},{1,193},{65,1},{129,65},{193,129... | collective-permute-start | bytes 393224 | tf_op jit(solution)/shard_map/ppermute | solution.py:359
  33.2 2.5 %collective-permute-start.3 = (bf16[64,1024]{1,0:T(8,128)(2,1)S(1)}, bf16[64,1024]{1,0:T(8,128)(2,1)S(1)}, u32[]{:S(2)}, u32[]{:S(2)}) collective-permute-start(bf16[64,1024]{1,0:T(8,128)(2,1)S(1)} %get-tuple-element.19), channel_id=1, source_target_pairs={{0,128},{64,192},{128,0},{192,64},{1,129},{65,193},{129,1},{193,65... | collective-permute-start | bytes 393224 | tf_op jit(solution)/shard_map/ppermute | solution.py:359
  35.8 2.3 %collective-permute-start.2 = (bf16[64,1024]{1,0:T(8,128)(2,1)S(1)}, bf16[64,1024]{1,0:T(8,128)(2,1)S(1)}, u32[]{:S(2)}, u32[]{:S(2)}) collective-permute-start(bf16[64,1024]{1,0:T(8,128)(2,1)S(1)} %get-tuple-element.19), channel_id=1, source_target_pairs={{0,64},{64,128},{128,192},{192,0},{1,65},{65,129},{129,193},{193,1... | collective-permute-start | bytes 393224 | tf_op jit(solution)/shard_map/ppermute | solution.py:359
  38.1 0.1 stack.35.place_ref
  38.1 2.1 %msa_gate.1 = (f32[256,256]{1,0:T(8,128)}, bf16[256,256]{1,0:T(8,128)(2,1)}) custom-call(bf16[256,4096]{1,0:T(8,128)(2,1)} %m_ref.2, s32[1,256]{1,0:T(1,128)} %bitcast.16, bf16[64,64]{1,0:T(8,128)(2,1)} %sigmoid_ref.1, bf16[64,64]{1,0:T(8,128)(2,1)} %closing_ref.1), custom_call_target="tpu_custom_call" | custom-call | flops 100000000 | bytes 600000 | tf_op jit(solution)/shard_map/msa_gate/pallas_call | solution.py:136
  40.3 3.3 %collective-permute-done.4.w3 = bf16[64,1024]{1,0:T(8,128)(2,1)S(1)} collective-permute-done((bf16[64,1024]{1,0:T(8,128)(2,1)S(1)}, bf16[64,1024]{1,0:T(8,128)(2,1)S(1)}, u32[]{:S(2)}, u32[]{:S(2)}) %collective-permute-start.4) | collective-permute-done | bytes 131104 | tf_op jit(solution)/shard_map/ppermute | solution.py:359
  43.6 0.2 collective-permute-done.3.w2
  43.8 1.8 %collective-permute-done.2.w1 = bf16[64,1024]{1,0:T(8,128)(2,1)S(1)} collective-permute-done((bf16[64,1024]{1,0:T(8,128)(2,1)S(1)}, bf16[64,1024]{1,0:T(8,128)(2,1)S(1)}, u32[]{:S(2)}, u32[]{:S(2)}) %collective-permute-start.2) | collective-permute-done | bytes 131104 | tf_op jit(solution)/shard_map/ppermute | solution.py:359
  45.6 5.5 %all-to-all-done.1 = bf16[16,512,128]{2,1,0:T(8,128)(2,1)S(1)} async-done(((bf16[16,512,128]{2,1,0:T(8,128)(2,1)}), bf16[16,512,128]{2,1,0:T(8,128)(2,1)S(1)}, u32[]{:S(2)}, u32[]{:S(2)}) %all-to-all-start.1) | async-done | bytes 2097184 | tf_op jit(solution)/shard_map/all_to_all | solution.py:337
  51.2 1.1 %partial_average.3 = bf16[32,32,128]{2,1,0:T(8,128)(2,1)S(1)} custom-call(s32[5]{0:T(128)S(1)} %stack.35.place_ref, bf16[64,1024]{1,0:T(8,128)(2,1)S(1)} %get-tuple-element.23.w0, bf16[64,1024]{1,0:T(8,128)(2,1)S(1)} %collective-permute-done.2.w1, bf16[64,1024]{1,0:T(8,128)(2,1)S(1)} %collective-permute-done.3.w2, ...), custom_call_target="tpu_custom_call" | custom-call | flops 300000000 | bytes 2800000 | tf_op jit(solution)/shard_map/partial_average/pallas_call | solution.py:258
  52.2 0.1 collective-permute-start.5
  52.3 0.1 stack.33.place_ref
  52.4 0.0 copy-start
  52.4 0.0 copy-start.1
  52.4 1.1 %partial_average.2.a_ref = f32[32,32,128]{2,1,0:T(8,128)S(1)} custom-call(s32[5]{0:T(128)S(1)} %stack.33.place_ref, bf16[64,1024]{1,0:T(8,128)(2,1)S(1)} %get-tuple-element.23.w0, bf16[64,1024]{1,0:T(8,128)(2,1)S(1)} %collective-permute-done.2.w1, bf16[64,1024]{1,0:T(8,128)(2,1)S(1)} %collective-permute-done.3.w2, ...), custom_call_target="tpu_custom_call" | custom-call | flops 300000000 | bytes 2800000 | tf_op jit(solution)/shard_map/partial_average/pallas_call | solution.py:258
  53.5 0.4 collective-permute-done.5.b_ref
  53.9 6.4 %collective-permute-start.6 = (bf16[16,32,128]{2,1,0:T(8,128)(2,1)S(1)}, bf16[16,32,128]{2,1,0:T(8,128)(2,1)S(1)}, u32[]{:S(2)}, u32[]{:S(2)}) collective-permute-start(bf16[16,32,128]{2,1,0:T(8,128)(2,1)S(1)} %get-tuple-element.28), channel_id=1, source_target_pairs={{0,8},{8,0},{1,9},{9,1},{2,10},{10,2},{3,11},{11,3},{4,12},{12,4},... | collective-permute-start | bytes 393224 | tf_op jit(solution)/shard_map/ppermute | solution.py:374
  60.3 6.7 %collective-permute-done.6.b_ref = bf16[16,32,128]{2,1,0:T(8,128)(2,1)S(1)} collective-permute-done((bf16[16,32,128]{2,1,0:T(8,128)(2,1)S(1)}, bf16[16,32,128]{2,1,0:T(8,128)(2,1)S(1)}, u32[]{:S(2)}, u32[]{:S(2)}) %collective-permute-start.6) | collective-permute-done | bytes 131104 | tf_op jit(solution)/shard_map/ppermute | solution.py:374
  67.0 11.5 %all_to_all.15.p_ref = bf16[16,32,128]{2,1,0:T(8,128)(2,1)S(1)} all-to-all(bf16[16,32,128]{2,1,0:T(8,128)(2,1)S(1)} %add_halves.1), channel_id=1, replica_groups=mesh['seq'=4,'y'=4,'zh'=2,'x'=4,'core'=2] {'x','y'}, dimensions={0} | all-to-all | bytes 262144 | tf_op jit(solution)/shard_map/all_to_all | solution.py:337
  78.5 0.0 copy-done
  78.5 0.0 copy-done.1
  78.5 0.9 %closing.1 = bf16[256,256]{1,0:T(8,128)(2,1)} custom-call(bf16[16,32,128]{2,1,0:T(8,128)(2,1)S(1)} %all_to_all.15.p_ref, f32[256,256]{1,0:T(8,128)S(1)} %copy-done, bf16[256,256]{1,0:T(8,128)(2,1)S(1)} %copy-done.1), custom_call_target="tpu_custom_call" | custom-call | flops 60000000 | bytes 1000000 | tf_op jit(solution)/shard_map/closing/pallas_call | solution.py:324
  (3 shorter events, 0.1 us)
Async XLA Ops:
  2.9 15.6 %all-to-all-start = ((f32[16,32,128]{2,1,0:T(8,128)}), f32[16,32,128]{2,1,0:T(8,128)S(1)}, u32[]{:S(2)}, u32[]{:S(2)}) async-start(f32[16,32,128]{2,1,0:T(8,128)} %bitcast.15), calls=%async_computation | async-start | bytes 524288 | tf_op jit(solution)/shard_map/all_to_all | solution.py:337
  18.5 32.7 %all-to-all-start.1 = ((bf16[16,512,128]{2,1,0:T(8,128)(2,1)}), bf16[16,512,128]{2,1,0:T(8,128)(2,1)S(1)}, u32[]{:S(2)}, u32[]{:S(2)}) async-start(bf16[16,512,128]{2,1,0:T(8,128)(2,1)} %bitcast.14), calls=%async_computation.1 | async-start | bytes 4194304 | tf_op jit(solution)/shard_map/all_to_all | solution.py:337
  22.4 1.3 %collective-permute-start = (f32[2,32,128]{2,1,0:T(8,128)S(1)}, f32[2,32,128]{2,1,0:T(8,128)S(1)}, u32[]{:S(2)}, u32[]{:S(2)}) collective-permute-start(f32[2,32,128]{2,1,0:T(8,128)S(1)} %local_stats.1.a_ref), channel_id=1, source_target_pairs={{0,1},{1,0},{2,3},{3,2},{4,5},{5,4},{6,7},{7,6},{8,9},{9,8},{10,11... | collective-permute-start | bytes 98312 | tf_op jit(solution)/shard_map/ppermute | solution.py:356
  23.7 8.3 %collective-permute-start.1 = (f32[2,32,128]{2,1,0:T(8,128)S(1)}, f32[2,32,128]{2,1,0:T(8,128)S(1)}, u32[]{:S(2)}, u32[]{:S(2)}) collective-permute-start(f32[2,32,128]{2,1,0:T(8,128)S(1)} %merge_stats.1.a_ref), channel_id=1, source_target_pairs={{0,8},{8,0},{1,9},{9,1},{2,10},{10,2},{3,11},{11,3},{4,12},{12,4},... | collective-permute-start | bytes 98312 | tf_op jit(solution)/shard_map/ppermute | solution.py:357
  32.2 11.4 %collective-permute-start.4 = (bf16[64,1024]{1,0:T(8,128)(2,1)S(1)}, bf16[64,1024]{1,0:T(8,128)(2,1)S(1)}, u32[]{:S(2)}, u32[]{:S(2)}) collective-permute-start(bf16[64,1024]{1,0:T(8,128)(2,1)S(1)} %get-tuple-element.19), channel_id=1, source_target_pairs={{0,192},{64,0},{128,64},{192,128},{1,193},{65,1},{129,65},{193,129... | collective-permute-start | bytes 393224 | tf_op jit(solution)/shard_map/ppermute | solution.py:359
  33.2 10.5 %collective-permute-start.3 = (bf16[64,1024]{1,0:T(8,128)(2,1)S(1)}, bf16[64,1024]{1,0:T(8,128)(2,1)S(1)}, u32[]{:S(2)}, u32[]{:S(2)}) collective-permute-start(bf16[64,1024]{1,0:T(8,128)(2,1)S(1)} %get-tuple-element.19), channel_id=1, source_target_pairs={{0,128},{64,192},{128,0},{192,64},{1,129},{65,193},{129,1},{193,65... | collective-permute-start | bytes 393224 | tf_op jit(solution)/shard_map/ppermute | solution.py:359
  35.8 9.9 %collective-permute-start.2 = (bf16[64,1024]{1,0:T(8,128)(2,1)S(1)}, bf16[64,1024]{1,0:T(8,128)(2,1)S(1)}, u32[]{:S(2)}, u32[]{:S(2)}) collective-permute-start(bf16[64,1024]{1,0:T(8,128)(2,1)S(1)} %get-tuple-element.19), channel_id=1, source_target_pairs={{0,64},{64,128},{128,192},{192,0},{1,65},{65,129},{129,193},{193,1... | collective-permute-start | bytes 393224 | tf_op jit(solution)/shard_map/ppermute | solution.py:359
  52.2 1.6 %collective-permute-start.5 = (bf16[32,32,128]{2,1,0:T(8,128)(2,1)S(1)}, bf16[32,32,128]{2,1,0:T(8,128)(2,1)S(1)}, u32[]{:S(2)}, u32[]{:S(2)}) collective-permute-start(bf16[32,32,128]{2,1,0:T(8,128)(2,1)S(1)} %partial_average.3), channel_id=1, source_target_pairs={{0,1},{1,0},{2,3},{3,2},{4,5},{5,4},{6,7},{7,6},{8,9},{9,8},{10,11... | collective-permute-start | bytes 786440 | tf_op jit(solution)/shard_map/ppermute | solution.py:371
  52.4 26.1 %copy-start = (f32[256,256]{1,0:T(8,128)S(1)}, f32[256,256]{1,0:T(8,128)}, u32[]{:S(2)}) copy-start(f32[256,256]{1,0:T(8,128)} %get-tuple-element.29.gate_ref) | copy-start | bytes 786436
  52.4 26.1 %copy-start.1 = (bf16[256,256]{1,0:T(8,128)(2,1)S(1)}, bf16[256,256]{1,0:T(8,128)(2,1)}, u32[]{:S(2)}) copy-start(bf16[256,256]{1,0:T(8,128)(2,1)} %get-tuple-element.30.block_ref) | copy-start | bytes 393220
  53.9 13.0 %collective-permute-start.6 = (bf16[16,32,128]{2,1,0:T(8,128)(2,1)S(1)}, bf16[16,32,128]{2,1,0:T(8,128)(2,1)S(1)}, u32[]{:S(2)}, u32[]{:S(2)}) collective-permute-start(bf16[16,32,128]{2,1,0:T(8,128)(2,1)S(1)} %get-tuple-element.28), channel_id=1, source_target_pairs={{0,8},{8,0},{1,9},{9,1},{2,10},{10,2},{3,11},{11,3},{4,12},{12,4},... | collective-permute-start | bytes 393224 | tf_op jit(solution)/shard_map/ppermute | solution.py:374

commit v7 on v6

--- a/solution.py
+++ b/solution.py
@@ -31,8 +31,9 @@
     return jnp.where(cond, 1.0, 0.0).astype(BF16)
 
 
-def logits_kernel(pair_ref, mask_ref, weight_ref, out_ref, scr):
-    x = pair_ref[...].reshape(4096, 128)
+def logits_kernel(low_ref, high_ref, mask_ref, weight_ref, out_ref, scr):
+    halves = [ref[...].reshape(2048, 128) for ref in (low_ref, high_ref)]
+    x = jnp.concatenate(halves, axis=0)
     centered = x.astype(F32) - dot(x, jnp.full((128, 128), 1.0 / 128, BF16))
     variance = jnp.mean(centered * centered, axis=-1, keepdims=True)
     normed = (centered * lax.rsqrt(variance + EPS)).astype(BF16)
@@ -53,7 +54,8 @@
         grid=(1,),
         out_shape=jax.ShapeDtypeStruct((8, 2, 32, 128), F32),
         in_specs=[
-            pl.BlockSpec((64, 64, 128), lambda i: (0, 0, 0)),
+            pl.BlockSpec((32, 64, 128), lambda i: (0, 0, 0)),
+            pl.BlockSpec((32, 64, 128), lambda i: (1, 0, 0)),
             pl.BlockSpec((1, 64), lambda i: (0, 0)),
             pl.BlockSpec((8, 128), lambda i: (0, 0)),
         ],
@@ -63,7 +65,7 @@
             flops=400_000_000, bytes_accessed=1_400_000, transcendentals=500_000
         ),
         name="pair_logits",
-    )(pair, mask, weight_t)
+    )(pair, pair, mask, weight_t)
 
 
 def diagonal(matrix, transposed=False, by_column=False):
@@ -228,8 +230,9 @@
     )(logits, a, b)
 
 
-def average_kernel(place_ref, w0, w1, w2, w3, v_ref, out_ref, wall, scr):
-    side = pl.multiple_of(place_ref[4] * 32, 32)
+def average_kernel(other, place_ref, w0, w1, w2, w3, v_ref, out_ref, wall, scr):
+    core = 1 - place_ref[4] if other else place_ref[4]
+    side = pl.multiple_of(core * 32, 32)
     for k, w in enumerate((w0, w1, w2, w3)):
         start = pl.multiple_of(place_ref[k] * 32, 32)
         wall[pl.ds(start, 32), :] = w[pl.ds(side, 32), :]
@@ -253,11 +256,11 @@
                 out_ref[zh * 16 + x * 4 + y] = scr[start : start + 32].astype(out_ref.dtype)
 
 
-def partial_average(place, weights, values, dtype):
+def partial_average(place, weights, values, other):
     vmem = pl.BlockSpec(memory_space=pltpu.VMEM)
     return pl.pallas_call(
-        average_kernel,
-        out_shape=jax.ShapeDtypeStruct((32, 32, 128), dtype),
+        functools.partial(average_kernel, other),
+        out_shape=jax.ShapeDtypeStruct((32, 32, 128), BF16 if other else F32),
         in_specs=[pl.BlockSpec(memory_space=pltpu.SMEM)] + [vmem] * 5,
         out_specs=vmem,
         scratch_shapes=[pltpu.VMEM((128, 1024), BF16), pltpu.VMEM((1024, 128), F32)],
@@ -367,9 +370,10 @@
     q, core = lax.axis_index("seq"), lax.axis_index("core")
     order = [(q - d) % 4 for d in range(4)]
     values = values.reshape(16, 8, 64, 128)
-    theirs = partial_average(jnp.stack(order + [1 - core]), gathered, values, BF16)
+    place = jnp.stack(order + [core])
+    theirs = partial_average(place, gathered, values, True)
     theirs = lax.ppermute(theirs, "core", swap)
-    ours = partial_average(jnp.stack(order + [core]), gathered, values, F32)
+    ours = partial_average(place, gathered, values, False)
     mine, cross = add_cores(ours, theirs)
     parts = exchange(add_halves(mine, lax.ppermute(cross, "zh", swap)), GROUP)
     return close(parts, gate, block)

time: 79.7 us -> 79.7 us (level)
  no operation moved by 1% of the time
where the time goes in v7:
time: 79.7 us; the launch traced here: 79.4 us
  starting transfers between devices  29.6 us (37%)
  waiting for transfers between devices  24.8 us (31%)
  Pallas kernels  13.3 us (17%)
  blocking collectives  11.6 us (15%)
    all_to_all x1, blocking collectives, exchange(): return lax.all_to_all(x, axes, split_axis=0, concat_axis=0, tiled=True)  11.6 us
    all_to_all x2, starting transfers between devices, exchange(): return lax.all_to_all(x, axes, split_axis=0, concat_axis=0, tiled=True)  10.8 us
    all_to_all x2, waiting for transfers between devices, exchange(): return lax.all_to_all(x, axes, split_axis=0, concat_axis=0, tiled=True)  9.24 us
    ppermute x1, waiting for transfers between devices, shards(): parts = exchange(add_halves(mine, lax.ppermute(cross, 'zh', swap)), GROUP)  6.65 us
    ppermute x1, starting transfers between devices, shards(): parts = exchange(add_halves(mine, lax.ppermute(cross, 'zh', swap)), GROUP)  6.38 us
    ppermute x1, starting transfers between devices, shards(): weights, own = softmax_weights(logits, mine, lax.ppermute(mine, 'zh', swap))  6.38 us
    ppermute x3, starting transfers between devices, shards(): lax.ppermute(weights, 'seq', [(k, (k + d) % 4) for k in range(4)])  5.91 us
    ppermute x3, waiting for transfers between devices, shards(): lax.ppermute(weights, 'seq', [(k, (k + d) % 4) for k in range(4)])  5.38 us
  transfers between devices with their start and end apart: 9, of which 9 were waited for; matrix products, arithmetic and copies ran while one was open for 0% of the time, Pallas kernels for 11%

profile of v7, /device:TPU:32, one launch (start us, length us, event | category | flops | bytes accessed | tf_op | source)
XLA Modules:
  0.0 79.4 jit_solution(2888485396198891345)
XLA Ops:
  0.0 2.9 %pair_logits.1 = f32[8,2,32,128]{3,2,1,0:T(8,128)} custom-call(bf16[64,64,128]{2,1,0:T(8,128)(2,1)} %high_ref.1, bf16[64,64,128]{2,1,0:T(8,128)(2,1)} %high_ref.1, s32[1,64]{1,0:T(1,128)} %bitcast.17, bf16[8,128]{1,0:T(8,128)(2,1)} %bitcast.15), custom_call_target="tpu_custom_call" | custom-call | flops 400000000 | bytes 1400000 | tf_op jit(solution)/shard_map/pair_logits/pallas_call | solution.py:52
  2.9 7.0 %all-to-all-start = ((f32[16,32,128]{2,1,0:T(8,128)}), f32[16,32,128]{2,1,0:T(8,128)S(1)}, u32[]{:S(2)}, u32[]{:S(2)}) async-start(f32[16,32,128]{2,1,0:T(8,128)} %bitcast.14), calls=%async_computation | async-start | bytes 524288 | tf_op jit(solution)/shard_map/all_to_all | solution.py:340
  9.9 4.8 %msa_values.1 = bf16[8,2,8,64,128]{4,3,2,1,0:T(8,128)(2,1)} custom-call(bf16[256,4096]{1,0:T(8,128)(2,1)} %m_ref.2, bf16[64,64]{1,0:T(8,128)(2,1)} %content_ref.1), custom_call_target="tpu_custom_call" | custom-call | flops 2000000000 | bytes 4500000 | tf_op jit(solution)/shard_map/msa_values/pallas_call | solution.py:113
  14.7 3.7 %all-to-all-done.l_ref = f32[16,32,128]{2,1,0:T(8,128)S(1)} async-done(((f32[16,32,128]{2,1,0:T(8,128)}), f32[16,32,128]{2,1,0:T(8,128)S(1)}, u32[]{:S(2)}, u32[]{:S(2)}) %all-to-all-start) | async-done | bytes 262176 | tf_op jit(solution)/shard_map/all_to_all | solution.py:340
  18.4 3.7 %all-to-all-start.1 = ((bf16[16,512,128]{2,1,0:T(8,128)(2,1)}), bf16[16,512,128]{2,1,0:T(8,128)(2,1)S(1)}, u32[]{:S(2)}, u32[]{:S(2)}) async-start(bf16[16,512,128]{2,1,0:T(8,128)(2,1)} %bitcast.13), calls=%async_computation.1 | async-start | bytes 4194304 | tf_op jit(solution)/shard_map/all_to_all | solution.py:340
  22.2 0.2 local_stats.1.a_ref
  22.4 0.1 collective-permute-start
  22.5 1.2 %collective-permute-done.b_ref = f32[2,32,128]{2,1,0:T(8,128)S(1)} collective-permute-done((f32[2,32,128]{2,1,0:T(8,128)S(1)}, f32[2,32,128]{2,1,0:T(8,128)S(1)}, u32[]{:S(2)}, u32[]{:S(2)}) %collective-permute-start) | collective-permute-done | bytes 32800 | tf_op jit(solution)/shard_map/ppermute | solution.py:359
  23.7 6.4 %collective-permute-start.1 = (f32[2,32,128]{2,1,0:T(8,128)S(1)}, f32[2,32,128]{2,1,0:T(8,128)S(1)}, u32[]{:S(2)}, u32[]{:S(2)}) collective-permute-start(f32[2,32,128]{2,1,0:T(8,128)S(1)} %merge_stats.1.a_ref), channel_id=1, source_target_pairs={{0,8},{8,0},{1,9},{9,1},{2,10},{10,2},{3,11},{11,3},{4,12},{12,4},... | collective-permute-start | bytes 98312 | tf_op jit(solution)/shard_map/ppermute | solution.py:360
  30.1 1.9 %collective-permute-done.1.b_ref = f32[2,32,128]{2,1,0:T(8,128)S(1)} collective-permute-done((f32[2,32,128]{2,1,0:T(8,128)S(1)}, f32[2,32,128]{2,1,0:T(8,128)S(1)}, u32[]{:S(2)}, u32[]{:S(2)}) %collective-permute-start.1) | collective-permute-done | bytes 32800 | tf_op jit(solution)/shard_map/ppermute | solution.py:360
  32.0 0.1 softmax_weights.1
  32.1 1.1 %collective-permute-start.4 = (bf16[64,1024]{1,0:T(8,128)(2,1)S(1)}, bf16[64,1024]{1,0:T(8,128)(2,1)S(1)}, u32[]{:S(2)}, u32[]{:S(2)}) collective-permute-start(bf16[64,1024]{1,0:T(8,128)(2,1)S(1)} %get-tuple-element.19), channel_id=1, source_target_pairs={{0,192},{64,0},{128,64},{192,128},{1,193},{65,1},{129,65},{193,129... | collective-permute-start | bytes 393224 | tf_op jit(solution)/shard_map/ppermute | solution.py:362
  33.2 2.5 %collective-permute-start.3 = (bf16[64,1024]{1,0:T(8,128)(2,1)S(1)}, bf16[64,1024]{1,0:T(8,128)(2,1)S(1)}, u32[]{:S(2)}, u32[]{:S(2)}) collective-permute-start(bf16[64,1024]{1,0:T(8,128)(2,1)S(1)} %get-tuple-element.19), channel_id=1, source_target_pairs={{0,128},{64,192},{128,0},{192,64},{1,129},{65,193},{129,1},{193,65... | collective-permute-start | bytes 393224 | tf_op jit(solution)/shard_map/ppermute | solution.py:362
  35.7 2.3 %collective-permute-start.2 = (bf16[64,1024]{1,0:T(8,128)(2,1)S(1)}, bf16[64,1024]{1,0:T(8,128)(2,1)S(1)}, u32[]{:S(2)}, u32[]{:S(2)}) collective-permute-start(bf16[64,1024]{1,0:T(8,128)(2,1)S(1)} %get-tuple-element.19), channel_id=1, source_target_pairs={{0,64},{64,128},{128,192},{192,0},{1,65},{65,129},{129,193},{193,1... | collective-permute-start | bytes 393224 | tf_op jit(solution)/shard_map/ppermute | solution.py:362
  38.0 0.1 stack.23.place_ref
  38.1 2.1 %msa_gate.1 = (f32[256,256]{1,0:T(8,128)}, bf16[256,256]{1,0:T(8,128)(2,1)}) custom-call(bf16[256,4096]{1,0:T(8,128)(2,1)} %m_ref.2, s32[1,256]{1,0:T(1,128)} %bitcast.16, bf16[64,64]{1,0:T(8,128)(2,1)} %sigmoid_ref.1, bf16[64,64]{1,0:T(8,128)(2,1)} %closing_ref.1), custom_call_target="tpu_custom_call" | custom-call | flops 100000000 | bytes 600000 | tf_op jit(solution)/shard_map/msa_gate/pallas_call | solution.py:138
  40.2 3.3 %collective-permute-done.4.w3 = bf16[64,1024]{1,0:T(8,128)(2,1)S(1)} collective-permute-done((bf16[64,1024]{1,0:T(8,128)(2,1)S(1)}, bf16[64,1024]{1,0:T(8,128)(2,1)S(1)}, u32[]{:S(2)}, u32[]{:S(2)}) %collective-permute-start.4) | collective-permute-done | bytes 131104 | tf_op jit(solution)/shard_map/ppermute | solution.py:362
  43.5 0.2 collective-permute-done.3.w2
  43.8 1.8 %collective-permute-done.2.w1 = bf16[64,1024]{1,0:T(8,128)(2,1)S(1)} collective-permute-done((bf16[64,1024]{1,0:T(8,128)(2,1)S(1)}, bf16[64,1024]{1,0:T(8,128)(2,1)S(1)}, u32[]{:S(2)}, u32[]{:S(2)}) %collective-permute-start.2) | collective-permute-done | bytes 131104 | tf_op jit(solution)/shard_map/ppermute | solution.py:362
  45.6 5.5 %all-to-all-done.1 = bf16[16,512,128]{2,1,0:T(8,128)(2,1)S(1)} async-done(((bf16[16,512,128]{2,1,0:T(8,128)(2,1)}), bf16[16,512,128]{2,1,0:T(8,128)(2,1)S(1)}, u32[]{:S(2)}, u32[]{:S(2)}) %all-to-all-start.1) | async-done | bytes 2097184 | tf_op jit(solution)/shard_map/all_to_all | solution.py:340
  51.1 1.0 %partial_average.3 = bf16[32,32,128]{2,1,0:T(8,128)(2,1)S(1)} custom-call(s32[5]{0:T(128)S(1)} %stack.23.place_ref, bf16[64,1024]{1,0:T(8,128)(2,1)S(1)} %get-tuple-element.23.w0, bf16[64,1024]{1,0:T(8,128)(2,1)S(1)} %collective-permute-done.2.w1, bf16[64,1024]{1,0:T(8,128)(2,1)S(1)} %collective-permute-done.3.w2, ...), custom_call_target="tpu_custom_call" | custom-call | flops 300000000 | bytes 2800000 | tf_op jit(solution)/shard_map/partial_average/pallas_call | solution.py:261
  52.2 0.0 copy-start
  52.2 0.0 copy-start.1
  52.2 0.1 collective-permute-start.5
  52.3 1.1 %partial_average.2.a_ref = f32[32,32,128]{2,1,0:T(8,128)S(1)} custom-call(s32[5]{0:T(128)S(1)} %stack.23.place_ref, bf16[64,1024]{1,0:T(8,128)(2,1)S(1)} %get-tuple-element.23.w0, bf16[64,1024]{1,0:T(8,128)(2,1)S(1)} %collective-permute-done.2.w1, bf16[64,1024]{1,0:T(8,128)(2,1)S(1)} %collective-permute-done.3.w2, ...), custom_call_target="tpu_custom_call" | custom-call | flops 300000000 | bytes 2800000 | tf_op jit(solution)/shard_map/partial_average/pallas_call | solution.py:261
  53.4 0.5 collective-permute-done.5.b_ref
  53.9 6.4 %collective-permute-start.6 = (bf16[16,32,128]{2,1,0:T(8,128)(2,1)S(1)}, bf16[16,32,128]{2,1,0:T(8,128)(2,1)S(1)}, u32[]{:S(2)}, u32[]{:S(2)}) collective-permute-start(bf16[16,32,128]{2,1,0:T(8,128)(2,1)S(1)} %get-tuple-element.28), channel_id=1, source_target_pairs={{0,8},{8,0},{1,9},{9,1},{2,10},{10,2},{3,11},{11,3},{4,12},{12,4},... | collective-permute-start | bytes 393224 | tf_op jit(solution)/shard_map/ppermute | solution.py:378
  60.3 6.7 %collective-permute-done.6.b_ref = bf16[16,32,128]{2,1,0:T(8,128)(2,1)S(1)} collective-permute-done((bf16[16,32,128]{2,1,0:T(8,128)(2,1)S(1)}, bf16[16,32,128]{2,1,0:T(8,128)(2,1)S(1)}, u32[]{:S(2)}, u32[]{:S(2)}) %collective-permute-start.6) | collective-permute-done | bytes 131104 | tf_op jit(solution)/shard_map/ppermute | solution.py:378
  66.9 11.6 %all_to_all.15.p_ref = bf16[16,32,128]{2,1,0:T(8,128)(2,1)S(1)} all-to-all(bf16[16,32,128]{2,1,0:T(8,128)(2,1)S(1)} %add_halves.1), channel_id=1, replica_groups=mesh['seq'=4,'y'=4,'zh'=2,'x'=4,'core'=2] {'x','y'}, dimensions={0} | all-to-all | bytes 262144 | tf_op jit(solution)/shard_map/all_to_all | solution.py:340
  78.5 0.0 copy-done
  78.5 0.0 copy-done.1
  78.5 0.9 %closing.1 = bf16[256,256]{1,0:T(8,128)(2,1)} custom-call(bf16[16,32,128]{2,1,0:T(8,128)(2,1)S(1)} %all_to_all.15.p_ref, f32[256,256]{1,0:T(8,128)S(1)} %copy-done, bf16[256,256]{1,0:T(8,128)(2,1)S(1)} %copy-done.1), custom_call_target="tpu_custom_call" | custom-call | flops 60000000 | bytes 1000000 | tf_op jit(solution)/shard_map/closing/pallas_call | solution.py:327
  (3 shorter events, 0.1 us)
Async XLA Ops:
  2.9 15.6 %all-to-all-start = ((f32[16,32,128]{2,1,0:T(8,128)}), f32[16,32,128]{2,1,0:T(8,128)S(1)}, u32[]{:S(2)}, u32[]{:S(2)}) async-start(f32[16,32,128]{2,1,0:T(8,128)} %bitcast.14), calls=%async_computation | async-start | bytes 524288 | tf_op jit(solution)/shard_map/all_to_all | solution.py:340
  18.4 32.7 %all-to-all-start.1 = ((bf16[16,512,128]{2,1,0:T(8,128)(2,1)}), bf16[16,512,128]{2,1,0:T(8,128)(2,1)S(1)}, u32[]{:S(2)}, u32[]{:S(2)}) async-start(bf16[16,512,128]{2,1,0:T(8,128)(2,1)} %bitcast.13), calls=%async_computation.1 | async-start | bytes 4194304 | tf_op jit(solution)/shard_map/all_to_all | solution.py:340
  22.4 1.3 %collective-permute-start = (f32[2,32,128]{2,1,0:T(8,128)S(1)}, f32[2,32,128]{2,1,0:T(8,128)S(1)}, u32[]{:S(2)}, u32[]{:S(2)}) collective-permute-start(f32[2,32,128]{2,1,0:T(8,128)S(1)} %local_stats.1.a_ref), channel_id=1, source_target_pairs={{0,1},{1,0},{2,3},{3,2},{4,5},{5,4},{6,7},{7,6},{8,9},{9,8},{10,11... | collective-permute-start | bytes 98312 | tf_op jit(solution)/shard_map/ppermute | solution.py:359
  23.7 8.3 %collective-permute-start.1 = (f32[2,32,128]{2,1,0:T(8,128)S(1)}, f32[2,32,128]{2,1,0:T(8,128)S(1)}, u32[]{:S(2)}, u32[]{:S(2)}) collective-permute-start(f32[2,32,128]{2,1,0:T(8,128)S(1)} %merge_stats.1.a_ref), channel_id=1, source_target_pairs={{0,8},{8,0},{1,9},{9,1},{2,10},{10,2},{3,11},{11,3},{4,12},{12,4},... | collective-permute-start | bytes 98312 | tf_op jit(solution)/shard_map/ppermute | solution.py:360
  32.1 11.4 %collective-permute-start.4 = (bf16[64,1024]{1,0:T(8,128)(2,1)S(1)}, bf16[64,1024]{1,0:T(8,128)(2,1)S(1)}, u32[]{:S(2)}, u32[]{:S(2)}) collective-permute-start(bf16[64,1024]{1,0:T(8,128)(2,1)S(1)} %get-tuple-element.19), channel_id=1, source_target_pairs={{0,192},{64,0},{128,64},{192,128},{1,193},{65,1},{129,65},{193,129... | collective-permute-start | bytes 393224 | tf_op jit(solution)/shard_map/ppermute | solution.py:362
  33.2 10.5 %collective-permute-start.3 = (bf16[64,1024]{1,0:T(8,128)(2,1)S(1)}, bf16[64,1024]{1,0:T(8,128)(2,1)S(1)}, u32[]{:S(2)}, u32[]{:S(2)}) collective-permute-start(bf16[64,1024]{1,0:T(8,128)(2,1)S(1)} %get-tuple-element.19), channel_id=1, source_target_pairs={{0,128},{64,192},{128,0},{192,64},{1,129},{65,193},{129,1},{193,65... | collective-permute-start | bytes 393224 | tf_op jit(solution)/shard_map/ppermute | solution.py:362
  35.7 9.9 %collective-permute-start.2 = (bf16[64,1024]{1,0:T(8,128)(2,1)S(1)}, bf16[64,1024]{1,0:T(8,128)(2,1)S(1)}, u32[]{:S(2)}, u32[]{:S(2)}) collective-permute-start(bf16[64,1024]{1,0:T(8,128)(2,1)S(1)} %get-tuple-element.19), channel_id=1, source_target_pairs={{0,64},{64,128},{128,192},{192,0},{1,65},{65,129},{129,193},{193,1... | collective-permute-start | bytes 393224 | tf_op jit(solution)/shard_map/ppermute | solution.py:362
  52.2 26.3 %copy-start = (f32[256,256]{1,0:T(8,128)S(1)}, f32[256,256]{1,0:T(8,128)}, u32[]{:S(2)}) copy-start(f32[256,256]{1,0:T(8,128)} %get-tuple-element.29.gate_ref) | copy-start | bytes 786436
  52.2 26.3 %copy-start.1 = (bf16[256,256]{1,0:T(8,128)(2,1)S(1)}, bf16[256,256]{1,0:T(8,128)(2,1)}, u32[]{:S(2)}) copy-start(bf16[256,256]{1,0:T(8,128)(2,1)} %get-tuple-element.30.block_ref) | copy-start | bytes 393220
  52.2 1.6 %collective-permute-start.5 = (bf16[32,32,128]{2,1,0:T(8,128)(2,1)S(1)}, bf16[32,32,128]{2,1,0:T(8,128)(2,1)S(1)}, u32[]{:S(2)}, u32[]{:S(2)}) collective-permute-start(bf16[32,32,128]{2,1,0:T(8,128)(2,1)S(1)} %partial_average.3), channel_id=1, source_target_pairs={{0,1},{1,0},{2,3},{3,2},{4,5},{5,4},{6,7},{7,6},{8,9},{9,8},{10,11... | collective-permute-start | bytes 786440 | tf_op jit(solution)/shard_map/ppermute | solution.py:375
  53.9 13.0 %collective-permute-start.6 = (bf16[16,32,128]{2,1,0:T(8,128)(2,1)S(1)}, bf16[16,32,128]{2,1,0:T(8,128)(2,1)S(1)}, u32[]{:S(2)}, u32[]{:S(2)}) collective-permute-start(bf16[16,32,128]{2,1,0:T(8,128)(2,1)S(1)} %get-tuple-element.28), channel_id=1, source_target_pairs={{0,8},{8,0},{1,9},{9,1},{2,10},{10,2},{3,11},{11,3},{4,12},{12,4},... | collective-permute-start | bytes 393224 | tf_op jit(solution)/shard_map/ppermute | solution.py:378

commit v8 on v5

--- a/solution.py
+++ b/solution.py
@@ -15,7 +15,6 @@
 NN = (((1,), (0,)), ((), ()))
 TN = (((0,), (0,)), ((), ()))
 GROUP = ("x", "y")
-CHIPS = ("zh", "y", "x")
 RES = ("y", "zh", "x", "core")
 SMALL_LIMIT = 24 * 1024 * 1024
 
@@ -211,7 +210,13 @@
         b = jnp.exp(l_ref[2 * k + 1] - top) / total
         even = jnp.where(low, a, pltpu.roll(b, 64, 1))
         odd = jnp.where(low, pltpu.roll(a, 64, 1), b)
-        block = jnp.concatenate([even[:16], odd[:16], even[16:], odd[16:]], axis=0)
+        eights = [
+            part[core * 16 + zh * 8 : core * 16 + zh * 8 + 8]
+            for zh in range(2)
+            for core in range(2)
+            for part in (even, odd)
+        ]
+        block = jnp.concatenate(eights, axis=0)
         block = block.astype(BF16)
         out_ref[:, k * 128 : (k + 1) * 128] = block
         own_ref[:, k * 128 : (k + 1) * 128] = block
@@ -229,8 +234,10 @@
     )(logits, a, b)
 
 
-def average_kernel(place_ref, w0, w1, w2, w3, v_ref, out_ref, wall, scr):
-    side = pl.multiple_of(place_ref[4] * 32, 32)
+def average_kernel(other, place_ref, w0, w1, w2, w3, v_ref, own_ref, send_ref, wall, scr):
+    core = place_ref[4]
+    half = 1 - place_ref[5] if other else place_ref[5]
+    side = pl.multiple_of(half * 32, 32)
     for k, w in enumerate((w0, w1, w2, w3)):
         start = pl.multiple_of(place_ref[k] * 32, 32)
         wall[pl.ds(start, 32), :] = w[pl.ds(side, 32), :]
@@ -242,25 +249,32 @@
         part = dot(weights, right)
         for e in range(2):
             for q in range(4):
-                for par in range(2):
-                    row = q * 32 + par * 16
-                    scr[pl.ds(q * 256 + par * 8 + 2 * c2 + e, 16, stride=16), :] = part[
-                        row : row + 16, e * 128 : (e + 1) * 128
-                    ]
+                for c in range(2):
+                    for par in range(2):
+                        row = q * 32 + c * 16 + par * 8
+                        start = c * 512 + q * 128 + par * 8 + 2 * c2 + e
+                        scr[pl.ds(start, 8, stride=16), :] = part[
+                            row : row + 8, e * 128 : (e + 1) * 128
+                        ]
     for y in range(4):
-        for zh in range(2):
-            for x in range(4):
-                start = (y * 8 + zh * 4 + x) * 32
-                out_ref[y * 4 + zh * 16 + x * 1] = scr[start : start + 32].astype(out_ref.dtype)
-
-
-def partial_average(place, weights, values, dtype):
+        for x in range(4):
+            at = (y * 4 + x) * 32
+            own = pl.multiple_of(core * 512 + at, 32)
+            send = pl.multiple_of((1 - core) * 512 + at, 32)
+            own_ref[x * 4 + y] = scr[pl.ds(own, 32), :]
+            send_ref[x * 4 + y] = scr[pl.ds(send, 32), :].astype(BF16)
+
+
+def partial_average(place, weights, values, other):
     vmem = pl.BlockSpec(memory_space=pltpu.VMEM)
     return pl.pallas_call(
-        average_kernel,
-        out_shape=jax.ShapeDtypeStruct((32, 32, 128), dtype),
+        functools.partial(average_kernel, other),
+        out_shape=(
+            jax.ShapeDtypeStruct((16, 32, 128), F32),
+            jax.ShapeDtypeStruct((16, 32, 128), BF16),
+        ),
         in_specs=[pl.BlockSpec(memory_space=pltpu.SMEM)] + [vmem] * 5,
-        out_specs=vmem,
+        out_specs=(vmem, vmem),
         scratch_shapes=[pltpu.VMEM((128, 1024), BF16), pltpu.VMEM((1024, 128), F32)],
         compiler_params=pltpu.CompilerParams(vmem_limit_bytes=SMALL_LIMIT),
         cost_estimate=pl.CostEstimate(
@@ -270,29 +284,30 @@
     )(place, *weights, values)
 
 
-def add_kernel(a_ref, b_ref, out_ref):
-    out_ref[...] = (a_ref[...] + b_ref[...].astype(F32)).astype(BF16)
-
-
-def add_cores(a, b):
+def add_kernel(own_ref, *refs):
+    total = own_ref[...]
+    for ref in refs[:-1]:
+        total = total + ref[...].astype(F32)
+    refs[-1][...] = total.astype(BF16)
+
+
+def add_parts(*parts):
     return pl.pallas_call(
         add_kernel,
-        out_shape=jax.ShapeDtypeStruct((32, 32, 128), BF16),
-        compiler_params=pltpu.CompilerParams(vmem_limit_bytes=SMALL_LIMIT),
-        cost_estimate=pl.CostEstimate(
-            flops=200_000, bytes_accessed=1_000_000, transcendentals=0
-        ),
-        name="add_cores",
-    )(a, b)
+        out_shape=jax.ShapeDtypeStruct((16, 32, 128), BF16),
+        compiler_params=pltpu.CompilerParams(vmem_limit_bytes=SMALL_LIMIT),
+        cost_estimate=pl.CostEstimate(
+            flops=100_000, bytes_accessed=500_000, transcendentals=0
+        ),
+        name="add_parts",
+    )(*parts)
 
 
 def closing_kernel(p_ref, gate_ref, block_ref, out_ref, gated):
     for y in range(4):
         for x in range(4):
             head, half = 2 * x + y // 2, y % 2
-            total = sum(
-                p_ref[y * 4 + zh * 16 + x * 1].astype(F32) for zh in range(2)
-            )
+            total = p_ref[x * 4 + y].astype(F32)
             cols = slice(half * 128, half * 128 + 128)
             for i in range(4):
                 rows = slice(i * 64 + head * 8, i * 64 + head * 8 + 8)
@@ -347,10 +362,13 @@
     q, core = lax.axis_index("seq"), lax.axis_index("core")
     order = [(q - d) % 4 for d in range(4)]
     values = values.reshape(16, 8, 64, 128)
-    theirs = partial_average(jnp.stack(order + [1 - core]), gathered, values, BF16)
-    theirs = lax.ppermute(theirs, "core", swap)
-    ours = partial_average(jnp.stack(order + [core]), gathered, values, F32)
-    parts = exchange(add_cores(ours, theirs), CHIPS)
+    place = jnp.stack(order + [core, lax.axis_index("zh")])
+    far, theirs = partial_average(place, gathered, values, True)
+    far = add_parts(far, lax.ppermute(theirs, "core", swap))
+    far = lax.ppermute(far, "zh", swap)
+    near, theirs = partial_average(place, gathered, values, False)
+    parts = add_parts(near, lax.ppermute(theirs, "core", swap), far)
+    parts = exchange(parts, GROUP)
     return close(parts, gate, block)
 
 

time: 80.9 us -> 79.8 us (0.986)
  blocking collectives: 25.8 us -> 11.6 us
  starting transfers between devices: 23.2 us -> 30.2 us
  waiting for transfers between devices: 18.1 us -> 24.3 us
    all_to_all x1, blocking collectives: 25.8 us -> 11.6 us  [exchange(): return lax.all_to_all(x, axes, split_axis=0, concat_axis=0, tiled=True)]
    ppermute x1 -> x3, starting transfers between devices: 0.09 us -> 7.04 us  [the longest x1 6.37 us: shards(): far = lax.ppermute(far, 'zh', swap)]
    ppermute x1 -> x3, waiting for transfers between devices: 0.37 us -> 6.55 us  [the longest x1 6.54 us: shards(): far = lax.ppermute(far, 'zh', swap)]
    pallas_call x3 -> x4, Pallas kernels: 2.18 us -> 2.19 us  [the longest x2 2.12 us: partial_average(): pl.pallas_call(functools.partial(average_kernel, other), out_shape=(jax.S...]
  transfers between devices with their start and end apart: 8 -> 10, of which waited for: 8 -> 8; matrix products, arithmetic and copies ran while one was open for 0% -> 0% of each run, Pallas kernels for 10% -> 11%
where the time goes in v8:
time: 79.8 us; the launch traced here: 79.5 us
  starting transfers between devices  30.2 us (38%)
  waiting for transfers between devices  24.3 us (30%)
  Pallas kernels  13.3 us (17%)
  blocking collectives  11.6 us (15%)
    all_to_all x1, blocking collectives, exchange(): return lax.all_to_all(x, axes, split_axis=0, concat_axis=0, tiled=True)  11.6 us
    all_to_all x2, starting transfers between devices, exchange(): return lax.all_to_all(x, axes, split_axis=0, concat_axis=0, tiled=True)  10.8 us
    all_to_all x2, waiting for transfers between devices, exchange(): return lax.all_to_all(x, axes, split_axis=0, concat_axis=0, tiled=True)  9.25 us
    ppermute x1, waiting for transfers between devices, shards(): far = lax.ppermute(far, 'zh', swap)  6.54 us
    ppermute x1, starting transfers between devices, shards(): weights, own = softmax_weights(logits, mine, lax.ppermute(mine, 'zh', swap))  6.38 us
    ppermute x1, starting transfers between devices, shards(): far = lax.ppermute(far, 'zh', swap)  6.37 us
    ppermute x3, starting transfers between devices, shards(): lax.ppermute(weights, 'seq', [(k, (k + d) % 4) for k in range(4)])  5.91 us
    ppermute x3, waiting for transfers between devices, shards(): lax.ppermute(weights, 'seq', [(k, (k + d) % 4) for k in range(4)])  5.38 us
  transfers between devices with their start and end apart: 10, of which 8 were waited for; matrix products, arithmetic and copies ran while one was open for 0% of the time, Pallas kernels for 11%

profile of v8, /device:TPU:32, one launch (start us, length us, event | category | flops | bytes accessed | tf_op | source)
XLA Modules:
  0.0 79.5 jit_solution(14020354968524674251)
XLA Ops:
  0.0 2.9 %pair_logits.1 = f32[8,2,32,128]{3,2,1,0:T(8,128)} custom-call(bf16[64,64,128]{2,1,0:T(8,128)(2,1)} %pair_ref.1, s32[1,64]{1,0:T(1,128)} %bitcast.18, bf16[8,128]{1,0:T(8,128)(2,1)} %bitcast.17), custom_call_target="tpu_custom_call" | custom-call | flops 400000000 | bytes 1400000 | tf_op jit(solution)/shard_map/pair_logits/pallas_call | solution.py:51
  2.9 7.0 %all-to-all-start = ((f32[16,32,128]{2,1,0:T(8,128)}), f32[16,32,128]{2,1,0:T(8,128)S(1)}, u32[]{:S(2)}, u32[]{:S(2)}) async-start(f32[16,32,128]{2,1,0:T(8,128)} %bitcast.15), calls=%async_computation | async-start | bytes 524288 | tf_op jit(solution)/shard_map/all_to_all | solution.py:332
  10.0 4.8 %msa_values.1 = bf16[8,2,8,64,128]{4,3,2,1,0:T(8,128)(2,1)} custom-call(bf16[256,4096]{1,0:T(8,128)(2,1)} %m_ref.2, bf16[64,64]{1,0:T(8,128)(2,1)} %content_ref.1), custom_call_target="tpu_custom_call" | custom-call | flops 2000000000 | bytes 4500000 | tf_op jit(solution)/shard_map/msa_values/pallas_call | solution.py:111
  14.8 3.7 %all-to-all-done.l_ref = f32[16,32,128]{2,1,0:T(8,128)S(1)} async-done(((f32[16,32,128]{2,1,0:T(8,128)}), f32[16,32,128]{2,1,0:T(8,128)S(1)}, u32[]{:S(2)}, u32[]{:S(2)}) %all-to-all-start) | async-done | bytes 262176 | tf_op jit(solution)/shard_map/all_to_all | solution.py:332
  18.5 3.7 %all-to-all-start.1 = ((bf16[16,512,128]{2,1,0:T(8,128)(2,1)}), bf16[16,512,128]{2,1,0:T(8,128)(2,1)S(1)}, u32[]{:S(2)}, u32[]{:S(2)}) async-start(bf16[16,512,128]{2,1,0:T(8,128)(2,1)} %bitcast.14), calls=%async_computation.1 | async-start | bytes 4194304 | tf_op jit(solution)/shard_map/all_to_all | solution.py:332
  22.2 0.2 local_stats.1.a_ref
  22.5 0.1 collective-permute-start
  22.5 1.2 %collective-permute-done.b_ref = f32[2,32,128]{2,1,0:T(8,128)S(1)} collective-permute-done((f32[2,32,128]{2,1,0:T(8,128)S(1)}, f32[2,32,128]{2,1,0:T(8,128)S(1)}, u32[]{:S(2)}, u32[]{:S(2)}) %collective-permute-start) | collective-permute-done | bytes 32800 | tf_op jit(solution)/shard_map/ppermute | solution.py:351
  23.7 6.4 %collective-permute-start.1 = (f32[2,32,128]{2,1,0:T(8,128)S(1)}, f32[2,32,128]{2,1,0:T(8,128)S(1)}, u32[]{:S(2)}, u32[]{:S(2)}) collective-permute-start(f32[2,32,128]{2,1,0:T(8,128)S(1)} %merge_stats.1.a_ref), channel_id=1, source_target_pairs={{0,8},{8,0},{1,9},{9,1},{2,10},{10,2},{3,11},{11,3},{4,12},{12,4},... | collective-permute-start | bytes 98312 | tf_op jit(solution)/shard_map/ppermute | solution.py:352
  30.1 1.9 %collective-permute-done.1.b_ref = f32[2,32,128]{2,1,0:T(8,128)S(1)} collective-permute-done((f32[2,32,128]{2,1,0:T(8,128)S(1)}, f32[2,32,128]{2,1,0:T(8,128)S(1)}, u32[]{:S(2)}, u32[]{:S(2)}) %collective-permute-start.1) | collective-permute-done | bytes 32800 | tf_op jit(solution)/shard_map/ppermute | solution.py:352
  32.0 0.1 softmax_weights.1
  32.2 1.1 %collective-permute-start.4 = (bf16[64,1024]{1,0:T(8,128)(2,1)S(1)}, bf16[64,1024]{1,0:T(8,128)(2,1)S(1)}, u32[]{:S(2)}, u32[]{:S(2)}) collective-permute-start(bf16[64,1024]{1,0:T(8,128)(2,1)S(1)} %get-tuple-element.21), channel_id=1, source_target_pairs={{0,192},{64,0},{128,64},{192,128},{1,193},{65,1},{129,65},{193,129... | collective-permute-start | bytes 393224 | tf_op jit(solution)/shard_map/ppermute | solution.py:354
  33.3 2.5 %collective-permute-start.3 = (bf16[64,1024]{1,0:T(8,128)(2,1)S(1)}, bf16[64,1024]{1,0:T(8,128)(2,1)S(1)}, u32[]{:S(2)}, u32[]{:S(2)}) collective-permute-start(bf16[64,1024]{1,0:T(8,128)(2,1)S(1)} %get-tuple-element.21), channel_id=1, source_target_pairs={{0,128},{64,192},{128,0},{192,64},{1,129},{65,193},{129,1},{193,65... | collective-permute-start | bytes 393224 | tf_op jit(solution)/shard_map/ppermute | solution.py:354
  35.8 2.3 %collective-permute-start.2 = (bf16[64,1024]{1,0:T(8,128)(2,1)S(1)}, bf16[64,1024]{1,0:T(8,128)(2,1)S(1)}, u32[]{:S(2)}, u32[]{:S(2)}) collective-permute-start(bf16[64,1024]{1,0:T(8,128)(2,1)S(1)} %get-tuple-element.21), channel_id=1, source_target_pairs={{0,64},{64,128},{128,192},{192,0},{1,65},{65,129},{129,193},{193,1... | collective-permute-start | bytes 393224 | tf_op jit(solution)/shard_map/ppermute | solution.py:354
  38.1 0.1 stack.27.place_ref
  38.2 2.1 %msa_gate.1 = (f32[256,256]{1,0:T(8,128)}, bf16[256,256]{1,0:T(8,128)(2,1)}) custom-call(bf16[256,4096]{1,0:T(8,128)(2,1)} %m_ref.2, s32[1,256]{1,0:T(1,128)} %bitcast.16, bf16[64,64]{1,0:T(8,128)(2,1)} %sigmoid_ref.1, bf16[64,64]{1,0:T(8,128)(2,1)} %closing_ref.1), custom_call_target="tpu_custom_call" | custom-call | flops 100000000 | bytes 600000 | tf_op jit(solution)/shard_map/msa_gate/pallas_call | solution.py:136
  40.3 3.3 %collective-permute-done.4.w3 = bf16[64,1024]{1,0:T(8,128)(2,1)S(1)} collective-permute-done((bf16[64,1024]{1,0:T(8,128)(2,1)S(1)}, bf16[64,1024]{1,0:T(8,128)(2,1)S(1)}, u32[]{:S(2)}, u32[]{:S(2)}) %collective-permute-start.4) | collective-permute-done | bytes 131104 | tf_op jit(solution)/shard_map/ppermute | solution.py:354
  43.6 0.2 collective-permute-done.3.w2
  43.8 1.8 %collective-permute-done.2.w1 = bf16[64,1024]{1,0:T(8,128)(2,1)S(1)} collective-permute-done((bf16[64,1024]{1,0:T(8,128)(2,1)S(1)}, bf16[64,1024]{1,0:T(8,128)(2,1)S(1)}, u32[]{:S(2)}, u32[]{:S(2)}) %collective-permute-start.2) | collective-permute-done | bytes 131104 | tf_op jit(solution)/shard_map/ppermute | solution.py:354
  45.6 5.5 %all-to-all-done.1 = bf16[16,512,128]{2,1,0:T(8,128)(2,1)S(1)} async-done(((bf16[16,512,128]{2,1,0:T(8,128)(2,1)}), bf16[16,512,128]{2,1,0:T(8,128)(2,1)S(1)}, u32[]{:S(2)}, u32[]{:S(2)}) %all-to-all-start.1) | async-done | bytes 2097184 | tf_op jit(solution)/shard_map/all_to_all | solution.py:332
  51.2 1.1 %partial_average.3 = (f32[16,32,128]{2,1,0:T(8,128)S(1)}, bf16[16,32,128]{2,1,0:T(8,128)(2,1)S(1)}) custom-call(s32[6]{0:T(128)S(1)} %stack.27.place_ref, bf16[64,1024]{1,0:T(8,128)(2,1)S(1)} %get-tuple-element.25.w0, bf16[64,1024]{1,0:T(8,128)(2,1)S(1)} %collective-permute-done.2.w1, bf16[64,1024]{1,0:T(8,128)(2,1)S(1)} %collective-permute-done.3.w2, ...), custom_call_target="tpu_custom_call" | custom-call | flops 300000000 | bytes 2800000 | tf_op jit(solution)/shard_map/partial_average/pallas_call | solution.py:270
  52.3 0.0 copy-start
  52.3 0.0 copy-start.1
  52.3 0.1 collective-permute-start.6
  52.4 1.1 %partial_average.2 = (f32[16,32,128]{2,1,0:T(8,128)S(1)}, bf16[16,32,128]{2,1,0:T(8,128)(2,1)S(1)}) custom-call(s32[6]{0:T(128)S(1)} %stack.27.place_ref, bf16[64,1024]{1,0:T(8,128)(2,1)S(1)} %get-tuple-element.25.w0, bf16[64,1024]{1,0:T(8,128)(2,1)S(1)} %collective-permute-done.2.w1, bf16[64,1024]{1,0:T(8,128)(2,1)S(1)} %collective-permute-done.3.w2, ...), custom_call_target="tpu_custom_call" | custom-call | flops 300000000 | bytes 2800000 | tf_op jit(solution)/shard_map/partial_average/pallas_call | solution.py:270
  53.4 0.6 collective-permute-start.5
  54.0 0.0 collective-permute-done.6.refs_0_
  54.1 6.4 %collective-permute-start.7 = (bf16[16,32,128]{2,1,0:T(8,128)(2,1)S(1)}, bf16[16,32,128]{2,1,0:T(8,128)(2,1)S(1)}, u32[]{:S(2)}, u32[]{:S(2)}) collective-permute-start(bf16[16,32,128]{2,1,0:T(8,128)(2,1)S(1)} %add_parts.2), channel_id=1, source_target_pairs={{0,8},{8,0},{1,9},{9,1},{2,10},{10,2},{3,11},{11,3},{4,12},{12,4},... | collective-permute-start | bytes 393224 | tf_op jit(solution)/shard_map/ppermute | solution.py:368
  60.4 0.0 collective-permute-done.5.refs_0_
  60.4 6.5 %collective-permute-done.7.refs_1_ = bf16[16,32,128]{2,1,0:T(8,128)(2,1)S(1)} collective-permute-done((bf16[16,32,128]{2,1,0:T(8,128)(2,1)S(1)}, bf16[16,32,128]{2,1,0:T(8,128)(2,1)S(1)}, u32[]{:S(2)}, u32[]{:S(2)}) %collective-permute-start.7) | collective-permute-done | bytes 131104 | tf_op jit(solution)/shard_map/ppermute | solution.py:368
  67.0 11.6 %all_to_all.15.p_ref = bf16[16,32,128]{2,1,0:T(8,128)(2,1)S(1)} all-to-all(bf16[16,32,128]{2,1,0:T(8,128)(2,1)S(1)} %add_parts.3), channel_id=1, replica_groups=mesh['seq'=4,'y'=4,'zh'=2,'x'=4,'core'=2] {'x','y'}, dimensions={0} | all-to-all | bytes 262144 | tf_op jit(solution)/shard_map/all_to_all | solution.py:332
  78.6 0.0 copy-done
  78.6 0.0 copy-done.1
  78.6 0.9 %closing.1 = bf16[256,256]{1,0:T(8,128)(2,1)} custom-call(bf16[16,32,128]{2,1,0:T(8,128)(2,1)S(1)} %all_to_all.15.p_ref, f32[256,256]{1,0:T(8,128)S(1)} %copy-done, bf16[256,256]{1,0:T(8,128)(2,1)S(1)} %copy-done.1), custom_call_target="tpu_custom_call" | custom-call | flops 60000000 | bytes 1000000 | tf_op jit(solution)/shard_map/closing/pallas_call | solution.py:319
  (3 shorter events, 0.1 us)
Async XLA Ops:
  2.9 15.6 %all-to-all-start = ((f32[16,32,128]{2,1,0:T(8,128)}), f32[16,32,128]{2,1,0:T(8,128)S(1)}, u32[]{:S(2)}, u32[]{:S(2)}) async-start(f32[16,32,128]{2,1,0:T(8,128)} %bitcast.15), calls=%async_computation | async-start | bytes 524288 | tf_op jit(solution)/shard_map/all_to_all | solution.py:332
  18.5 32.7 %all-to-all-start.1 = ((bf16[16,512,128]{2,1,0:T(8,128)(2,1)}), bf16[16,512,128]{2,1,0:T(8,128)(2,1)S(1)}, u32[]{:S(2)}, u32[]{:S(2)}) async-start(bf16[16,512,128]{2,1,0:T(8,128)(2,1)} %bitcast.14), calls=%async_computation.1 | async-start | bytes 4194304 | tf_op jit(solution)/shard_map/all_to_all | solution.py:332
  22.5 1.3 %collective-permute-start = (f32[2,32,128]{2,1,0:T(8,128)S(1)}, f32[2,32,128]{2,1,0:T(8,128)S(1)}, u32[]{:S(2)}, u32[]{:S(2)}) collective-permute-start(f32[2,32,128]{2,1,0:T(8,128)S(1)} %local_stats.1.a_ref), channel_id=1, source_target_pairs={{0,1},{1,0},{2,3},{3,2},{4,5},{5,4},{6,7},{7,6},{8,9},{9,8},{10,11... | collective-permute-start | bytes 98312 | tf_op jit(solution)/shard_map/ppermute | solution.py:351
  23.7 8.3 %collective-permute-start.1 = (f32[2,32,128]{2,1,0:T(8,128)S(1)}, f32[2,32,128]{2,1,0:T(8,128)S(1)}, u32[]{:S(2)}, u32[]{:S(2)}) collective-permute-start(f32[2,32,128]{2,1,0:T(8,128)S(1)} %merge_stats.1.a_ref), channel_id=1, source_target_pairs={{0,8},{8,0},{1,9},{9,1},{2,10},{10,2},{3,11},{11,3},{4,12},{12,4},... | collective-permute-start | bytes 98312 | tf_op jit(solution)/shard_map/ppermute | solution.py:352
  32.2 11.4 %collective-permute-start.4 = (bf16[64,1024]{1,0:T(8,128)(2,1)S(1)}, bf16[64,1024]{1,0:T(8,128)(2,1)S(1)}, u32[]{:S(2)}, u32[]{:S(2)}) collective-permute-start(bf16[64,1024]{1,0:T(8,128)(2,1)S(1)} %get-tuple-element.21), channel_id=1, source_target_pairs={{0,192},{64,0},{128,64},{192,128},{1,193},{65,1},{129,65},{193,129... | collective-permute-start | bytes 393224 | tf_op jit(solution)/shard_map/ppermute | solution.py:354
  33.3 10.5 %collective-permute-start.3 = (bf16[64,1024]{1,0:T(8,128)(2,1)S(1)}, bf16[64,1024]{1,0:T(8,128)(2,1)S(1)}, u32[]{:S(2)}, u32[]{:S(2)}) collective-permute-start(bf16[64,1024]{1,0:T(8,128)(2,1)S(1)} %get-tuple-element.21), channel_id=1, source_target_pairs={{0,128},{64,192},{128,0},{192,64},{1,129},{65,193},{129,1},{193,65... | collective-permute-start | bytes 393224 | tf_op jit(solution)/shard_map/ppermute | solution.py:354
  35.8 9.9 %collective-permute-start.2 = (bf16[64,1024]{1,0:T(8,128)(2,1)S(1)}, bf16[64,1024]{1,0:T(8,128)(2,1)S(1)}, u32[]{:S(2)}, u32[]{:S(2)}) collective-permute-start(bf16[64,1024]{1,0:T(8,128)(2,1)S(1)} %get-tuple-element.21), channel_id=1, source_target_pairs={{0,64},{64,128},{128,192},{192,0},{1,65},{65,129},{129,193},{193,1... | collective-permute-start | bytes 393224 | tf_op jit(solution)/shard_map/ppermute | solution.py:354
  52.3 26.3 %copy-start = (f32[256,256]{1,0:T(8,128)S(1)}, f32[256,256]{1,0:T(8,128)}, u32[]{:S(2)}) copy-start(f32[256,256]{1,0:T(8,128)} %get-tuple-element.33.gate_ref) | copy-start | bytes 786436
  52.3 26.3 %copy-start.1 = (bf16[256,256]{1,0:T(8,128)(2,1)S(1)}, bf16[256,256]{1,0:T(8,128)(2,1)}, u32[]{:S(2)}) copy-start(bf16[256,256]{1,0:T(8,128)(2,1)} %get-tuple-element.34.block_ref) | copy-start | bytes 393220
  52.3 1.8 %collective-permute-start.6 = (bf16[16,32,128]{2,1,0:T(8,128)(2,1)S(1)}, bf16[16,32,128]{2,1,0:T(8,128)(2,1)S(1)}, u32[]{:S(2)}, u32[]{:S(2)}) collective-permute-start(bf16[16,32,128]{2,1,0:T(8,128)(2,1)S(1)} %get-tuple-element.32), channel_id=1, source_target_pairs={{0,1},{1,0},{2,3},{3,2},{4,5},{5,4},{6,7},{7,6},{8,9},{9,8},{10,11... | collective-permute-start | bytes 393224 | tf_op jit(solution)/shard_map/ppermute | solution.py:367
  53.4 7.0 %collective-permute-start.5 = (bf16[16,32,128]{2,1,0:T(8,128)(2,1)S(1)}, bf16[16,32,128]{2,1,0:T(8,128)(2,1)S(1)}, u32[]{:S(2)}, u32[]{:S(2)}) collective-permute-start(bf16[16,32,128]{2,1,0:T(8,128)(2,1)S(1)} %get-tuple-element.30), channel_id=1, source_target_pairs={{0,1},{1,0},{2,3},{3,2},{4,5},{5,4},{6,7},{7,6},{8,9},{9,8},{10,11... | collective-permute-start | bytes 393224 | tf_op jit(solution)/shard_map/ppermute | solution.py:370
  54.1 12.9 %collective-permute-start.7 = (bf16[16,32,128]{2,1,0:T(8,128)(2,1)S(1)}, bf16[16,32,128]{2,1,0:T(8,128)(2,1)S(1)}, u32[]{:S(2)}, u32[]{:S(2)}) collective-permute-start(bf16[16,32,128]{2,1,0:T(8,128)(2,1)S(1)} %add_parts.2), channel_id=1, source_target_pairs={{0,8},{8,0},{1,9},{9,1},{2,10},{10,2},{3,11},{11,3},{4,12},{12,4},... | collective-permute-start | bytes 393224 | tf_op jit(solution)/shard_map/ppermute | solution.py:368
